TPU v7x, 512 devices: a whole 4x8x8 slice. The times are simulated.
512 devices in a mesh: tm: 32 (over z_lo, y), tile: 16 (over z_hi, x, core).
Axes of the slice: x: 4, y: 8, z: 8 (z_hi: 2, z_lo: 4; z = z_hi * 4 + z_lo), core: 2. Of those that a mesh axis runs over, the one named last changes fastest.
Arguments:
- latents: float32 [32, 64, 16, 128], P('tm', 'tile'), may hold values from -15 to 15
- new_frames: float32 [1, 64, 16, 128], P(None, 'tile'), may hold values from -15 to 15
- levels: int32 [2, 32], P(None, 'tm'), may hold values from 1 to 64
- offset: int32 [1], replicated, may hold values from 0 to 511
- w_in: bfloat16 [64, 1152], P('tm', 'tile'), may hold values from -0.75 to 0.75
- w_qkv: bfloat16 [1152, 3456], P('tm', 'tile'), as said below
- w_o: bfloat16 [1152, 1152], P('tm', 'tile'), may hold values from -0.1875 to 0.1875
- w_out: bfloat16 [1152, 64], P('tm', 'tile'), may hold values from -0.1875 to 0.1875
- w_time: bfloat16 [256, 1152], P('tm', 'tile'), may hold values from -0.375 to 0.375
- w_pos: bfloat16 [256, 1152], P('tm', 'tile'), may hold values from -0.375 to 0.375
- mod_gain: float32 [3, 1152], replicated, may hold values from -3 to 3
- mod_bias: float32 [3, 1152], replicated, may hold values from -3 to 3
- refiner: float32 [16, 27, 16], replicated, may hold values from -0.3125 to 0.3125
Outputs:
- window: float32 [32, 64, 16, 128], P('tm', 'tile')
Inputs may be any that keep to these rules, and one draw needn't show every extreme that they name: `w_qkv`: a projection.
All inputs are finite; a program needn't handle non-finite values.
Results may differ from a plain program's by a relative error of at most 0.00555.
Values may be sent and summed in bfloat16 or wider, within the bound.
No kernel may reach another device: no remote copies, remote signals or barrier semaphores. Data moves between devices by JAX's collectives and lax.ppermute only.
A program may use at most 64 MiB of HBM per device.

v0:
```python
import functools
import math

import jax
import jax.numpy as jnp
import numpy as np
from jax import lax
from jax.experimental import pallas as pl
from jax.experimental.pallas import tpu as pltpu
from jax.sharding import PartitionSpec as P

D = 1152
HEADS = 16
HEAD = 72
C = 16
PF = 64
FREQ = 256
STEPS = 2
LEVELS = 64
TM = 32
TILE = 16
ROWS = 36
TOK = 128
LANES = 128
SPAN = TILE * TOK
WIDE = 32 * 40

SIGMA_LOW = 0.02
SIGMA_RATIO = 1000.0
NORM_EPS = 1e-06

F32 = jnp.float32
BF16 = jnp.bfloat16
HIGHEST = lax.Precision.HIGHEST


def swapped(block, axis, mask):
    size = lax.axis_size(axis)
    return lax.ppermute(block, axis, [(i, i ^ mask) for i in range(size)])


def shifted(block, axis, distance):
    devices = range(lax.axis_size(axis))
    route = [(i - distance, i) for i in devices if i - distance in devices]
    return lax.ppermute(block, axis, route)


def exchanged(copies, axis):
    return lax.all_to_all(copies, axis, split_axis=0, concat_axis=0, tiled=True)


def sigma_of(level_ids):
    scaled_level = level_ids.astype(F32) / LEVELS
    return jnp.where(
        level_ids > 0, SIGMA_LOW * jnp.exp(math.log(SIGMA_RATIO) * scaled_level), F32(0.0)
    )


def sinusoid(values):
    half_freq = FREQ // 2
    frequency = jnp.exp(-math.log(10000.0) * jnp.arange(half_freq, dtype=F32) / half_freq)
    angles = values[:, None] * frequency[None, :]
    return jnp.concatenate([jnp.cos(angles), jnp.sin(angles)], axis=1)


def nn(a, b, precision=None):
    return lax.dot_general(
        a, b, (((1,), (0,)), ((), ())), preferred_element_type=F32, precision=precision
    )


def nt(a, b):
    return lax.dot_general(a, b, (((1,), (1,)), ((), ())), preferred_element_type=F32)


def tn(a, b):
    return lax.dot_general(a, b, (((0,), (0,)), ((), ())), preferred_element_type=F32)


def lane_of(shape):
    return lax.broadcasted_iota(jnp.int32, shape, 1)


def spread_matrix(shape, token_dim, hp, b, dtype):
    token = lax.broadcasted_iota(jnp.int32, shape, token_dim)
    col = lax.broadcasted_iota(jnp.int32, shape, 1 - token_dim)
    hit = col + 128 * hp == 2 * token + b
    return jnp.where(hit, 1.0, 0.0).astype(dtype)


def patch_rows(scaled):
    halves = []
    for b in range(2):
        total = None
        for hp in range(2):
            rows = scaled[2 * hp : 2 * hp + 2].reshape(2 * C, LANES)
            term = nn(rows, spread_matrix((LANES, TOK), 1, hp, b, BF16))
            total = term if total is None else total + term
        halves.append(total)
    return jnp.concatenate(halves, axis=0).astype(BF16)


def prep_kernel(scalar_ref, lat_ref, out_ref):
    scaled = (lat_ref[...] * scalar_ref[0]).astype(BF16)
    rows = patch_rows(scaled)
    for t in range(TILE):
        out_ref[t] = rows


def refined_rows(noise_ref, mix_ref):
    lane = lax.broadcasted_iota(jnp.int32, (C, LANES), 1)
    tri = {}
    for td in range(3):
        for row in range(6):
            x = noise_ref[td, row]
            before = jnp.where(lane == 0, 0.0, pltpu.roll(x, 1, 1))
            after = jnp.where(lane == LANES - 1, 0.0, pltpu.roll(x, LANES - 1, 1))
            tri[td, row] = [before, x, after]
    columns = []
    for r in range(4):
        pieces = []
        for td in range(3):
            for dr in range(3):
                pieces += tri[td, r + dr]
        columns.append(jnp.concatenate(pieces, axis=0))
    cells = jnp.concatenate(columns, axis=1)
    mixed = nn(mix_ref[...], cells, HIGHEST)
    return [noise_ref[1, r + 1] + mixed[:, r * LANES : (r + 1) * LANES] for r in range(4)]


def middle_kernel(scalar_ref, flag_ref, noise_ref, lat_ref, new_ref, mix_ref, lat_out, patch_out):
    refined = refined_rows(noise_ref, mix_ref)
    last = flag_ref[0] == 1
    rows = []
    for r in range(4):
        moved = lat_ref[r] + lat_ref[4, 0:1, :] * refined[r]
        rows.append(jnp.where(last, new_ref[r], moved))
        lat_out[r] = rows[r]
    scaled = (jnp.stack(rows) * scalar_ref[0]).astype(BF16)
    patches = patch_rows(scaled)
    for t in range(TILE):
        patch_out[t] = patches


def final_kernel(scalar_ref, noise_ref, lat_ref, mix_ref, out_ref):
    refined = refined_rows(noise_ref, mix_ref)
    for r in range(4):
        out_ref[r] = lat_ref[r] + scalar_ref[0] * refined[r]


def spread_kernel(x_ref, pick_ref, emb_ref, mod_ref, order_ref, pay_ref, out_t_ref):
    out_t_ref[...] = nt(order_ref[...], x_ref[:, 256:384]).astype(BF16)
    cols = x_ref[:, 128:256]
    halves = []
    for h in range(2):
        found = jnp.concatenate(
            [nn(pick_ref[h], cols), nn(emb_ref[h], cols), jnp.zeros((48, LANES), F32)], axis=0
        )
        turned = pltpu.roll(found, 40, 1).T[0:40]
        mod = mod_ref[40 * h : 40 * h + 40]
        lane = lane_of((40, LANES))
        valid = lax.broadcasted_iota(jnp.int32, (40, LANES), 0) < ROWS
        block = jnp.where(lane < PF, turned, jnp.where(lane == 76, 1.0, 0.0))
        for step in range(STEPS):
            hidden = turned[:, PF + step : PF + step + 1]
            condition = hidden / (1.0 + jnp.exp(-hidden))
            for j, kind in enumerate((1, 0, 2)):
                value = condition * mod[:, kind : kind + 1] + mod[:, 3 + kind : 4 + kind]
                if kind == 1:
                    value = value + 1.0
                upper = value.astype(BF16).astype(F32)
                block = jnp.where(lane == PF + 3 * step + j, upper, block)
                block = jnp.where(lane == PF + 6 + 3 * step + j, value - upper, block)
        halves.append(jnp.where(valid, block, 0.0))
    pay = jnp.concatenate(halves, axis=0).astype(BF16)
    for t in range(TILE):
        pay_ref[t] = pay


def fold_kernel(feat_ref, x_ref, first_ref, second_ref, gram_ref):
    lane = lane_of((WIDE, LANES))
    feat = feat_ref[...].astype(F32)
    mods = feat + pltpu.roll(feat, LANES - 6, 1)
    wide = jnp.where(lane < PF, feat, 0.0)
    mean = jnp.sum(wide, axis=0, keepdims=True) * (1.0 / D)
    centred = (wide - mean) * feat[:, 76:77]
    upper = centred.astype(BF16)
    lower = (centred - upper.astype(F32)).astype(BF16)
    gram = tn(upper, upper) + tn(upper, lower) + tn(lower, upper)
    gram_ref[...] = gram[0:PF, 0:PF]
    for step, out_ref in enumerate((first_ref, second_ref)):
        at = PF + 3 * step
        lines = jnp.where(
            lane < PF,
            centred * mods[:, at : at + 1],
            jnp.where(lane == PF, mods[:, at + 1 : at + 2], 0.0),
        )
        upper = lines.astype(BF16)
        lower = (lines - upper.astype(F32)).astype(BF16)
        weights = x_ref[:, 0:256]
        folded = tn(weights, upper) + tn(weights, lower)
        unit = [folded[HEAD * j : HEAD * j + HEAD] for j in range(3)]
        spot = lane_of((HEAD, LANES))
        top = jnp.where(spot < PF, unit[0], pltpu.roll(unit[1], PF, 1))
        low = jnp.where(spot < PF, unit[2], 0.0)
        low = jnp.where(spot == PF, unit[0], low)
        low = jnp.where(spot == PF + 1, pltpu.roll(unit[1], 1, 1), low)
        low = jnp.where(spot == PF + 2, pltpu.roll(unit[2], 2, 1), low)
        packed = jnp.concatenate([top, low], axis=0).astype(BF16)
        for t in range(TILE):
            out_ref[t] = packed


def heads_kernel(folded_ref, widen_ref, n_ref, mvt_ref, units):
    spot = lane_of((HEAD, LANES))
    for t in range(TILE):
        both = folded_ref[t].astype(F32)
        top, low = both[0:HEAD], both[HEAD : 2 * HEAD]
        parts = (
            (top, low),
            (pltpu.roll(top, PF, 1), pltpu.roll(low, LANES - 1, 1)),
            (low, pltpu.roll(low, LANES - 2, 1)),
        )
        for j, (main, bias) in enumerate(parts):
            unit = jnp.where(spot < PF, main, jnp.where(spot == PF, bias, 0.0))
            units[3 * t + j] = unit
    fold_scale = math.log2(math.e) / math.sqrt(HEAD)
    for h in range(HEADS):
        q, k, v = (units[HEADS * kind + h].astype(BF16) for kind in range(3))
        n_ref[h] = (tn(q, k) * fold_scale).astype(BF16)
        mvt_ref[h] = nn(widen_ref[...], v).astype(BF16)


def block_kernel(
    step, spot_ref, pt_ref, gram_ref, n_ref, mvt_ref, feat_ref, wot_ref, wot2_ref, out_ref,
    keys_t, keys, att, stream_ref,
):
    me = spot_ref[0]
    row = lax.broadcasted_iota(jnp.int32, (PF, TOK), 0)
    ones = jnp.where(row == 0, 1.0, 0.0).astype(F32)
    for j in range(TILE):
        patches = pt_ref[j].astype(F32)
        spread = jnp.sum(patches * nn(gram_ref[...], patches, HIGHEST), axis=0, keepdims=True)
        unit = patches * lax.rsqrt(jnp.maximum(spread, 0.0) * (1.0 / D) + NORM_EPS)
        wide = jnp.concatenate([unit, ones], axis=0)
        keys_t[:, j * TOK : (j + 1) * TOK] = wide.astype(BF16)
        keys[j * TOK : (j + 1) * TOK, :] = wide.T.astype(BF16)

    def two_heads(pair):
        own = keys[pl.ds(pl.multiple_of(me * TOK, TOK), TOK), :]
        queries = jnp.concatenate(
            [nn(own, n_ref[2 * pair]), nn(own, n_ref[2 * pair + 1])], axis=0
        ).astype(BF16)
        scores = nn(queries, keys_t[...])
        highest = jnp.max(scores, axis=1, keepdims=True)
        weights = jnp.exp2(scores - highest).astype(BF16)
        summed = nn(weights, keys[...])
        mean = (summed / summed[:, PF : PF + 1]).astype(BF16)
        for k in range(2):
            head = 2 * pair + k
            value = nt(mvt_ref[head], mean[k * TOK : (k + 1) * TOK])
            att[pl.ds(pl.multiple_of(head * 80, 80), 80), :] = value

    @pl.loop(0, HEADS // 4)
    def _(i):
        two_heads(2 * i)
        two_heads(2 * i + 1)

    attended = att[...].astype(BF16)
    for c, ref in enumerate((wot_ref, wot2_ref)):
        delta = nn(ref[...], attended)
        for b in range(8):
            tile = me ^ (8 * (b % 2) + 2 * (b // 2) + c)
            rows = pl.ds(pl.multiple_of(tile * 80, 80), 80)
            stream_ref[rows, :] = delta[96 * b : 96 * b + 80]
    feat = feat_ref[...]
    own = jnp.concatenate([pt_ref[me], jnp.zeros((PF, TOK), BF16)], axis=0)
    at = PF + 3 * step + 2
    gate = feat[:, at : at + 1].astype(F32) + feat[:, at + 6 : at + 7].astype(F32)
    stream = nn(feat, own) + gate * stream_ref[...]
    mean = jnp.sum(stream, axis=0, keepdims=True) * (1.0 / D)
    center = (stream - mean) * feat[:, 76:77].astype(F32)
    spread = jnp.sum(center * center, axis=0, keepdims=True) * (1.0 / D)
    final = (center * lax.rsqrt(spread + NORM_EPS)).astype(BF16)
    out_rows = [
        ref[96 * b + 80 : 96 * b + 96, :] for ref in (wot_ref, wot2_ref) for b in range(8)
    ]
    noise = nn(jnp.concatenate(out_rows, axis=0), final)
    feature = lax.broadcasted_iota(jnp.int32, (PF, 256), 0)
    source = lane_of((PF, 256))
    block = source >> 4
    mask = ((block & 1) << 3) | (((block >> 1) & 3) << 1) | (block >> 3)
    q = source & 15
    wanted = ((q & 1) << 5) + ((q >> 1) << 4) + (mask ^ me)
    order = jnp.where((q < 4) & (feature == wanted), 1.0, 0.0).astype(F32)
    noise = nn(order, noise, HIGHEST)
    for hp in range(2):
        rows = None
        for b in range(2):
            term = nn(
                noise[b * 32 : (b + 1) * 32], spread_matrix((TOK, LANES), 0, hp, b, F32), HIGHEST
            )
            rows = term if rows is None else rows + term
        out_ref[2 * hp] = rows[0:C]
        out_ref[2 * hp + 1] = rows[C : 2 * C]


VMEM = pl.BlockSpec(memory_space=pltpu.VMEM)
SMEM = pl.BlockSpec(memory_space=pltpu.SMEM)


def spread(x, emb, mod):
    return pl.pallas_call(
        spread_kernel,
        out_shape=(
            jax.ShapeDtypeStruct((TILE, 80, LANES), BF16),
            jax.ShapeDtypeStruct((96, WIDE), BF16),
        ),
        in_specs=[VMEM] * 5,
        out_specs=(VMEM, VMEM),
        compiler_params=pltpu.CompilerParams(vmem_limit_bytes=32 * 1024 * 1024),
        name="spread",
    )(x, jnp.asarray(PICK, BF16), emb, mod, jnp.asarray(ORDER, BF16))


def fold(feat, x):
    folded = jax.ShapeDtypeStruct((TILE, 2 * HEAD, LANES), BF16)
    return pl.pallas_call(
        fold_kernel,
        out_shape=(folded, folded, jax.ShapeDtypeStruct((PF, PF), F32)),
        in_specs=[VMEM] * 2,
        out_specs=(VMEM,) * 3,
        compiler_params=pltpu.CompilerParams(vmem_limit_bytes=32 * 1024 * 1024),
        name="fold",
    )(feat, x)


def heads(folded):
    return pl.pallas_call(
        heads_kernel,
        out_shape=(
            jax.ShapeDtypeStruct((HEADS, LANES, LANES), BF16),
            jax.ShapeDtypeStruct((HEADS, 80, LANES), BF16),
        ),
        in_specs=[VMEM] * 2,
        out_specs=(VMEM,) * 2,
        scratch_shapes=[pltpu.VMEM((3 * HEADS, HEAD, LANES), F32)],
        compiler_params=pltpu.CompilerParams(vmem_limit_bytes=32 * 1024 * 1024),
        name="heads",
    )(folded, jnp.asarray(ORDER[0:80, 0:HEAD], BF16))


def frame_block(step, spot, pt, gram, n, mvt, feat, wot, wot2):
    return pl.pallas_call(
        functools.partial(block_kernel, step),
        out_shape=jax.ShapeDtypeStruct((4, C, LANES), F32),
        in_specs=[SMEM] + [VMEM] * 7,
        out_specs=VMEM,
        scratch_shapes=[
            pltpu.VMEM((LANES, SPAN), BF16),
            pltpu.VMEM((SPAN, LANES), BF16),
            pltpu.VMEM((WIDE, TOK), F32),
            pltpu.VMEM((WIDE, TOK), F32),
        ],
        compiler_params=pltpu.CompilerParams(vmem_limit_bytes=48 * 1024 * 1024),
        cost_estimate=pl.CostEstimate(
            flops=2 * 2 * SPAN * SPAN * LANES + 2 * D * D * TOK,
            bytes_accessed=2 * D * D + 4 * SPAN * LANES,
            transcendentals=SPAN * SPAN,
        ),
        name="frame_block",
    )(spot, pt, gram, n, mvt, feat, wot, wot2)


def prep(scale_in, latent):
    return pl.pallas_call(
        prep_kernel,
        out_shape=jax.ShapeDtypeStruct((TILE, PF, TOK), BF16),
        in_specs=[SMEM, VMEM],
        out_specs=VMEM,
        name="prep",
    )(scale_in, latent)


def middle(scale_in, last, noise, lat, new, mix):
    return pl.pallas_call(
        middle_kernel,
        out_shape=(
            jax.ShapeDtypeStruct((4, C, LANES), F32),
            jax.ShapeDtypeStruct((TILE, PF, TOK), BF16),
        ),
        in_specs=[SMEM, SMEM] + [VMEM] * 4,
        out_specs=(VMEM, VMEM),
        compiler_params=pltpu.CompilerParams(vmem_limit_bytes=32 * 1024 * 1024),
        name="middle",
    )(scale_in, last, noise, lat, new, mix)


def finish(drop, noise, lat, mix):
    return pl.pallas_call(
        final_kernel,
        out_shape=jax.ShapeDtypeStruct((4, C, LANES), F32),
        in_specs=[SMEM] + [VMEM] * 3,
        out_specs=VMEM,
        compiler_params=pltpu.CompilerParams(vmem_limit_bytes=32 * 1024 * 1024),
        name="finish",
    )(drop, noise, lat, mix)


def with_rows(frames):
    before = shifted(frames[:, 3:4], "tile", 1)
    after = shifted(frames[:, 0:1], "tile", -1)
    return jnp.concatenate([before, frames, after], axis=1)


def pick_matrix():
    pick = np.zeros((2, 2, 2, C, TM, 20, 2), np.float32)
    for h in range(2):
        for b in range(2):
            for a in range(2):
                for c in range(C):
                    pick[h, b, a, c, 2 * c + a, 16 + b, h] = 1.0
    return pick.reshape(2, PF, WIDE)


def order_matrix():
    order = np.zeros((96, LANES), np.float32)
    for j in range(ROWS):
        order[j, j] = 1.0
        order[40 + j, ROWS + j] = 1.0
    for j in range(4):
        order[80 + j, HEAD + j] = 1.0
    return order


PICK = pick_matrix()
ORDER = order_matrix()


def packed_weights(w_in, w_qkv, w_o, w_out, w_time, w_pos):
    small = jnp.concatenate([w_time, w_pos, w_in], axis=0).reshape(ROWS, ROWS)
    gap = jnp.zeros((ROWS, 4), BF16)
    tail = jnp.zeros((ROWS, 52), BF16)
    packed = jnp.concatenate([w_qkv, small, gap, w_o, w_out, tail], axis=1)
    return jnp.pad(packed, ((0, 4), (0, 0)))


def embeddings(level, position):
    level_emb = sinusoid(level.astype(F32)).reshape(STEPS, TM, 8)
    position_emb = sinusoid(position.astype(F32)).reshape(STEPS, TM, 8)
    rest = jnp.zeros((STEPS, TM, 4), F32)
    emb = jnp.concatenate([level_emb, position_emb, rest], axis=2).astype(BF16)
    half = jnp.eye(2, dtype=BF16)[:, None, None, None, :]
    emb = (emb[None, :, :, :, None] * half).reshape(2, STEPS, WIDE)
    return jnp.pad(emb, ((0, 0), (0, 14), (0, 0)))


def own_mods(mod_gain, mod_bias, tile):
    mods = jnp.concatenate([mod_gain, mod_bias, jnp.zeros((2, D), F32)], axis=0)
    mods = lax.dynamic_slice_in_dim(mods.reshape(8, TILE, HEAD), tile, 1, axis=1)
    return jnp.pad(mods.reshape(8, 2, ROWS), ((0, 0), (0, 0), (0, 4))).reshape(8, 80).T


def per_device(
    latents, new_frames, levels, offset, w_in, w_qkv, w_o, w_out, w_time, w_pos,
    mod_gain, mod_bias, refiner,
):
    frame = lax.axis_index("tm")
    tile = lax.axis_index("tile")
    spot = tile.astype(jnp.int32)[None]
    mix = refiner.reshape(C, 27 * C)
    latent = latents[0]
    level = levels[:, 0]
    sigma_now = sigma_of(level)
    drop = sigma_of(level - 1) - sigma_now
    scale_in = lax.rsqrt(1.0 + sigma_now * sigma_now)

    packed = packed_weights(w_in, w_qkv, w_o, w_out, w_time, w_pos)
    rows = exchanged(jnp.broadcast_to(packed[None], (TM,) + packed.shape), "tm")
    rows = rows.reshape(WIDE, 384)

    patches = exchanged(prep(scale_in[0:1], latent), "tile")
    marked = jnp.concatenate([latent, jnp.full((1, C, LANES), drop[0], F32)], axis=0)
    marked = shifted(marked, "tm", -1)

    steps = jnp.arange(STEPS, dtype=jnp.int32)
    emb = embeddings(level, offset + frame + steps)
    pay, out_t = spread(rows, emb, own_mods(mod_gain, mod_bias, tile))
    feat = exchanged(pay, "tile").reshape(WIDE, LANES)

    first, second, gram = fold(feat, rows)
    folded = [exchanged(first, "tile"), exchanged(second, "tile")]

    both = jnp.stack([out_t, swapped(out_t, "tile", 8)])
    four = jnp.concatenate([both] + [swapped(both, "tile", 2 * k) for k in (1, 2, 3)])
    other = swapped(four, "tile", 1)
    four = four.reshape(8 * 96, WIDE)
    other = other.reshape(8 * 96, WIDE)

    for step in range(STEPS):
        n, mvt = heads(folded[step])
        noise = frame_block(step, spot, patches, gram, n, mvt, feat, four, other)
        if step == 0:
            frames = jnp.stack([noise, shifted(noise, "tm", -1), shifted(noise, "tm", -2)])
            last = (frame == TM - 1).astype(jnp.int32)[None]
            latent, patches = middle(
                scale_in[1:2], last, with_rows(frames), marked, new_frames[0], mix
            )
            patches = exchanged(patches, "tile")
        else:
            frames = jnp.stack([shifted(noise, "tm", 1), noise, shifted(noise, "tm", -1)])
            return finish(drop[1:2], with_rows(frames), latent, mix)[None]


def solution(mesh):
    in_specs = (
        P("tm", "tile", None, None),
        P(None, "tile", None, None),
        P(None, "tm"),
        P(),
        P("tm", "tile"),
        P("tm", "tile"),
        P("tm", "tile"),
        P("tm", "tile"),
        P("tm", "tile"),
        P("tm", "tile"),
        P(),
        P(),
        P(),
    )
    out_specs = P("tm", "tile", None, None)
    return jax.shard_map(
        per_device, mesh=mesh, in_specs=in_specs, out_specs=out_specs, check_vma=False
    )
```

profile of v0, /device:TPU:191, one launch (start us, length us, event | category | flops | bytes accessed | tf_op | source)
XLA Modules:
  0.0 253.2 jit_solution(3764848185733830698)
XLA Ops:
  0.0 0.7 pad_maximum_fusion.9
  0.8 0.8 copy.25
  1.6 0.8 concatenate.41
  2.5 1.1 broadcast_in_dim.47
  3.5 10.3 %all-to-all-start.1 = ((bf16[32,40,384]{2,1,0:T(8,128)(2,1)}), bf16[32,40,384]{2,1,0:T(8,128)(2,1)S(1)}, u32[]{:S(2)}, u32[]{:S(2)}) async-start(bf16[32,40,384]{2,1,0:T(8,128)(2,1)} %broadcast_in_dim.47), calls=%async_computation.1 | async-start | bytes 1966080 | tf_op jit(solution)/shard_map/all_to_all | solution.py:49
  14.6 0.1 fusion
  14.8 0.1 copy.26
  14.9 0.3 mul.92
  15.2 0.4 mul.93
  15.7 0.4 mul.96
  16.5 0.1 copy.31
  16.6 20.4 %all-to-all-done.1 = bf16[32,40,384]{2,1,0:T(8,128)(2,1)S(1)} async-done(((bf16[32,40,384]{2,1,0:T(8,128)(2,1)}), bf16[32,40,384]{2,1,0:T(8,128)(2,1)S(1)}, u32[]{:S(2)}, u32[]{:S(2)}) %all-to-all-start.1) | async-done | bytes 983072 | tf_op jit(solution)/shard_map/all_to_all | solution.py:49
  37.0 1.5 spread.1
  38.5 7.9 %collective-permute-start = (bf16[96,1280]{1,0:T(8,128)(2,1)S(1)}, bf16[96,1280]{1,0:T(8,128)(2,1)S(1)}, u32[]{:S(2)}, u32[]{:S(2)}) collective-permute-start(bf16[96,1280]{1,0:T(8,128)(2,1)S(1)} %get-tuple-element.21), channel_id=1, source_target_pairs={{0,8},{1,9},{2,10},{3,11},{4,12},{5,13},{6,14},{7,15},{8,0},{9,1},... | collective-permute-start | bytes 737288 | tf_op jit(solution)/shard_map/ppermute | solution.py:39
  46.5 0.7 fusion.5
  47.2 2.2 prep.1
  49.4 8.7 %collective-permute-done = bf16[96,1280]{1,0:T(8,128)(2,1)S(1)} collective-permute-done((bf16[96,1280]{1,0:T(8,128)(2,1)S(1)}, bf16[96,1280]{1,0:T(8,128)(2,1)S(1)}, u32[]{:S(2)}, u32[]{:S(2)}) %collective-permute-start) | collective-permute-done | bytes 245792 | tf_op jit(solution)/shard_map/ppermute | solution.py:39
  58.2 2.5 collective-permute-start.1
  60.7 0.7 constant_dynamic-update-slice_fusion.4
  61.4 10.1 %all-to-all-start.2 = ((bf16[16,80,128]{2,1,0:T(8,128)(2,1)}), bf16[16,80,128]{2,1,0:T(8,128)(2,1)S(1)}, u32[]{:S(2)}, u32[]{:S(2)}) async-start(bf16[16,80,128]{2,1,0:T(8,128)(2,1)} %get-tuple-element.16), calls=%async_computation.2 | async-start | bytes 655360 | tf_op jit(solution)/shard_map/all_to_all | solution.py:49
  71.5 3.1 %collective-permute-start.2 = (bf16[2,96,1280]{2,1,0:T(8,128)(2,1)S(1)}, bf16[2,96,1280]{2,1,0:T(8,128)(2,1)S(1)}, u32[]{:S(2)}, u32[]{:S(2)}) collective-permute-start(bf16[2,96,1280]{2,1,0:T(8,128)(2,1)S(1)} %pad_maximum_fusion), channel_id=1, source_target_pairs={{0,4},{1,5},{2,6},{3,7},{4,0},{5,1},{6,2},{7,3},{8,12},{9,13},{10,... | collective-permute-start | bytes 1474568 | tf_op jit(solution)/shard_map/ppermute | solution.py:39
  74.6 3.7 %collective-permute-start.3 = (bf16[2,96,1280]{2,1,0:T(8,128)(2,1)S(1)}, bf16[2,96,1280]{2,1,0:T(8,128)(2,1)S(1)}, u32[]{:S(2)}, u32[]{:S(2)}) collective-permute-start(bf16[2,96,1280]{2,1,0:T(8,128)(2,1)S(1)} %pad_maximum_fusion), channel_id=1, source_target_pairs={{0,6},{1,7},{2,4},{3,5},{4,2},{5,3},{6,0},{7,1},{8,14},{9,15},{10,... | collective-permute-start | bytes 1474568 | tf_op jit(solution)/shard_map/ppermute | solution.py:39
  78.3 0.7 constant_dynamic-update-slice_fusion.3
  79.0 0.8 constant_dynamic-update-slice_fusion.2
  79.8 9.7 %collective-permute-done.2 = bf16[2,96,1280]{2,1,0:T(8,128)(2,1)S(1)} collective-permute-done((bf16[2,96,1280]{2,1,0:T(8,128)(2,1)S(1)}, bf16[2,96,1280]{2,1,0:T(8,128)(2,1)S(1)}, u32[]{:S(2)}, u32[]{:S(2)}) %collective-permute-start.2) | collective-permute-done | bytes 491552 | tf_op jit(solution)/shard_map/ppermute | solution.py:39
  89.5 0.8 constant_dynamic-update-slice_fusion.1
  90.3 9.8 %all-to-all-start = ((bf16[16,64,128]{2,1,0:T(8,128)(2,1)}), bf16[16,64,128]{2,1,0:T(8,128)(2,1)S(1)}, u32[]{:S(2)}, u32[]{:S(2)}) async-start(bf16[16,64,128]{2,1,0:T(8,128)(2,1)} %prep.1), calls=%async_computation | async-start | bytes 524288 | tf_op jit(solution)/shard_map/all_to_all | solution.py:49
  100.2 0.5 collective-permute-done.3
  100.7 0.8 constant_dynamic-update-slice_fusion
  101.5 2.5 collective-permute-start.4
  104.0 3.2 %fold.1 = (bf16[16,144,128]{2,1,0:T(8,128)(2,1)S(1)}, bf16[16,144,128]{2,1,0:T(8,128)(2,1)}, f32[64,64]{1,0:T(8,128)S(1)}) custom-call(bf16[1280,128]{1,0:T(8,128)(2,1)S(1)} %bitcast.35, bf16[1280,384]{1,0:T(8,128)(2,1)S(1)} %bitcast.34), custom_call_target="tpu_custom_call" | custom-call | tf_op jit(solution)/shard_map/fold/pallas_call | solution.py:328
  107.2 5.3 %all-to-all-done.pt_ref = bf16[16,64,128]{2,1,0:T(8,128)(2,1)S(1)} async-done(((bf16[16,64,128]{2,1,0:T(8,128)(2,1)}), bf16[16,64,128]{2,1,0:T(8,128)(2,1)S(1)}, u32[]{:S(2)}, u32[]{:S(2)}) %all-to-all-start) | async-done | bytes 262176 | tf_op jit(solution)/shard_map/all_to_all | solution.py:49
  112.5 23.0 %all_to_all.30.folded_ref = bf16[16,144,128]{2,1,0:T(8,128)(2,1)S(1)} all-to-all(bf16[16,144,128]{2,1,0:T(8,128)(2,1)S(1)} %get-tuple-element.18), channel_id=1, replica_groups=mesh['tm'=32,'tile'=16] {'tile'}, dimensions={0} | all-to-all | bytes 1179648 | tf_op jit(solution)/shard_map/all_to_all | solution.py:49
  135.5 5.3 %all-to-all-start.5 = ((bf16[16,144,128]{2,1,0:T(8,128)(2,1)}), bf16[16,144,128]{2,1,0:T(8,128)(2,1)S(1)}, u32[]{:S(2)}, u32[]{:S(2)}) async-start(bf16[16,144,128]{2,1,0:T(8,128)(2,1)} %get-tuple-element.23), calls=%async_computation.5 | async-start | bytes 1179648 | tf_op jit(solution)/shard_map/all_to_all | solution.py:49
  140.8 0.8 heads.2
  141.6 1.5 copy-done.3
  143.1 13.6 %frame_block.2 = f32[4,16,128]{2,1,0:T(8,128)S(1)} custom-call(s32[1]{0:T(128)} %bitcast.1.spot_ref, bf16[16,64,128]{2,1,0:T(8,128)(2,1)S(1)} %all-to-all-done.pt_ref, f32[64,64]{1,0:T(8,128)S(1)} %get-tuple-element.17.gram_ref, bf16[16,128,128]{2,1,0:T(8,128)(2,1)S(1)} %get-tuple-element.19.n_ref, bf16[16,80,128]{2,1,0:T(8,128)(2,1)S(1)} %get-tuple-element.20.mvt_ref, ...), custom_call_target="tpu_custom_call" | custom-call | flops 2487222272 | bytes 3702784 | tf_op jit(solution)/shard_map/frame_block/pallas_call | solution.py:354
  156.7 2.5 collective-permute-start.5
  159.2 4.2 %collective-permute-start.6 = (f32[4,16,128]{2,1,0:T(8,128)S(1)}, f32[4,16,128]{2,1,0:T(8,128)S(1)}, u32[]{:S(2)}, u32[]{:S(2)}) collective-permute-start(f32[4,16,128]{2,1,0:T(8,128)S(1)} %frame_block.2), channel_id=1, source_target_pairs={{32,0},{48,16},{64,32},{80,48},{96,64},{112,80},{128,96},{144,112}... | collective-permute-start | bytes 98312 | tf_op jit(solution)/shard_map/ppermute | solution.py:45
  163.4 0.2 collective-permute-done.5
  163.6 3.4 %collective-permute-done.6 = f32[4,16,128]{2,1,0:T(8,128)S(1)} collective-permute-done((f32[4,16,128]{2,1,0:T(8,128)S(1)}, f32[4,16,128]{2,1,0:T(8,128)S(1)}, u32[]{:S(2)}, u32[]{:S(2)}) %collective-permute-start.6) | collective-permute-done | bytes 32800 | tf_op jit(solution)/shard_map/ppermute | solution.py:45
  167.1 8.7 %collective-permute-start.7 = (f32[3,1,16,128]{3,2,1,0:T(8,128)S(1)}, f32[3,1,16,128]{3,2,1,0:T(8,128)S(1)}, u32[]{:S(2)}, u32[]{:S(2)}) collective-permute-start(f32[3,1,16,128]{3,2,1,0:T(8,128)S(1)} %get-tuple-element.29), channel_id=1, source_target_pairs={{0,1},{1,2},{2,3},{3,4},{4,5},{5,6},{6,7},{7,8},{8,9},{9,10},{10,1... | collective-permute-start | bytes 73736 | tf_op jit(solution)/shard_map/ppermute | solution.py:45
  175.7 1.9 collective-permute-start.8
  177.7 0.7 concatenate.48
  178.3 3.6 %collective-permute-start.9 = (f32[5,16,128]{2,1,0:T(8,128)S(1)}, f32[5,16,128]{2,1,0:T(8,128)S(1)}, u32[]{:S(2)}, u32[]{:S(2)}) collective-permute-start(f32[5,16,128]{2,1,0:T(8,128)S(1)} %concatenate.48), channel_id=1, source_target_pairs={{16,0},{32,16},{48,32},{64,48},{80,64},{96,80},{112,96},{128,112},... | collective-permute-start | bytes 122888 | tf_op jit(solution)/shard_map/ppermute | solution.py:45
  182.0 0.9 copy.29
  182.9 1.1 reshape.138.mix_ref
  183.9 3.0 %collective-permute-done.8 = f32[3,1,16,128]{3,2,1,0:T(8,128)S(1)} collective-permute-done((f32[3,1,16,128]{3,2,1,0:T(8,128)S(1)}, f32[3,1,16,128]{3,2,1,0:T(8,128)S(1)}, u32[]{:S(2)}, u32[]{:S(2)}) %collective-permute-start.8) | collective-permute-done | bytes 24608 | tf_op jit(solution)/shard_map/ppermute | solution.py:45
  186.9 2.0 middle.1
  188.9 9.0 %all-to-all-start.4 = ((bf16[16,64,128]{2,1,0:T(8,128)(2,1)}), bf16[16,64,128]{2,1,0:T(8,128)(2,1)S(1)}, u32[]{:S(2)}, u32[]{:S(2)}) async-start(bf16[16,64,128]{2,1,0:T(8,128)(2,1)} %get-tuple-element.22), calls=%async_computation.4 | async-start | bytes 524288 | tf_op jit(solution)/shard_map/all_to_all | solution.py:49
  198.0 0.8 heads.3
  198.7 0.8 copy-done.6
  199.5 0.7 copy-done.8
  200.3 9.5 %all-to-all-done.4.pt_ref = bf16[16,64,128]{2,1,0:T(8,128)(2,1)S(1)} async-done(((bf16[16,64,128]{2,1,0:T(8,128)(2,1)}), bf16[16,64,128]{2,1,0:T(8,128)(2,1)S(1)}, u32[]{:S(2)}, u32[]{:S(2)}) %all-to-all-start.4) | async-done | bytes 262176 | tf_op jit(solution)/shard_map/all_to_all | solution.py:49
  209.7 1.0 copy-done.7
  210.8 1.0 copy-done.9
  211.8 13.6 %frame_block.3 = f32[4,16,128]{2,1,0:T(8,128)S(1)} custom-call(s32[1]{0:T(128)} %bitcast.1.spot_ref, bf16[16,64,128]{2,1,0:T(8,128)(2,1)S(1)} %all-to-all-done.4.pt_ref, f32[64,64]{1,0:T(8,128)S(1)} %get-tuple-element.17.gram_ref, bf16[16,128,128]{2,1,0:T(8,128)(2,1)S(1)} %copy-done.7, bf16[16,80,128]{2,1,0:T(8,128)(2,1)S(1)} %copy-done.9, ...), custom_call_target="tpu_custom_call" | custom-call | flops 2487222272 | bytes 3702784 | tf_op jit(solution)/shard_map/frame_block/pallas_call | solution.py:354
  225.3 1.9 collective-permute-start.10
  227.3 3.4 %collective-permute-start.11 = (f32[4,16,128]{2,1,0:T(8,128)S(1)}, f32[4,16,128]{2,1,0:T(8,128)S(1)}, u32[]{:S(2)}, u32[]{:S(2)}) collective-permute-start(f32[4,16,128]{2,1,0:T(8,128)S(1)} %frame_block.3), channel_id=1, source_target_pairs={{16,0},{32,16},{48,32},{64,48},{80,64},{96,80},{112,96},{128,112},... | collective-permute-start | bytes 98312 | tf_op jit(solution)/shard_map/ppermute | solution.py:45
  230.7 3.4 %collective-permute-done.11 = f32[4,16,128]{2,1,0:T(8,128)S(1)} collective-permute-done((f32[4,16,128]{2,1,0:T(8,128)S(1)}, f32[4,16,128]{2,1,0:T(8,128)S(1)}, u32[]{:S(2)}, u32[]{:S(2)}) %collective-permute-start.11) | collective-permute-done | bytes 32800 | tf_op jit(solution)/shard_map/ppermute | solution.py:45
  234.0 6.2 %collective-permute-start.12 = (f32[3,1,16,128]{3,2,1,0:T(8,128)S(1)}, f32[3,1,16,128]{3,2,1,0:T(8,128)S(1)}, u32[]{:S(2)}, u32[]{:S(2)}) collective-permute-start(f32[3,1,16,128]{3,2,1,0:T(8,128)S(1)} %get-tuple-element.27), channel_id=1, source_target_pairs={{0,1},{1,2},{2,3},{3,4},{4,5},{5,6},{6,7},{7,8},{8,9},{9,10},{10,1... | collective-permute-start | bytes 73736 | tf_op jit(solution)/shard_map/ppermute | solution.py:45
  240.2 1.9 collective-permute-start.13
  242.1 9.2 %collective-permute-done.13 = f32[3,1,16,128]{3,2,1,0:T(8,128)S(1)} collective-permute-done((f32[3,1,16,128]{3,2,1,0:T(8,128)S(1)}, f32[3,1,16,128]{3,2,1,0:T(8,128)S(1)}, u32[]{:S(2)}, u32[]{:S(2)}) %collective-permute-start.13) | collective-permute-done | bytes 24608 | tf_op jit(solution)/shard_map/ppermute | solution.py:45
  251.4 1.9 finish.1
  (60 shorter events, 0.9 us)
Async XLA Ops:
  0.0 14.6 %copy-start.14 = (s32[2,1]{0,1:T(1,128)S(1)}, s32[2,1]{0,1:T(1,128)}, u32[]{:S(2)}) copy-start(s32[2,1]{0,1:T(1,128)} %param.19) | copy-start | bytes 28
  3.5 12.7 %copy-start.12 = (f32[3,1152]{1,0:T(4,128)S(1)}, f32[3,1152]{1,0:T(4,128)}, u32[]{:S(2)}) copy-start(f32[3,1152]{1,0:T(4,128)} %param.28) | copy-start | bytes 41476
  3.5 12.7 %copy-start.13 = (f32[3,1152]{1,0:T(4,128)S(1)}, f32[3,1152]{1,0:T(4,128)}, u32[]{:S(2)}) copy-start(f32[3,1152]{1,0:T(4,128)} %param.27) | copy-start | bytes 41476
  3.5 33.5 %copy-start = (bf16[2,64,1280]{2,1,0:T(8,128)(2,1)S(1)}, bf16[2,64,1280]{2,1,0:T(8,128)(2,1)}, u32[]{:S(2)}) copy-start(bf16[2,64,1280]{2,1,0:T(8,128)(2,1)} %constant.53.clone.pick_ref) | copy-start | bytes 983044
  3.5 33.5 %copy-start.5 = (bf16[96,128]{1,0:T(8,128)(2,1)S(1)}, bf16[96,128]{1,0:T(8,128)(2,1)}, u32[]{:S(2)}) copy-start(bf16[96,128]{1,0:T(8,128)(2,1)} %constant.54.clone.order_ref) | copy-start | bytes 73732
  3.5 33.5 %all-to-all-start.1 = ((bf16[32,40,384]{2,1,0:T(8,128)(2,1)}), bf16[32,40,384]{2,1,0:T(8,128)(2,1)S(1)}, u32[]{:S(2)}, u32[]{:S(2)}) async-start(bf16[32,40,384]{2,1,0:T(8,128)(2,1)} %broadcast_in_dim.47), calls=%async_computation.1 | async-start | bytes 1966080 | tf_op jit(solution)/shard_map/all_to_all | solution.py:49
  38.5 19.6 %collective-permute-start = (bf16[96,1280]{1,0:T(8,128)(2,1)S(1)}, bf16[96,1280]{1,0:T(8,128)(2,1)S(1)}, u32[]{:S(2)}, u32[]{:S(2)}) collective-permute-start(bf16[96,1280]{1,0:T(8,128)(2,1)S(1)} %get-tuple-element.21), channel_id=1, source_target_pairs={{0,8},{1,9},{2,10},{3,11},{4,12},{5,13},{6,14},{7,15},{8,0},{9,1},... | collective-permute-start | bytes 737288 | tf_op jit(solution)/shard_map/ppermute | solution.py:39
  58.2 20.8 %collective-permute-start.1 = (bf16[2,96,1280]{2,1,0:T(8,128)(2,1)S(1)}, bf16[2,96,1280]{2,1,0:T(8,128)(2,1)S(1)}, u32[]{:S(2)}, u32[]{:S(2)}) collective-permute-start(bf16[2,96,1280]{2,1,0:T(8,128)(2,1)S(1)} %pad_maximum_fusion), channel_id=1, source_target_pairs={{0,2},{1,3},{2,0},{3,1},{4,6},{5,7},{6,4},{7,5},{8,10},{9,11},{10,... | collective-permute-start | bytes 1474568 | tf_op jit(solution)/shard_map/ppermute | solution.py:39
  61.4 29.0 %all-to-all-start.2 = ((bf16[16,80,128]{2,1,0:T(8,128)(2,1)}), bf16[16,80,128]{2,1,0:T(8,128)(2,1)S(1)}, u32[]{:S(2)}, u32[]{:S(2)}) async-start(bf16[16,80,128]{2,1,0:T(8,128)(2,1)} %get-tuple-element.16), calls=%async_computation.2 | async-start | bytes 655360 | tf_op jit(solution)/shard_map/all_to_all | solution.py:49
  71.5 18.0 %collective-permute-start.2 = (bf16[2,96,1280]{2,1,0:T(8,128)(2,1)S(1)}, bf16[2,96,1280]{2,1,0:T(8,128)(2,1)S(1)}, u32[]{:S(2)}, u32[]{:S(2)}) collective-permute-start(bf16[2,96,1280]{2,1,0:T(8,128)(2,1)S(1)} %pad_maximum_fusion), channel_id=1, source_target_pairs={{0,4},{1,5},{2,6},{3,7},{4,0},{5,1},{6,2},{7,3},{8,12},{9,13},{10,... | collective-permute-start | bytes 1474568 | tf_op jit(solution)/shard_map/ppermute | solution.py:39
  74.6 26.1 %collective-permute-start.3 = (bf16[2,96,1280]{2,1,0:T(8,128)(2,1)S(1)}, bf16[2,96,1280]{2,1,0:T(8,128)(2,1)S(1)}, u32[]{:S(2)}, u32[]{:S(2)}) collective-permute-start(bf16[2,96,1280]{2,1,0:T(8,128)(2,1)S(1)} %pad_maximum_fusion), channel_id=1, source_target_pairs={{0,6},{1,7},{2,4},{3,5},{4,2},{5,3},{6,0},{7,1},{8,14},{9,15},{10,... | collective-permute-start | bytes 1474568 | tf_op jit(solution)/shard_map/ppermute | solution.py:39
  90.3 22.2 %all-to-all-start = ((bf16[16,64,128]{2,1,0:T(8,128)(2,1)}), bf16[16,64,128]{2,1,0:T(8,128)(2,1)S(1)}, u32[]{:S(2)}, u32[]{:S(2)}) async-start(bf16[16,64,128]{2,1,0:T(8,128)(2,1)} %prep.1), calls=%async_computation | async-start | bytes 524288 | tf_op jit(solution)/shard_map/all_to_all | solution.py:49
  101.5 39.3 %copy-start.1 = (bf16[80,72]{1,0:T(8,128)(2,1)S(1)}, bf16[80,72]{1,0:T(8,128)(2,1)}, u32[]{:S(2)}) copy-start(bf16[80,72]{1,0:T(8,128)(2,1)} %constant.55.clone.widen_ref) | copy-start | bytes 34564
  101.5 40.0 %collective-permute-start.4 = (bf16[8,96,1280]{2,1,0:T(8,128)(2,1)}, bf16[8,96,1280]{2,1,0:T(8,128)(2,1)}, u32[]{:S(2)}, u32[]{:S(2)}) collective-permute-start(bf16[8,96,1280]{2,1,0:T(8,128)(2,1)} %constant_dynamic-update-slice_fusion), channel_id=1, source_target_pairs={{0,1},{1,0},{2,3},{3,2},{4,5},{5,4},{6,7},{7,6},{8,9},{9,8},{10,11... | collective-permute-start | bytes 5898248 | tf_op jit(solution)/shard_map/ppermute | solution.py:39
  135.5 53.4 %all-to-all-start.5 = ((bf16[16,144,128]{2,1,0:T(8,128)(2,1)}), bf16[16,144,128]{2,1,0:T(8,128)(2,1)S(1)}, u32[]{:S(2)}, u32[]{:S(2)}) async-start(bf16[16,144,128]{2,1,0:T(8,128)(2,1)} %get-tuple-element.23), calls=%async_computation.5 | async-start | bytes 1179648 | tf_op jit(solution)/shard_map/all_to_all | solution.py:49
  141.5 1.5 copy-start.3
  143.1 34.6 %copy-start.11 = (f32[1,4,16,128]{3,2,1,0:T(8,128)S(1)}, f32[1,4,16,128]{3,2,1,0:T(8,128)}, u32[]{:S(2)}) copy-start(f32[1,4,16,128]{3,2,1,0:T(8,128)} %param.17) | copy-start | bytes 98308
  143.1 38.9 %copy-start.10 = (f32[16,27,16]{1,2,0:T(8,128)S(1)}, f32[16,27,16]{1,2,0:T(8,128)}, u32[]{:S(2)}) copy-start(f32[16,27,16]{1,2,0:T(8,128)} %param.29) | copy-start | bytes 82948
  143.1 43.8 %copy-start.2 = (f32[1,4,16,128]{3,2,1,0:T(8,128)S(1)}, f32[1,4,16,128]{3,2,1,0:T(8,128)}, u32[]{:S(2)}) copy-start(f32[1,4,16,128]{3,2,1,0:T(8,128)} %param.18) | copy-start | bytes 98308
  156.7 53.0 %copy-start.4 = (bf16[8,96,1280]{2,1,0:T(8,128)(2,1)S(1)}, bf16[8,96,1280]{2,1,0:T(8,128)(2,1)}, u32[]{:S(2)}) copy-start(bf16[8,96,1280]{2,1,0:T(8,128)(2,1)} %constant_dynamic-update-slice_fusion) | copy-start | bytes 5898244
  156.7 6.9 %collective-permute-start.5 = (f32[4,16,128]{2,1,0:T(8,128)S(1)}, f32[4,16,128]{2,1,0:T(8,128)S(1)}, u32[]{:S(2)}, u32[]{:S(2)}) collective-permute-start(f32[4,16,128]{2,1,0:T(8,128)S(1)} %frame_block.2), channel_id=1, source_target_pairs={{16,0},{32,16},{48,32},{64,48},{80,64},{96,80},{112,96},{128,112},... | collective-permute-start | bytes 98312 | tf_op jit(solution)/shard_map/ppermute | solution.py:45
  159.2 7.8 %collective-permute-start.6 = (f32[4,16,128]{2,1,0:T(8,128)S(1)}, f32[4,16,128]{2,1,0:T(8,128)S(1)}, u32[]{:S(2)}, u32[]{:S(2)}) collective-permute-start(f32[4,16,128]{2,1,0:T(8,128)S(1)} %frame_block.2), channel_id=1, source_target_pairs={{32,0},{48,16},{64,32},{80,48},{96,64},{112,80},{128,96},{144,112}... | collective-permute-start | bytes 98312 | tf_op jit(solution)/shard_map/ppermute | solution.py:45
  167.1 16.9 %collective-permute-start.7 = (f32[3,1,16,128]{3,2,1,0:T(8,128)S(1)}, f32[3,1,16,128]{3,2,1,0:T(8,128)S(1)}, u32[]{:S(2)}, u32[]{:S(2)}) collective-permute-start(f32[3,1,16,128]{3,2,1,0:T(8,128)S(1)} %get-tuple-element.29), channel_id=1, source_target_pairs={{0,1},{1,2},{2,3},{3,4},{4,5},{5,6},{6,7},{7,8},{8,9},{9,10},{10,1... | collective-permute-start | bytes 73736 | tf_op jit(solution)/shard_map/ppermute | solution.py:45
  175.7 11.2 %collective-permute-start.8 = (f32[3,1,16,128]{3,2,1,0:T(8,128)S(1)}, f32[3,1,16,128]{3,2,1,0:T(8,128)S(1)}, u32[]{:S(2)}, u32[]{:S(2)}) collective-permute-start(f32[3,1,16,128]{3,2,1,0:T(8,128)S(1)} %get-tuple-element.30), channel_id=1, source_target_pairs={{1,0},{2,1},{3,2},{4,3},{5,4},{6,5},{7,6},{8,7},{9,8},{10,9},{11,1... | collective-permute-start | bytes 73736 | tf_op jit(solution)/shard_map/ppermute | solution.py:45
  178.3 8.6 %collective-permute-start.9 = (f32[5,16,128]{2,1,0:T(8,128)S(1)}, f32[5,16,128]{2,1,0:T(8,128)S(1)}, u32[]{:S(2)}, u32[]{:S(2)}) collective-permute-start(f32[5,16,128]{2,1,0:T(8,128)S(1)} %concatenate.48), channel_id=1, source_target_pairs={{16,0},{32,16},{48,32},{64,48},{80,64},{96,80},{112,96},{128,112},... | collective-permute-start | bytes 122888 | tf_op jit(solution)/shard_map/ppermute | solution.py:45
  188.9 20.8 %all-to-all-start.4 = ((bf16[16,64,128]{2,1,0:T(8,128)(2,1)}), bf16[16,64,128]{2,1,0:T(8,128)(2,1)S(1)}, u32[]{:S(2)}, u32[]{:S(2)}) async-start(bf16[16,64,128]{2,1,0:T(8,128)(2,1)} %get-tuple-element.22), calls=%async_computation.4 | async-start | bytes 524288 | tf_op jit(solution)/shard_map/all_to_all | solution.py:49
  198.7 0.8 copy-start.6
  199.5 0.7 copy-start.8
  209.7 1.0 copy-start.7
  210.8 1.0 copy-start.9
  225.3 5.3 %collective-permute-start.10 = (f32[4,16,128]{2,1,0:T(8,128)S(1)}, f32[4,16,128]{2,1,0:T(8,128)S(1)}, u32[]{:S(2)}, u32[]{:S(2)}) collective-permute-start(f32[4,16,128]{2,1,0:T(8,128)S(1)} %frame_block.3), channel_id=1, source_target_pairs={{0,16},{16,32},{32,48},{48,64},{64,80},{80,96},{96,112},{112,128},... | collective-permute-start | bytes 98312 | tf_op jit(solution)/shard_map/ppermute | solution.py:45
  227.3 6.8 %collective-permute-start.11 = (f32[4,16,128]{2,1,0:T(8,128)S(1)}, f32[4,16,128]{2,1,0:T(8,128)S(1)}, u32[]{:S(2)}, u32[]{:S(2)}) collective-permute-start(f32[4,16,128]{2,1,0:T(8,128)S(1)} %frame_block.3), channel_id=1, source_target_pairs={{16,0},{32,16},{48,32},{64,48},{80,64},{96,80},{112,96},{128,112},... | collective-permute-start | bytes 98312 | tf_op jit(solution)/shard_map/ppermute | solution.py:45
  234.0 8.1 %collective-permute-start.12 = (f32[3,1,16,128]{3,2,1,0:T(8,128)S(1)}, f32[3,1,16,128]{3,2,1,0:T(8,128)S(1)}, u32[]{:S(2)}, u32[]{:S(2)}) collective-permute-start(f32[3,1,16,128]{3,2,1,0:T(8,128)S(1)} %get-tuple-element.27), channel_id=1, source_target_pairs={{0,1},{1,2},{2,3},{3,4},{4,5},{5,6},{6,7},{7,8},{8,9},{9,10},{10,1... | collective-permute-start | bytes 73736 | tf_op jit(solution)/shard_map/ppermute | solution.py:45
  240.2 11.2 %collective-permute-start.13 = (f32[3,1,16,128]{3,2,1,0:T(8,128)S(1)}, f32[3,1,16,128]{3,2,1,0:T(8,128)S(1)}, u32[]{:S(2)}, u32[]{:S(2)}) collective-permute-start(f32[3,1,16,128]{3,2,1,0:T(8,128)S(1)} %get-tuple-element.28), channel_id=1, source_target_pairs={{1,0},{2,1},{3,2},{4,3},{5,4},{6,5},{7,6},{8,7},{9,8},{10,9},{11,1... | collective-permute-start | bytes 73736 | tf_op jit(solution)/shard_map/ppermute | solution.py:45
where the time goes:
time: 255 us; the launch traced here: 253 us
  starting transfers between devices  98.5 us (39%)
  waiting for transfers between devices  73.4 us (29%)
  Pallas kernels  39.5 us (15%)
  blocking collectives  23 us (9%)
  local copies, waits for them, and re-layouts  16.7 us (7%)
    all_to_all x5, starting transfers between devices, exchanged(): return lax.all_to_all(copies, axis, split_axis=0, concat_axis=0, tiled=True)  44.5 us
    all_to_all x5, waiting for transfers between devices, exchanged(): return lax.all_to_all(copies, axis, split_axis=0, concat_axis=0, tiled=True)  35.2 us
    ppermute x9, starting transfers between devices, shifted(): return lax.ppermute(block, axis, route)  34.3 us
    pallas_call x2, Pallas kernels, frame_block(): pl.pallas_call(functools.partial(block_kernel, step), out_shape=jax.Shape...  27.2 us
    all_to_all x1, blocking collectives, exchanged(): return lax.all_to_all(copies, axis, split_axis=0, concat_axis=0, tiled=True)  23 us
    ppermute x5, starting transfers between devices, swapped(): return lax.ppermute(block, axis, [(i, i ^ mask) for i in range(size)])  19.7 us
    ppermute x9, waiting for transfers between devices, shifted(): return lax.ppermute(block, axis, route)  19.2 us
    ppermute x5, waiting for transfers between devices, swapped(): return lax.ppermute(block, axis, [(i, i ^ mask) for i in range(size)])  19 us
  transfers between devices with their start and end apart: 19, of which 11 were waited for; matrix products, arithmetic and copies ran while one was open for 4% of the time, Pallas kernels for 9%

commit v1 on v0

--- a/solution.py
+++ b/solution.py
@@ -29,14 +29,18 @@
 SIGMA_RATIO = 1000.0
 NORM_EPS = 1e-06
 
+AXES = ("zl", "y", "zh", "x", "core")
+SPLIT = (4, 8, 2, 4, 2)
+TM_AXES = AXES[:2]
+TILE_AXES = AXES[2:]
+
 F32 = jnp.float32
 BF16 = jnp.bfloat16
 HIGHEST = lax.Precision.HIGHEST
 
 
-def swapped(block, axis, mask):
-    size = lax.axis_size(axis)
-    return lax.ppermute(block, axis, [(i, i ^ mask) for i in range(size)])
+def swapped(block, axis):
+    return lax.ppermute(block, axis, [(0, 1), (1, 0)])
 
 
 def shifted(block, axis, distance):
@@ -107,45 +111,77 @@
         out_ref[t] = rows
 
 
-def refined_rows(noise_ref, mix_ref):
+def columns_around(x):
     lane = lax.broadcasted_iota(jnp.int32, (C, LANES), 1)
-    tri = {}
-    for td in range(3):
-        for row in range(6):
-            x = noise_ref[td, row]
-            before = jnp.where(lane == 0, 0.0, pltpu.roll(x, 1, 1))
-            after = jnp.where(lane == LANES - 1, 0.0, pltpu.roll(x, LANES - 1, 1))
-            tri[td, row] = [before, x, after]
+    before = jnp.where(lane == 0, 0.0, pltpu.roll(x, 1, 1))
+    after = jnp.where(lane == LANES - 1, 0.0, pltpu.roll(x, LANES - 1, 1))
+    return jnp.concatenate([before, x, after], axis=0)
+
+
+def convolved(frames, mix_ref):
+    around = [[None if x is None else columns_around(x) for x in rows] for rows in frames]
+    blank = jnp.zeros((3 * C, LANES), F32)
     columns = []
-    for r in range(4):
-        pieces = []
-        for td in range(3):
-            for dr in range(3):
-                pieces += tri[td, r + dr]
+    for r in range(len(frames[0]) - 2):
+        pieces = [
+            blank if around[td][r + dr] is None else around[td][r + dr]
+            for td in range(3)
+            for dr in range(3)
+        ]
         columns.append(jnp.concatenate(pieces, axis=0))
-    cells = jnp.concatenate(columns, axis=1)
-    mixed = nn(mix_ref[...], cells, HIGHEST)
-    return [noise_ref[1, r + 1] + mixed[:, r * LANES : (r + 1) * LANES] for r in range(4)]
-
-
-def middle_kernel(scalar_ref, flag_ref, noise_ref, lat_ref, new_ref, mix_ref, lat_out, patch_out):
-    refined = refined_rows(noise_ref, mix_ref)
+    mixed = nn(mix_ref[...], jnp.concatenate(columns, axis=1), HIGHEST)
+    return [mixed[:, r * LANES : (r + 1) * LANES] for r in range(len(columns))]
+
+
+def middle_kernel(
+    scalar_ref, flag_ref, noise_ref, next_ref, after_ref, lat_ref, new_ref, mix_ref,
+    lat_out, edge_out, patch_out,
+):
+    frames = [
+        [None, None] + [ref[r] for r in range(4)] + [None, None]
+        for ref in (noise_ref, next_ref, after_ref)
+    ]
+    mixed = convolved(frames, mix_ref)
     last = flag_ref[0] == 1
+    drop = lat_ref[4, 0:1, :]
     rows = []
     for r in range(4):
-        moved = lat_ref[r] + lat_ref[4, 0:1, :] * refined[r]
+        moved = lat_ref[r] + drop * (next_ref[r] + mixed[r + 1])
         rows.append(jnp.where(last, new_ref[r], moved))
         lat_out[r] = rows[r]
-    scaled = (jnp.stack(rows) * scalar_ref[0]).astype(BF16)
-    patches = patch_rows(scaled)
+    above = jnp.where(last, 0.0, drop * mixed[0])
+    below = jnp.where(last, 0.0, drop * mixed[5])
+    edge_out[0] = above
+    edge_out[1] = below
+    patches = patch_rows((jnp.stack(rows) * scalar_ref[0]).astype(BF16))
+    above = (above * scalar_ref[0]).astype(BF16)
+    below = (below * scalar_ref[0]).astype(BF16)
+    edges = [
+        nn(above, spread_matrix((LANES, TOK), 1, 0, b, BF16))
+        + nn(below, spread_matrix((LANES, TOK), 1, 1, b, BF16))
+        for b in range(2)
+    ]
+    patches = jnp.concatenate([patches, jnp.concatenate(edges, axis=0).astype(BF16)], axis=0)
     for t in range(TILE):
         patch_out[t] = patches
 
 
-def final_kernel(scalar_ref, noise_ref, lat_ref, mix_ref, out_ref):
-    refined = refined_rows(noise_ref, mix_ref)
+def final_kernel(
+    scalar_ref, before_ref, noise_ref, next_ref, up_ref, down_ref, lat_ref, above_ref, below_ref,
+    mix_ref, out_ref,
+):
+    frames = [
+        [up_ref[td]] + [ref[r] for r in range(4)] + [down_ref[td]]
+        for td, ref in enumerate((before_ref, noise_ref, next_ref))
+    ]
+    mixed = convolved(frames, mix_ref)
     for r in range(4):
-        out_ref[r] = lat_ref[r] + scalar_ref[0] * refined[r]
+        latent = lat_ref[r]
+        if r == 0:
+            latent = latent + above_ref[...]
+        if r == 3:
+            latent = latent + below_ref[...]
+        out_ref[r] = latent + scalar_ref[0] * (noise_ref[r] + mixed[r])
 
 
 def spread_kernel(x_ref, pick_ref, emb_ref, mod_ref, order_ref, pay_ref, out_t_ref):
@@ -231,20 +267,37 @@
         mvt_ref[h] = nn(widen_ref[...], v).astype(BF16)
 
 
-def block_kernel(
-    step, spot_ref, pt_ref, gram_ref, n_ref, mvt_ref, feat_ref, wot_ref, wot2_ref, out_ref,
-    keys_t, keys, att, stream_ref,
+def with_edges(pt_ref, j):
+    patches = pt_ref[j].astype(F32)[0:PF]
+    lane = lane_of((2 * C, LANES))
+    blank = jnp.zeros((2 * C, LANES), F32)
+    first, last = blank, blank
+    if j > 0:
+        edge = pltpu.roll(pt_ref[j - 1].astype(F32)[PF : PF + 2 * C], PF, 1)
+        first = jnp.where(lane < PF, edge, 0.0)
+    if j < TILE - 1:
+        edge = pltpu.roll(pt_ref[j + 1].astype(F32)[PF : PF + 2 * C], PF, 1)
+        last = jnp.where(lane >= PF, edge, 0.0)
+    added = jnp.concatenate([first[0:C], last[0:C], first[C:], last[C:]], axis=0)
+    return (patches + added).astype(BF16)
+
+
+def attend_kernel(
+    edges, spot_ref, pt_ref, gram_ref, n_ref, mvt_ref, att_ref, own_ref, keys_t, keys, held
 ):
     me = spot_ref[0]
     row = lax.broadcasted_iota(jnp.int32, (PF, TOK), 0)
     ones = jnp.where(row == 0, 1.0, 0.0).astype(F32)
     for j in range(TILE):
-        patches = pt_ref[j].astype(F32)
+        rounded = with_edges(pt_ref, j) if edges else pt_ref[j]
+        held[j] = rounded
+        patches = rounded.astype(F32)
         spread = jnp.sum(patches * nn(gram_ref[...], patches, HIGHEST), axis=0, keepdims=True)
         unit = patches * lax.rsqrt(jnp.maximum(spread, 0.0) * (1.0 / D) + NORM_EPS)
         wide = jnp.concatenate([unit, ones], axis=0)
         keys_t[:, j * TOK : (j + 1) * TOK] = wide.astype(BF16)
         keys[j * TOK : (j + 1) * TOK, :] = wide.T.astype(BF16)
+    own_ref[...] = held[me]
 
     def two_heads(pair):
         own = keys[pl.ds(pl.multiple_of(me * TOK, TOK), TOK), :]
@@ -259,40 +312,46 @@
         for k in range(2):
             head = 2 * pair + k
             value = nt(mvt_ref[head], mean[k * TOK : (k + 1) * TOK])
-            att[pl.ds(pl.multiple_of(head * 80, 80), 80), :] = value
+            att_ref[pl.ds(pl.multiple_of(head * 80, 80), 80), :] = value.astype(BF16)
 
     @pl.loop(0, HEADS // 4)
     def _(i):
         two_heads(2 * i)
         two_heads(2 * i + 1)
 
-    attended = att[...].astype(BF16)
+
+def output_kernel(
+    step, spot_ref, att_ref, own_ref, feat_ref, wot_ref, wot2_ref, out_ref, stream_ref
+):
+    me = spot_ref[0]
+    attended = att_ref[...]
     for c, ref in enumerate((wot_ref, wot2_ref)):
         delta = nn(ref[...], attended)
         for b in range(8):
-            tile = me ^ (8 * (b % 2) + 2 * (b // 2) + c)
+            tile = ((me ^ (8 * (b % 2))) & 8) + 2 * (b // 2) + ((me & 1) ^ c)
             rows = pl.ds(pl.multiple_of(tile * 80, 80), 80)
-            stream_ref[rows, :] = delta[96 * b : 96 * b + 80]
+            stream_ref[rows, :] = delta[80 * b : 80 * b + 80]
     feat = feat_ref[...]
-    own = jnp.concatenate([pt_ref[me], jnp.zeros((PF, TOK), BF16)], axis=0)
+    own = jnp.concatenate([own_ref[...], jnp.zeros((PF, TOK), BF16)], axis=0)
     at = PF + 3 * step + 2
     gate = feat[:, at : at + 1].astype(F32) + feat[:, at + 6 : at + 7].astype(F32)
-    stream = nn(feat, own) + gate * stream_ref[...]
+    valid = feat[:, 76:77].astype(F32)
+    stream = (nn(feat, own) + gate * stream_ref[...]) * valid
     mean = jnp.sum(stream, axis=0, keepdims=True) * (1.0 / D)
-    center = (stream - mean) * feat[:, 76:77].astype(F32)
+    center = (stream - mean) * valid
     spread = jnp.sum(center * center, axis=0, keepdims=True) * (1.0 / D)
     final = (center * lax.rsqrt(spread + NORM_EPS)).astype(BF16)
     out_rows = [
-        ref[96 * b + 80 : 96 * b + 96, :] for ref in (wot_ref, wot2_ref) for b in range(8)
+        ref[80 * b + 32 : 80 * b + 48, :] for ref in (wot_ref, wot2_ref) for b in range(8)
     ]
     noise = nn(jnp.concatenate(out_rows, axis=0), final)
     feature = lax.broadcasted_iota(jnp.int32, (PF, 256), 0)
     source = lane_of((PF, 256))
     block = source >> 4
-    mask = ((block & 1) << 3) | (((block >> 1) & 3) << 1) | (block >> 3)
-    q = source & 15
-    wanted = ((q & 1) << 5) + ((q >> 1) << 4) + (mask ^ me)
-    order = jnp.where((q < 4) & (feature == wanted), 1.0, 0.0).astype(F32)
+    tile = ((me ^ ((block & 1) << 3)) & 8) + (block & 6) + ((me & 1) ^ (block >> 3))
+    q = (source & 15) - 4
+    wanted = ((q & 1) << 5) + ((q >> 1) << 4) + tile
+    order = jnp.where((q >= 0) & (q < 4) & (feature == wanted), 1.0, 0.0).astype(F32)
     noise = nn(order, noise, HIGHEST)
     for hp in range(2):
         rows = None
@@ -314,7 +373,7 @@
         spread_kernel,
         out_shape=(
             jax.ShapeDtypeStruct((TILE, 80, LANES), BF16),
-            jax.ShapeDtypeStruct((96, WIDE), BF16),
+            jax.ShapeDtypeStruct((80, WIDE), BF16),
         ),
         in_specs=[VMEM] * 5,
         out_specs=(VMEM, VMEM),
@@ -347,29 +406,43 @@
         scratch_shapes=[pltpu.VMEM((3 * HEADS, HEAD, LANES), F32)],
         compiler_params=pltpu.CompilerParams(vmem_limit_bytes=32 * 1024 * 1024),
         name="heads",
-    )(folded, jnp.asarray(ORDER[0:80, 0:HEAD], BF16))
-
-
-def frame_block(step, spot, pt, gram, n, mvt, feat, wot, wot2):
-    return pl.pallas_call(
-        functools.partial(block_kernel, step),
-        out_shape=jax.ShapeDtypeStruct((4, C, LANES), F32),
-        in_specs=[SMEM] + [VMEM] * 7,
-        out_specs=VMEM,
+    )(folded, jnp.asarray(ORDER[:, 0:HEAD], BF16))
+
+
+def attend(edges, spot, pt, gram, n, mvt):
+    return pl.pallas_call(
+        functools.partial(attend_kernel, edges),
+        out_shape=(
+            jax.ShapeDtypeStruct((WIDE, TOK), BF16),
+            jax.ShapeDtypeStruct((PF, TOK), BF16),
+        ),
+        in_specs=[SMEM] + [VMEM] * 4,
+        out_specs=(VMEM, VMEM),
         scratch_shapes=[
             pltpu.VMEM((LANES, SPAN), BF16),
             pltpu.VMEM((SPAN, LANES), BF16),
-            pltpu.VMEM((WIDE, TOK), F32),
-            pltpu.VMEM((WIDE, TOK), F32),
+            pltpu.VMEM((TILE, PF, TOK), BF16),
         ],
-        compiler_params=pltpu.CompilerParams(vmem_limit_bytes=48 * 1024 * 1024),
+        compiler_params=pltpu.CompilerParams(vmem_limit_bytes=40 * 1024 * 1024),
         cost_estimate=pl.CostEstimate(
-            flops=2 * 2 * SPAN * SPAN * LANES + 2 * D * D * TOK,
-            bytes_accessed=2 * D * D + 4 * SPAN * LANES,
+            flops=4 * 2 * SPAN * SPAN * LANES,
+            bytes_accessed=8 * SPAN * LANES,
             transcendentals=SPAN * SPAN,
         ),
-        name="frame_block",
-    )(spot, pt, gram, n, mvt, feat, wot, wot2)
+        name="attend",
+    )(spot, pt, gram, n, mvt)
+
+
+def output(step, spot, att, own, feat, wot, wot2):
+    return pl.pallas_call(
+        functools.partial(output_kernel, step),
+        out_shape=jax.ShapeDtypeStruct((4, C, LANES), F32),
+        in_specs=[SMEM] + [VMEM] * 5,
+        out_specs=VMEM,
+        scratch_shapes=[pltpu.VMEM((WIDE, TOK), F32)],
+        compiler_params=pltpu.CompilerParams(vmem_limit_bytes=32 * 1024 * 1024),
+        name="output",
+    )(spot, att, own, feat, wot, wot2)
 
 
 def prep(scale_in, latent):
@@ -382,35 +455,30 @@
     )(scale_in, latent)
 
 
-def middle(scale_in, last, noise, lat, new, mix):
+def middle(scale_in, last, noise, following, after, lat, new, mix):
     return pl.pallas_call(
         middle_kernel,
         out_shape=(
             jax.ShapeDtypeStruct((4, C, LANES), F32),
-            jax.ShapeDtypeStruct((TILE, PF, TOK), BF16),
+            jax.ShapeDtypeStruct((2, C, LANES), F32),
+            jax.ShapeDtypeStruct((TILE, PF + 2 * C, TOK), BF16),
         ),
-        in_specs=[SMEM, SMEM] + [VMEM] * 4,
-        out_specs=(VMEM, VMEM),
+        in_specs=[SMEM, SMEM] + [VMEM] * 6,
+        out_specs=(VMEM,) * 3,
         compiler_params=pltpu.CompilerParams(vmem_limit_bytes=32 * 1024 * 1024),
         name="middle",
-    )(scale_in, last, noise, lat, new, mix)
-
-
-def finish(drop, noise, lat, mix):
+    )(scale_in, last, noise, following, after, lat, new, mix)
+
+
+def finish(drop, before, noise, following, up, down, lat, above, below, mix):
     return pl.pallas_call(
         final_kernel,
         out_shape=jax.ShapeDtypeStruct((4, C, LANES), F32),
-        in_specs=[SMEM] + [VMEM] * 3,
+        in_specs=[SMEM] + [VMEM] * 9,
         out_specs=VMEM,
         compiler_params=pltpu.CompilerParams(vmem_limit_bytes=32 * 1024 * 1024),
         name="finish",
-    )(drop, noise, lat, mix)
-
-
-def with_rows(frames):
-    before = shifted(frames[:, 3:4], "tile", 1)
-    after = shifted(frames[:, 0:1], "tile", -1)
-    return jnp.concatenate([before, frames, after], axis=1)
+    )(drop, before, noise, following, up, down, lat, above, below, mix)
 
 
 def pick_matrix():
@@ -424,12 +492,12 @@
 
 
 def order_matrix():
-    order = np.zeros((96, LANES), np.float32)
+    order = np.zeros((80, LANES), np.float32)
     for j in range(ROWS):
         order[j, j] = 1.0
         order[40 + j, ROWS + j] = 1.0
     for j in range(4):
-        order[80 + j, HEAD + j] = 1.0
+        order[ROWS + j, HEAD + j] = 1.0
     return order
 
 
@@ -465,8 +533,8 @@
     latents, new_frames, levels, offset, w_in, w_qkv, w_o, w_out, w_time, w_pos,
     mod_gain, mod_bias, refiner,
 ):
-    frame = lax.axis_index("tm")
-    tile = lax.axis_index("tile")
+    frame = lax.axis_index(TM_AXES)
+    tile = lax.axis_index(TILE_AXES)
     spot = tile.astype(jnp.int32)[None]
     mix = refiner.reshape(C, 27 * C)
     latent = latents[0]
@@ -476,59 +544,70 @@
     scale_in = lax.rsqrt(1.0 + sigma_now * sigma_now)
 
     packed = packed_weights(w_in, w_qkv, w_o, w_out, w_time, w_pos)
-    rows = exchanged(jnp.broadcast_to(packed[None], (TM,) + packed.shape), "tm")
+    rows = exchanged(jnp.broadcast_to(packed[None], (TM,) + packed.shape), TM_AXES)
     rows = rows.reshape(WIDE, 384)
 
-    patches = exchanged(prep(scale_in[0:1], latent), "tile")
+    patches = exchanged(prep(scale_in[0:1], latent), TILE_AXES)
     marked = jnp.concatenate([latent, jnp.full((1, C, LANES), drop[0], F32)], axis=0)
-    marked = shifted(marked, "tm", -1)
-
+    marked = shifted(marked, TM_AXES, -1)
     steps = jnp.arange(STEPS, dtype=jnp.int32)
     emb = embeddings(level, offset + frame + steps)
-    pay, out_t = spread(rows, emb, own_mods(mod_gain, mod_bias, tile))
-    feat = exchanged(pay, "tile").reshape(WIDE, LANES)
+    mods = own_mods(mod_gain, mod_bias, tile)
+    rows, patches, marked, mix = lax.optimization_barrier((rows, patches, marked, mix))
+
+    pay, out_t = spread(rows, emb, mods)
+    feat = exchanged(pay, TILE_AXES).reshape(WIDE, LANES)
+    feat, out_t = lax.optimization_barrier((feat, out_t))
 
     first, second, gram = fold(feat, rows)
-    folded = [exchanged(first, "tile"), exchanged(second, "tile")]
-
-    both = jnp.stack([out_t, swapped(out_t, "tile", 8)])
-    four = jnp.concatenate([both] + [swapped(both, "tile", 2 * k) for k in (1, 2, 3)])
-    other = swapped(four, "tile", 1)
-    four = four.reshape(8 * 96, WIDE)
-    other = other.reshape(8 * 96, WIDE)
-
-    for step in range(STEPS):
-        n, mvt = heads(folded[step])
-        noise = frame_block(step, spot, patches, gram, n, mvt, feat, four, other)
-        if step == 0:
-            frames = jnp.stack([noise, shifted(noise, "tm", -1), shifted(noise, "tm", -2)])
-            last = (frame == TM - 1).astype(jnp.int32)[None]
-            latent, patches = middle(
-                scale_in[1:2], last, with_rows(frames), marked, new_frames[0], mix
-            )
-            patches = exchanged(patches, "tile")
-        else:
-            frames = jnp.stack([shifted(noise, "tm", 1), noise, shifted(noise, "tm", -1)])
-            return finish(drop[1:2], with_rows(frames), latent, mix)[None]
+    n, mvt = heads(exchanged(first, TILE_AXES))
+
+    both = jnp.stack([out_t, swapped(out_t, "zh")])
+    four = exchanged(jnp.broadcast_to(both[None], (4,) + both.shape), "x")
+    other = swapped(four, "core").reshape(8 * 80, WIDE)
+    four = four.reshape(8 * 80, WIDE)
+
+    att, own = attend(False, spot, patches, gram, n, mvt)
+    noise = output(0, spot, att, own, feat, four, other)
+
+    following, after = shifted(noise, TM_AXES, -1), shifted(noise, TM_AXES, -2)
+    last = (frame == TM - 1).astype(jnp.int32)[None]
+    latent, edges, patches = middle(
+        scale_in[1:2], last, noise, following, after, marked, new_frames[0], mix
+    )
+    patches, second = lax.optimization_barrier((patches, second))
+    patches = exchanged(patches, TILE_AXES)
+    n, mvt = heads(exchanged(second, TILE_AXES))
+    above = shifted(edges[1], TILE_AXES, 1)
+    below = shifted(edges[0], TILE_AXES, -1)
+
+    att, own = attend(True, spot, patches, gram, n, mvt)
+    noise = output(1, spot, att, own, feat, four, other)
+    frames = [shifted(noise, TM_AXES, 1), noise, shifted(noise, TM_AXES, -1)]
+    up = shifted(jnp.stack([x[3] for x in frames]), TILE_AXES, 1)
+    down = shifted(jnp.stack([x[0] for x in frames]), TILE_AXES, -1)
+    return finish(drop[1:2], *frames, up, down, latent, above, below, mix)[None]
 
 
 def solution(mesh):
+    mesh = jax.sharding.Mesh(mesh.devices.reshape(SPLIT), AXES)
+    rows, cols = TM_AXES, TILE_AXES
     in_specs = (
-        P("tm", "tile", None, None),
-        P(None, "tile", None, None),
-        P(None, "tm"),
+        P(rows, cols, None, None),
+        P(None, cols, None, None),
+        P(None, rows),
         P(),
-        P("tm", "tile"),
-        P("tm", "tile"),
-        P("tm", "tile"),
-        P("tm", "tile"),
-        P("tm", "tile"),
-        P("tm", "tile"),
+        P(rows, cols),
+        P(rows, cols),
+        P(rows, cols),
+        P(rows, cols),
+        P(rows, cols),
+        P(rows, cols),
         P(),
         P(),
         P(),
     )
-    out_specs = P("tm", "tile", None, None)
+    out_specs = P(rows, cols, None, None)
     return jax.shard_map(
         per_device, mesh=mesh, in_specs=in_specs, out_specs=out_specs, check_vma=False
     )

time: 255 us -> 266 us (1.043)
  the two profiles are of different devices: /device:TPU:191 before, /device:TPU:31 now
where the time goes in v1:
time: 266 us; the launch traced here: 265 us
  blocking collectives  89.3 us (34%)
  starting transfers between devices  76.9 us (29%)
  waiting for transfers between devices  48.3 us (18%)
  Pallas kernels  35 us (13%)
  local copies, waits for them, and re-layouts  12 us (5%)
    all_to_all x4, blocking collectives, exchanged(): return lax.all_to_all(copies, axis, split_axis=0, concat_axis=0, tiled=True)  89.3 us
    ppermute x9, starting transfers between devices, shifted(): return lax.ppermute(block, axis, route)  39.1 us
    all_to_all x3, waiting for transfers between devices, exchanged(): return lax.all_to_all(copies, axis, split_axis=0, concat_axis=0, tiled=True)  34.8 us
    all_to_all x3, starting transfers between devices, exchanged(): return lax.all_to_all(copies, axis, split_axis=0, concat_axis=0, tiled=True)  31.3 us
    pallas_call x2, Pallas kernels, attend(): pl.pallas_call(functools.partial(attend_kernel, edges), out_shape=(jax.Sh...  19.2 us
    ppermute x2, waiting for transfers between devices, swapped(): return lax.ppermute(block, axis, [(0, 1), (1, 0)])  10.1 us
    ppermute x2, starting transfers between devices, swapped(): return lax.ppermute(block, axis, [(0, 1), (1, 0)])  6.55 us
    unnamed x49, local copies, waits for them, and re-layouts  5.54 us
  transfers between devices with their start and end apart: 14, of which 7 were waited for; matrix products, arithmetic and copies ran while one was open for 3% of the time, Pallas kernels for 5%

profile of v1, /device:TPU:31, one launch (start us, length us, event | category | flops | bytes accessed | tf_op | source)
XLA Modules:
  0.0 264.5 jit_solution(217023833954334059)
XLA Ops:
  0.0 0.7 add_rsqrt_fusion
  0.7 0.6 fusion.8
  1.4 2.3 prep.1
  3.7 13.6 %all-to-all-start.1 = ((bf16[16,64,128]{2,1,0:T(8,128)(2,1)}), bf16[16,64,128]{2,1,0:T(8,128)(2,1)S(1)}, u32[]{:S(2)}, u32[]{:S(2)}) async-start(bf16[16,64,128]{2,1,0:T(8,128)(2,1)} %prep.1), calls=%async_computation.1 | async-start | bytes 524288 | tf_op jit(solution)/shard_map/all_to_all | solution.py:53
  17.2 1.4 concatenate.32
  18.6 2.2 collective-permute-start
  21.5 0.7 pad_maximum_fusion.3
  22.2 0.1 reshape.131
  22.3 0.8 copy.25
  23.1 0.8 concatenate.31
  24.0 0.1 pad.31.clone
  24.1 5.0 %all-to-all-done.1.pt_ref = bf16[16,64,128]{2,1,0:T(8,128)(2,1)S(1)} async-done(((bf16[16,64,128]{2,1,0:T(8,128)(2,1)}), bf16[16,64,128]{2,1,0:T(8,128)(2,1)S(1)}, u32[]{:S(2)}, u32[]{:S(2)}) %all-to-all-start.1) | async-done | bytes 262176 | tf_op jit(solution)/shard_map/all_to_all | solution.py:53
  29.1 1.1 broadcast_in_dim.53
  30.1 10.0 %all-to-all-start = ((bf16[32,40,384]{2,1,0:T(8,128)(2,1)}), bf16[32,40,384]{2,1,0:T(8,128)(2,1)S(1)}, u32[]{:S(2)}, u32[]{:S(2)}) async-start(bf16[32,40,384]{2,1,0:T(8,128)(2,1)} %broadcast_in_dim.53), calls=%async_computation | async-start | bytes 1966080 | tf_op jit(solution)/shard_map/all_to_all | solution.py:53
  40.2 0.1 fusion
  40.4 0.1 copy.27
  40.6 0.1 pad.26.clone
  40.6 0.1 maximum_maximum_fusion
  40.7 0.1 reshape.134
  40.8 0.3 mul.104
  41.1 0.4 mul.105
  41.6 0.4 mul.108
  42.0 0.1 reshape.135
  42.1 0.1 copy.31
  42.2 0.2 copy.26
  42.4 0.8 reshape.133.mix_ref
  43.2 0.6 copy-done.9
  43.8 20.7 %all-to-all-done = bf16[32,40,384]{2,1,0:T(8,128)(2,1)S(1)} async-done(((bf16[32,40,384]{2,1,0:T(8,128)(2,1)}), bf16[32,40,384]{2,1,0:T(8,128)(2,1)S(1)}, u32[]{:S(2)}, u32[]{:S(2)}) %all-to-all-start) | async-done | bytes 983072 | tf_op jit(solution)/shard_map/all_to_all | solution.py:53
  64.5 0.8 spread.1
  65.3 17.4 %all_to_all.35 = bf16[16,80,128]{2,1,0:T(8,128)(2,1)S(1)} all-to-all(bf16[16,80,128]{2,1,0:T(8,128)(2,1)S(1)} %get-tuple-element.31), channel_id=1, replica_groups=mesh['zl'=4,'y'=8,'zh'=2,'x'=4,'core'=2] {'zh','x','core'}, dimensions={0} | all-to-all | bytes 655360 | tf_op jit(solution)/shard_map/all_to_all | solution.py:53
  82.7 2.2 collective-permute-start.1
  84.9 10.1 %collective-permute-done.1 = bf16[80,1280]{1,0:T(8,128)(2,1)S(1)} collective-permute-done((bf16[80,1280]{1,0:T(8,128)(2,1)S(1)}, bf16[80,1280]{1,0:T(8,128)(2,1)S(1)}, u32[]{:S(2)}, u32[]{:S(2)}) %collective-permute-start.1) | collective-permute-done | bytes 204832 | tf_op jit(solution)/shard_map/ppermute | solution.py:43
  95.0 0.1 broadcast_in_dim.56
  95.1 22.0 %all_to_all.36 = bf16[4,2,80,1280]{3,2,1,0:T(8,128)(2,1)S(1)} all-to-all(bf16[4,2,80,1280]{3,2,1,0:T(8,128)(2,1)S(1)} %broadcast_in_dim.56), channel_id=1, replica_groups=mesh['zl'=4,'y'=8,'zh'=2,'x'=4,'core'=2] {'x'}, dimensions={0} | all-to-all | bytes 3276800 | tf_op jit(solution)/shard_map/all_to_all | solution.py:53
  117.1 4.4 %collective-permute-start.2 = (bf16[4,2,80,1280]{3,2,1,0:T(8,128)(2,1)S(1)}, bf16[4,2,80,1280]{3,2,1,0:T(8,128)(2,1)S(1)}, u32[]{:S(2)}, u32[]{:S(2)}) collective-permute-start(bf16[4,2,80,1280]{3,2,1,0:T(8,128)(2,1)S(1)} %all_to_all.36), channel_id=1, source_target_pairs={{0,1},{1,0},{2,3},{3,2},{4,5},{5,4},{6,7},{7,6},{8,9},{9,8},{10,11... | collective-permute-start | bytes 4915208 | tf_op jit(solution)/shard_map/ppermute | solution.py:43
  121.4 2.4 fold.1
  123.8 23.1 %all_to_all.37.folded_ref = bf16[16,144,128]{2,1,0:T(8,128)(2,1)S(1)} all-to-all(bf16[16,144,128]{2,1,0:T(8,128)(2,1)S(1)} %get-tuple-element.35), channel_id=1, replica_groups=mesh['zl'=4,'y'=8,'zh'=2,'x'=4,'core'=2] {'zh','x','core'}, dimensions={0} | all-to-all | bytes 1179648 | tf_op jit(solution)/shard_map/all_to_all | solution.py:53
  146.9 0.8 heads.2
  147.7 9.6 %attend.2 = (bf16[1280,128]{1,0:T(8,128)(2,1)S(1)}, bf16[64,128]{1,0:T(8,128)(2,1)S(1)}) custom-call(s32[1]{0:T(128)} %bitcast.1.spot_ref, bf16[16,64,128]{2,1,0:T(8,128)(2,1)S(1)} %copy-done.6, f32[64,64]{1,0:T(8,128)S(1)} %get-tuple-element.34.gram_ref, bf16[16,128,128]{2,1,0:T(8,128)(2,1)S(1)} %get-tuple-element.36.n_ref, ...), custom_call_target="tpu_custom_call" | custom-call | flops 4294967296 | bytes 2097152 | tf_op jit(solution)/shard_map/attend/pallas_call | solution.py:413
  157.4 2.4 output.2.noise_ref
  159.7 3.8 %collective-permute-start.4 = (f32[4,16,128]{2,1,0:T(8,128)S(1)}, f32[4,16,128]{2,1,0:T(8,128)S(1)}, u32[]{:S(2)}, u32[]{:S(2)}) collective-permute-start(f32[4,16,128]{2,1,0:T(8,128)S(1)} %output.2.noise_ref), channel_id=1, source_target_pairs={{32,0},{48,16},{64,32},{80,48},{96,64},{112,80},{128,96},{144,112}... | collective-permute-start | bytes 98312 | tf_op jit(solution)/shard_map/ppermute | solution.py:49
  163.5 4.6 %collective-permute-start.3 = (f32[4,16,128]{2,1,0:T(8,128)S(1)}, f32[4,16,128]{2,1,0:T(8,128)S(1)}, u32[]{:S(2)}, u32[]{:S(2)}) collective-permute-start(f32[4,16,128]{2,1,0:T(8,128)S(1)} %output.2.noise_ref), channel_id=1, source_target_pairs={{16,0},{32,16},{48,32},{64,48},{80,64},{96,80},{112,96},{128,112},... | collective-permute-start | bytes 98312 | tf_op jit(solution)/shard_map/ppermute | solution.py:49
  168.1 1.2 collective-permute-done.3.next_ref
  169.4 2.3 middle.1
  171.6 0.6 copy-done.12
  172.2 26.8 %all_to_all.38.folded_ref = bf16[16,144,128]{2,1,0:T(8,128)(2,1)S(1)} all-to-all(bf16[16,144,128]{2,1,0:T(8,128)(2,1)S(1)} %get-tuple-element.46), channel_id=1, replica_groups=mesh['zl'=4,'y'=8,'zh'=2,'x'=4,'core'=2] {'zh','x','core'}, dimensions={0} | all-to-all | bytes 1179648 | tf_op jit(solution)/shard_map/all_to_all | solution.py:53
  199.1 7.8 %all-to-all-start.5 = ((bf16[16,96,128]{2,1,0:T(8,128)(2,1)}), bf16[16,96,128]{2,1,0:T(8,128)(2,1)S(1)}, u32[]{:S(2)}, u32[]{:S(2)}) async-start(bf16[16,96,128]{2,1,0:T(8,128)(2,1)} %get-tuple-element.45), calls=%async_computation.5 | async-start | bytes 786432 | tf_op jit(solution)/shard_map/all_to_all | solution.py:53
  206.8 0.7 copy-done.8
  207.6 0.8 heads.3
  208.3 0.7 copy-done.15
  209.1 9.1 %all-to-all-done.5.pt_ref = bf16[16,96,128]{2,1,0:T(8,128)(2,1)S(1)} async-done(((bf16[16,96,128]{2,1,0:T(8,128)(2,1)}), bf16[16,96,128]{2,1,0:T(8,128)(2,1)S(1)}, u32[]{:S(2)}, u32[]{:S(2)}) %all-to-all-start.5) | async-done | bytes 393248 | tf_op jit(solution)/shard_map/all_to_all | solution.py:53
  218.2 1.0 copy-done.16
  219.2 0.8 copy-done.18
  219.9 9.6 %attend.3 = (bf16[1280,128]{1,0:T(8,128)(2,1)S(1)}, bf16[64,128]{1,0:T(8,128)(2,1)S(1)}) custom-call(s32[1]{0:T(128)} %bitcast.1.spot_ref, bf16[16,96,128]{2,1,0:T(8,128)(2,1)S(1)} %all-to-all-done.5.pt_ref, f32[64,64]{1,0:T(8,128)S(1)} %copy-done.18, bf16[16,128,128]{2,1,0:T(8,128)(2,1)S(1)} %get-tuple-element.47.n_ref, bf16[16,80,128]{2,1,0:T(8,128)(2,1)S(1)} %copy-done.16), custom_call_target="tpu_custom_call" | custom-call | flops 4294967296 | bytes 2097152 | tf_op jit(solution)/shard_map/attend/pallas_call | solution.py:413
  229.6 2.4 output.3.noise_ref
  231.9 3.3 %collective-permute-start.6 = (f32[4,16,128]{2,1,0:T(8,128)S(1)}, f32[4,16,128]{2,1,0:T(8,128)S(1)}, u32[]{:S(2)}, u32[]{:S(2)}) collective-permute-start(f32[4,16,128]{2,1,0:T(8,128)S(1)} %output.3.noise_ref), channel_id=1, source_target_pairs={{16,0},{32,16},{48,32},{64,48},{80,64},{96,80},{112,96},{128,112},... | collective-permute-start | bytes 98312 | tf_op jit(solution)/shard_map/ppermute | solution.py:49
  235.2 3.2 %collective-permute-start.5 = (f32[4,16,128]{2,1,0:T(8,128)S(1)}, f32[4,16,128]{2,1,0:T(8,128)S(1)}, u32[]{:S(2)}, u32[]{:S(2)}) collective-permute-start(f32[4,16,128]{2,1,0:T(8,128)S(1)} %output.3.noise_ref), channel_id=1, source_target_pairs={{0,16},{16,32},{32,48},{48,64},{64,80},{80,96},{96,112},{112,128},... | collective-permute-start | bytes 98312 | tf_op jit(solution)/shard_map/ppermute | solution.py:49
  238.5 1.4 collective-permute-done.5.before_ref
  239.9 8.5 %collective-permute-start.7 = (f32[3,16,128]{2,1,0:T(8,128)S(1)}, f32[3,16,128]{2,1,0:T(8,128)S(1)}, u32[]{:S(2)}, u32[]{:S(2)}) collective-permute-start(f32[3,16,128]{2,1,0:T(8,128)S(1)} %pad_maximum_fusion.1), channel_id=1, source_target_pairs={{0,1},{1,2},{2,3},{3,4},{4,5},{5,6},{6,7},{7,8},{8,9},{9,10},{10,1... | collective-permute-start | bytes 73736 | tf_op jit(solution)/shard_map/ppermute | solution.py:49
  248.4 1.9 collective-permute-start.8
  250.4 1.9 collective-permute-start.10
  252.3 9.7 %collective-permute-start.9 = (f32[16,128]{1,0:T(8,128)S(1)}, f32[16,128]{1,0:T(8,128)S(1)}, u32[]{:S(2)}, u32[]{:S(2)}) collective-permute-start(f32[16,128]{1,0:T(8,128)S(1)} %get-tuple-element.60), channel_id=1, source_target_pairs={{0,1},{1,2},{2,3},{3,4},{4,5},{5,6},{6,7},{7,8},{8,9},{9,10},{10,1... | collective-permute-start | bytes 24584 | tf_op jit(solution)/shard_map/ppermute | solution.py:49
  262.0 0.8 collective-permute-done.9.above_ref
  262.7 1.8 finish.1
  (69 shorter events, 0.4 us)
Async XLA Ops:
  3.7 25.4 %all-to-all-start.1 = ((bf16[16,64,128]{2,1,0:T(8,128)(2,1)}), bf16[16,64,128]{2,1,0:T(8,128)(2,1)S(1)}, u32[]{:S(2)}, u32[]{:S(2)}) async-start(bf16[16,64,128]{2,1,0:T(8,128)(2,1)} %prep.1), calls=%async_computation.1 | async-start | bytes 524288 | tf_op jit(solution)/shard_map/all_to_all | solution.py:53
  18.6 21.6 %copy-start.22 = (s32[2,1]{0,1:T(1,128)S(1)}, s32[2,1]{0,1:T(1,128)}, u32[]{:S(2)}) copy-start(s32[2,1]{0,1:T(1,128)} %param.19) | copy-start | bytes 28
  18.6 24.5 %collective-permute-start = (f32[5,16,128]{2,1,0:T(8,128)S(1)}, f32[5,16,128]{2,1,0:T(8,128)S(1)}, u32[]{:S(2)}, u32[]{:S(2)}) collective-permute-start(f32[5,16,128]{2,1,0:T(8,128)S(1)} %concatenate.32), channel_id=1, source_target_pairs={{16,0},{32,16},{48,32},{64,48},{80,64},{96,80},{112,96},{128,112},... | collective-permute-start | bytes 122888 | tf_op jit(solution)/shard_map/ppermute | solution.py:49
  23.1 17.5 %copy-start.20 = (f32[3,1152]{1,0:T(4,128)S(1)}, f32[3,1152]{1,0:T(4,128)}, u32[]{:S(2)}) copy-start(f32[3,1152]{1,0:T(4,128)} %param.28) | copy-start | bytes 41476
  23.1 17.5 %copy-start.21 = (f32[3,1152]{1,0:T(4,128)S(1)}, f32[3,1152]{1,0:T(4,128)}, u32[]{:S(2)}) copy-start(f32[3,1152]{1,0:T(4,128)} %param.27) | copy-start | bytes 41476
  29.1 1.1 copy-start.5
  30.1 12.1 %copy-start.19 = (f32[16,27,16]{1,2,0:T(8,128)S(1)}, f32[16,27,16]{1,2,0:T(8,128)}, u32[]{:S(2)}) copy-start(f32[16,27,16]{1,2,0:T(8,128)} %param.29) | copy-start | bytes 82948
  30.1 34.3 %all-to-all-start = ((bf16[32,40,384]{2,1,0:T(8,128)(2,1)}), bf16[32,40,384]{2,1,0:T(8,128)(2,1)S(1)}, u32[]{:S(2)}, u32[]{:S(2)}) async-start(bf16[32,40,384]{2,1,0:T(8,128)(2,1)} %broadcast_in_dim.53), calls=%async_computation | async-start | bytes 1966080 | tf_op jit(solution)/shard_map/all_to_all | solution.py:53
  40.2 24.3 %copy-start.2 = (bf16[2,64,1280]{2,1,0:T(8,128)(2,1)S(1)}, bf16[2,64,1280]{2,1,0:T(8,128)(2,1)}, u32[]{:S(2)}) copy-start(bf16[2,64,1280]{2,1,0:T(8,128)(2,1)} %constant.67.clone.pick_ref) | copy-start | bytes 983044
  40.2 24.3 %copy-start.14 = (bf16[80,128]{1,0:T(8,128)(2,1)S(1)}, bf16[80,128]{1,0:T(8,128)(2,1)}, u32[]{:S(2)}) copy-start(bf16[80,128]{1,0:T(8,128)(2,1)} %constant.68.clone.order_ref) | copy-start | bytes 61444
  43.2 0.6 copy-start.9
  82.7 12.2 %collective-permute-start.1 = (bf16[80,1280]{1,0:T(8,128)(2,1)S(1)}, bf16[80,1280]{1,0:T(8,128)(2,1)S(1)}, u32[]{:S(2)}, u32[]{:S(2)}) collective-permute-start(bf16[80,1280]{1,0:T(8,128)(2,1)S(1)} %get-tuple-element.40), channel_id=1, source_target_pairs={{0,8},{8,0},{1,9},{9,1},{2,10},{10,2},{3,11},{11,3},{4,12},{12,4},... | collective-permute-start | bytes 614408 | tf_op jit(solution)/shard_map/ppermute | solution.py:43
  117.1 29.9 %copy-start.7 = (bf16[80,72]{1,0:T(8,128)(2,1)S(1)}, bf16[80,72]{1,0:T(8,128)(2,1)}, u32[]{:S(2)}) copy-start(bf16[80,72]{1,0:T(8,128)(2,1)} %constant.69.clone.widen_ref) | copy-start | bytes 34564
  117.1 30.6 %copy-start.6 = (bf16[16,64,128]{2,1,0:T(8,128)(2,1)S(1)}, bf16[16,64,128]{2,1,0:T(8,128)(2,1)}, u32[]{:S(2)}) copy-start(bf16[16,64,128]{2,1,0:T(8,128)(2,1)} %copy-done.5) | copy-start | bytes 786436
  117.1 40.2 %collective-permute-start.2 = (bf16[4,2,80,1280]{3,2,1,0:T(8,128)(2,1)S(1)}, bf16[4,2,80,1280]{3,2,1,0:T(8,128)(2,1)S(1)}, u32[]{:S(2)}, u32[]{:S(2)}) collective-permute-start(bf16[4,2,80,1280]{3,2,1,0:T(8,128)(2,1)S(1)} %all_to_all.36), channel_id=1, source_target_pairs={{0,1},{1,0},{2,3},{3,2},{4,5},{5,4},{6,7},{7,6},{8,9},{9,8},{10,11... | collective-permute-start | bytes 4915208 | tf_op jit(solution)/shard_map/ppermute | solution.py:43
  123.8 33.5 %copy-start.17 = (f32[64,64]{1,0:T(8,128)}, f32[64,64]{1,0:T(8,128)S(1)}, u32[]{:S(2)}) copy-start(f32[64,64]{1,0:T(8,128)S(1)} %get-tuple-element.34.gram_ref) | copy-start | bytes 49156
  157.3 2.4 copy-start
  157.3 12.0 %copy-start.3 = (f32[16,432]{1,0:T(8,128)S(1)}, f32[16,432]{1,0:T(8,128)}, u32[]{:S(2)}) copy-start(f32[16,432]{1,0:T(8,128)} %reshape.133.mix_ref) | copy-start | bytes 82948
  157.3 12.0 %copy-start.10 = (f32[5,16,128]{2,1,0:T(8,128)S(1)}, f32[5,16,128]{2,1,0:T(8,128)}, u32[]{:S(2)}) copy-start(f32[5,16,128]{2,1,0:T(8,128)} %copy-done.9) | copy-start | bytes 122884
  157.3 12.0 %copy-start.11 = (f32[1,4,16,128]{3,2,1,0:T(8,128)S(1)}, f32[1,4,16,128]{3,2,1,0:T(8,128)}, u32[]{:S(2)}) copy-start(f32[1,4,16,128]{3,2,1,0:T(8,128)} %param.18) | copy-start | bytes 98308
  159.7 8.4 %collective-permute-start.4 = (f32[4,16,128]{2,1,0:T(8,128)S(1)}, f32[4,16,128]{2,1,0:T(8,128)S(1)}, u32[]{:S(2)}, u32[]{:S(2)}) collective-permute-start(f32[4,16,128]{2,1,0:T(8,128)S(1)} %output.2.noise_ref), channel_id=1, source_target_pairs={{32,0},{48,16},{64,32},{80,48},{96,64},{112,80},{128,96},{144,112}... | collective-permute-start | bytes 98312 | tf_op jit(solution)/shard_map/ppermute | solution.py:49
  163.5 5.9 %collective-permute-start.3 = (f32[4,16,128]{2,1,0:T(8,128)S(1)}, f32[4,16,128]{2,1,0:T(8,128)S(1)}, u32[]{:S(2)}, u32[]{:S(2)}) collective-permute-start(f32[4,16,128]{2,1,0:T(8,128)S(1)} %output.2.noise_ref), channel_id=1, source_target_pairs={{16,0},{32,16},{48,32},{64,48},{80,64},{96,80},{112,96},{128,112},... | collective-permute-start | bytes 98312 | tf_op jit(solution)/shard_map/ppermute | solution.py:49
  171.6 0.6 copy-start.12
  199.1 19.1 %all-to-all-start.5 = ((bf16[16,96,128]{2,1,0:T(8,128)(2,1)}), bf16[16,96,128]{2,1,0:T(8,128)(2,1)S(1)}, u32[]{:S(2)}, u32[]{:S(2)}) async-start(bf16[16,96,128]{2,1,0:T(8,128)(2,1)} %get-tuple-element.45), calls=%async_computation.5 | async-start | bytes 786432 | tf_op jit(solution)/shard_map/all_to_all | solution.py:53
  206.8 0.7 copy-start.8
  208.3 0.7 copy-start.15
  218.2 1.0 copy-start.16
  219.2 0.8 copy-start.18
  219.9 9.6 %copy-start.1 = (bf16[4,2,80,1280]{3,2,1,0:T(8,128)(2,1)S(1)}, bf16[4,2,80,1280]{3,2,1,0:T(8,128)(2,1)}, u32[]{:S(2)}) copy-start(bf16[4,2,80,1280]{3,2,1,0:T(8,128)(2,1)} %copy-done) | copy-start | bytes 4915204
  229.6 33.2 %copy-start.4 = (f32[16,432]{1,0:T(8,128)S(1)}, f32[16,432]{1,0:T(8,128)}, u32[]{:S(2)}) copy-start(f32[16,432]{1,0:T(8,128)} %reshape.133.mix_ref) | copy-start | bytes 82948
  229.6 33.2 %copy-start.13 = (f32[4,16,128]{2,1,0:T(8,128)S(1)}, f32[4,16,128]{2,1,0:T(8,128)}, u32[]{:S(2)}) copy-start(f32[4,16,128]{2,1,0:T(8,128)} %copy-done.12) | copy-start | bytes 98308
  231.9 6.5 %collective-permute-start.6 = (f32[4,16,128]{2,1,0:T(8,128)S(1)}, f32[4,16,128]{2,1,0:T(8,128)S(1)}, u32[]{:S(2)}, u32[]{:S(2)}) collective-permute-start(f32[4,16,128]{2,1,0:T(8,128)S(1)} %output.3.noise_ref), channel_id=1, source_target_pairs={{16,0},{32,16},{48,32},{64,48},{80,64},{96,80},{112,96},{128,112},... | collective-permute-start | bytes 98312 | tf_op jit(solution)/shard_map/ppermute | solution.py:49
  235.2 4.7 %collective-permute-start.5 = (f32[4,16,128]{2,1,0:T(8,128)S(1)}, f32[4,16,128]{2,1,0:T(8,128)S(1)}, u32[]{:S(2)}, u32[]{:S(2)}) collective-permute-start(f32[4,16,128]{2,1,0:T(8,128)S(1)} %output.3.noise_ref), channel_id=1, source_target_pairs={{0,16},{16,32},{32,48},{48,64},{64,80},{80,96},{96,112},{112,128},... | collective-permute-start | bytes 98312 | tf_op jit(solution)/shard_map/ppermute | solution.py:49
  239.9 22.8 %collective-permute-start.7 = (f32[3,16,128]{2,1,0:T(8,128)S(1)}, f32[3,16,128]{2,1,0:T(8,128)S(1)}, u32[]{:S(2)}, u32[]{:S(2)}) collective-permute-start(f32[3,16,128]{2,1,0:T(8,128)S(1)} %pad_maximum_fusion.1), channel_id=1, source_target_pairs={{0,1},{1,2},{2,3},{3,4},{4,5},{5,6},{6,7},{7,8},{8,9},{9,10},{10,1... | collective-permute-start | bytes 73736 | tf_op jit(solution)/shard_map/ppermute | solution.py:49
  248.4 14.3 %collective-permute-start.8 = (f32[3,16,128]{2,1,0:T(8,128)S(1)}, f32[3,16,128]{2,1,0:T(8,128)S(1)}, u32[]{:S(2)}, u32[]{:S(2)}) collective-permute-start(f32[3,16,128]{2,1,0:T(8,128)S(1)} %pad_maximum_fusion.2), channel_id=1, source_target_pairs={{1,0},{2,1},{3,2},{4,3},{5,4},{6,5},{7,6},{8,7},{9,8},{10,9},{11,1... | collective-permute-start | bytes 73736 | tf_op jit(solution)/shard_map/ppermute | solution.py:49
  250.4 11.6 %collective-permute-start.10 = (f32[16,128]{1,0:T(8,128)S(1)}, f32[16,128]{1,0:T(8,128)S(1)}, u32[]{:S(2)}, u32[]{:S(2)}) collective-permute-start(f32[16,128]{1,0:T(8,128)S(1)} %get-tuple-element.59), channel_id=1, source_target_pairs={{1,0},{2,1},{3,2},{4,3},{5,4},{6,5},{7,6},{8,7},{9,8},{10,9},{11,1... | collective-permute-start | bytes 24584 | tf_op jit(solution)/shard_map/ppermute | solution.py:49
  252.3 10.4 %collective-permute-start.9 = (f32[16,128]{1,0:T(8,128)S(1)}, f32[16,128]{1,0:T(8,128)S(1)}, u32[]{:S(2)}, u32[]{:S(2)}) collective-permute-start(f32[16,128]{1,0:T(8,128)S(1)} %get-tuple-element.60), channel_id=1, source_target_pairs={{0,1},{1,2},{2,3},{3,4},{4,5},{5,6},{6,7},{7,8},{8,9},{9,10},{10,1... | collective-permute-start | bytes 24584 | tf_op jit(solution)/shard_map/ppermute | solution.py:49

commit v2 on v1

--- a/solution.py
+++ b/solution.py
@@ -106,9 +106,7 @@
 
 def prep_kernel(scalar_ref, lat_ref, out_ref):
     scaled = (lat_ref[...] * scalar_ref[0]).astype(BF16)
-    rows = patch_rows(scaled)
-    for t in range(TILE):
-        out_ref[t] = rows
+    out_ref[...] = patch_rows(scaled)
 
 
 def columns_around(x):
@@ -167,8 +165,7 @@
 
 
 def final_kernel(
-    scalar_ref, before_ref, noise_ref, next_ref, up_ref, down_ref, lat_ref, above_ref, below_ref,
-    mix_ref, out_ref,
+    scalar_ref, before_ref, noise_ref, next_ref, up_ref, down_ref, lat_ref, mix_ref, out_ref
 ):
     frames = [
         [up_ref[td]] + [ref[r] for r in range(4)] + [down_ref[td]]
@@ -178,13 +175,13 @@
     for r in range(4):
         latent = lat_ref[r]
         if r == 0:
-            latent = latent + above_ref[...]
+            latent = latent + up_ref[3]
         if r == 3:
-            latent = latent + below_ref[...]
+            latent = latent + down_ref[3]
         out_ref[r] = latent + scalar_ref[0] * (noise_ref[r] + mixed[r])
 
 
-def spread_kernel(x_ref, pick_ref, emb_ref, mod_ref, order_ref, pay_ref, out_t_ref):
+def spread_kernel(x_ref, pick_ref, emb_ref, mod_ref, order_ref, patch_ref, pay_ref, out_t_ref):
     out_t_ref[...] = nt(order_ref[...], x_ref[:, 256:384]).astype(BF16)
     cols = x_ref[:, 128:256]
     halves = []
@@ -209,42 +206,43 @@
                 block = jnp.where(lane == PF + 6 + 3 * step + j, value - upper, block)
         halves.append(jnp.where(valid, block, 0.0))
     pay = jnp.concatenate(halves, axis=0).astype(BF16)
+    pay = jnp.concatenate([patch_ref[...], pay], axis=0)
     for t in range(TILE):
         pay_ref[t] = pay
 
 
-def fold_kernel(feat_ref, x_ref, first_ref, second_ref, gram_ref):
+def fold_kernel(step, feat_ref, x_ref, out_ref, *gram_refs):
     lane = lane_of((WIDE, LANES))
-    feat = feat_ref[...].astype(F32)
+    feat = jnp.concatenate([feat_ref[t, PF:].astype(F32) for t in range(TILE)], axis=0)
     mods = feat + pltpu.roll(feat, LANES - 6, 1)
     wide = jnp.where(lane < PF, feat, 0.0)
     mean = jnp.sum(wide, axis=0, keepdims=True) * (1.0 / D)
     centred = (wide - mean) * feat[:, 76:77]
-    upper = centred.astype(BF16)
-    lower = (centred - upper.astype(F32)).astype(BF16)
-    gram = tn(upper, upper) + tn(upper, lower) + tn(lower, upper)
-    gram_ref[...] = gram[0:PF, 0:PF]
-    for step, out_ref in enumerate((first_ref, second_ref)):
-        at = PF + 3 * step
-        lines = jnp.where(
-            lane < PF,
-            centred * mods[:, at : at + 1],
-            jnp.where(lane == PF, mods[:, at + 1 : at + 2], 0.0),
-        )
-        upper = lines.astype(BF16)
-        lower = (lines - upper.astype(F32)).astype(BF16)
-        weights = x_ref[:, 0:256]
-        folded = tn(weights, upper) + tn(weights, lower)
-        unit = [folded[HEAD * j : HEAD * j + HEAD] for j in range(3)]
-        spot = lane_of((HEAD, LANES))
-        top = jnp.where(spot < PF, unit[0], pltpu.roll(unit[1], PF, 1))
-        low = jnp.where(spot < PF, unit[2], 0.0)
-        low = jnp.where(spot == PF, unit[0], low)
-        low = jnp.where(spot == PF + 1, pltpu.roll(unit[1], 1, 1), low)
-        low = jnp.where(spot == PF + 2, pltpu.roll(unit[2], 2, 1), low)
-        packed = jnp.concatenate([top, low], axis=0).astype(BF16)
-        for t in range(TILE):
-            out_ref[t] = packed
+    for gram_ref in gram_refs:
+        upper = centred.astype(BF16)
+        lower = (centred - upper.astype(F32)).astype(BF16)
+        gram = tn(upper, upper) + tn(upper, lower) + tn(lower, upper)
+        gram_ref[...] = gram[0:PF, 0:PF]
+    at = PF + 3 * step
+    lines = jnp.where(
+        lane < PF,
+        centred * mods[:, at : at + 1],
+        jnp.where(lane == PF, mods[:, at + 1 : at + 2], 0.0),
+    )
+    upper = lines.astype(BF16)
+    lower = (lines - upper.astype(F32)).astype(BF16)
+    weights = x_ref[:, 0:256]
+    folded = tn(weights, upper) + tn(weights, lower)
+    unit = [folded[HEAD * j : HEAD * j + HEAD] for j in range(3)]
+    spot = lane_of((HEAD, LANES))
+    top = jnp.where(spot < PF, unit[0], pltpu.roll(unit[1], PF, 1))
+    low = jnp.where(spot < PF, unit[2], 0.0)
+    low = jnp.where(spot == PF, unit[0], low)
+    low = jnp.where(spot == PF + 1, pltpu.roll(unit[1], 1, 1), low)
+    low = jnp.where(spot == PF + 2, pltpu.roll(unit[2], 2, 1), low)
+    packed = jnp.concatenate([top, low], axis=0).astype(BF16)
+    for t in range(TILE):
+        out_ref[t] = packed
 
 
 def heads_kernel(folded_ref, widen_ref, n_ref, mvt_ref, units):
@@ -289,7 +287,7 @@
     row = lax.broadcasted_iota(jnp.int32, (PF, TOK), 0)
     ones = jnp.where(row == 0, 1.0, 0.0).astype(F32)
     for j in range(TILE):
-        rounded = with_edges(pt_ref, j) if edges else pt_ref[j]
+        rounded = with_edges(pt_ref, j) if edges else pt_ref[j, 0:PF]
         held[j] = rounded
         patches = rounded.astype(F32)
         spread = jnp.sum(patches * nn(gram_ref[...], patches, HIGHEST), axis=0, keepdims=True)
@@ -331,7 +329,7 @@
             tile = ((me ^ (8 * (b % 2))) & 8) + 2 * (b // 2) + ((me & 1) ^ c)
             rows = pl.ds(pl.multiple_of(tile * 80, 80), 80)
             stream_ref[rows, :] = delta[80 * b : 80 * b + 80]
-    feat = feat_ref[...]
+    feat = jnp.concatenate([feat_ref[t, PF:] for t in range(TILE)], axis=0)
     own = jnp.concatenate([own_ref[...], jnp.zeros((PF, TOK), BF16)], axis=0)
     at = PF + 3 * step + 2
     gate = feat[:, at : at + 1].astype(F32) + feat[:, at + 6 : at + 7].astype(F32)
@@ -368,28 +366,33 @@
 SMEM = pl.BlockSpec(memory_space=pltpu.SMEM)
 
 
-def spread(x, emb, mod):
+def spread(x, emb, mod, patches):
     return pl.pallas_call(
         spread_kernel,
         out_shape=(
-            jax.ShapeDtypeStruct((TILE, 80, LANES), BF16),
+            jax.ShapeDtypeStruct((TILE, PF + 80, LANES), BF16),
             jax.ShapeDtypeStruct((80, WIDE), BF16),
         ),
-        in_specs=[VMEM] * 5,
+        in_specs=[VMEM] * 6,
         out_specs=(VMEM, VMEM),
         compiler_params=pltpu.CompilerParams(vmem_limit_bytes=32 * 1024 * 1024),
         name="spread",
-    )(x, jnp.asarray(PICK, BF16), emb, mod, jnp.asarray(ORDER, BF16))
-
-
-def fold(feat, x):
-    folded = jax.ShapeDtypeStruct((TILE, 2 * HEAD, LANES), BF16)
-    return pl.pallas_call(
-        fold_kernel,
-        out_shape=(folded, folded, jax.ShapeDtypeStruct((PF, PF), F32)),
+    )(x, jnp.asarray(PICK, BF16), emb, mod, jnp.asarray(ORDER, BF16), patches)
+
+
+def fold(step, feat, x):
+    shapes = [jax.ShapeDtypeStruct((TILE, 2 * HEAD, LANES), BF16)]
+    if step == 0:
+        shapes.append(jax.ShapeDtypeStruct((PF, PF), F32))
+    return pl.pallas_call(
+        functools.partial(fold_kernel, step),
+        out_shape=tuple(shapes),
         in_specs=[VMEM] * 2,
-        out_specs=(VMEM,) * 3,
+        out_specs=(VMEM,) * len(shapes),
         compiler_params=pltpu.CompilerParams(vmem_limit_bytes=32 * 1024 * 1024),
+        cost_estimate=pl.CostEstimate(
+            flops=4 * WIDE * 256 * LANES, bytes_accessed=8 * WIDE * LANES, transcendentals=0
+        ),
         name="fold",
     )(feat, x)
 
@@ -448,7 +451,7 @@
 def prep(scale_in, latent):
     return pl.pallas_call(
         prep_kernel,
-        out_shape=jax.ShapeDtypeStruct((TILE, PF, TOK), BF16),
+        out_shape=jax.ShapeDtypeStruct((PF, TOK), BF16),
         in_specs=[SMEM, VMEM],
         out_specs=VMEM,
         name="prep",
@@ -470,15 +473,15 @@
     )(scale_in, last, noise, following, after, lat, new, mix)
 
 
-def finish(drop, before, noise, following, up, down, lat, above, below, mix):
+def finish(drop, before, noise, following, up, down, lat, mix):
     return pl.pallas_call(
         final_kernel,
         out_shape=jax.ShapeDtypeStruct((4, C, LANES), F32),
-        in_specs=[SMEM] + [VMEM] * 9,
+        in_specs=[SMEM] + [VMEM] * 7,
         out_specs=VMEM,
         compiler_params=pltpu.CompilerParams(vmem_limit_bytes=32 * 1024 * 1024),
         name="finish",
-    )(drop, before, noise, following, up, down, lat, above, below, mix)
+    )(drop, before, noise, following, up, down, lat, mix)
 
 
 def pick_matrix():
@@ -547,27 +550,32 @@
     rows = exchanged(jnp.broadcast_to(packed[None], (TM,) + packed.shape), TM_AXES)
     rows = rows.reshape(WIDE, 384)
 
-    patches = exchanged(prep(scale_in[0:1], latent), TILE_AXES)
+    own = prep(scale_in[0:1], latent)
     marked = jnp.concatenate([latent, jnp.full((1, C, LANES), drop[0], F32)], axis=0)
     marked = shifted(marked, TM_AXES, -1)
     steps = jnp.arange(STEPS, dtype=jnp.int32)
     emb = embeddings(level, offset + frame + steps)
     mods = own_mods(mod_gain, mod_bias, tile)
-    rows, patches, marked, mix = lax.optimization_barrier((rows, patches, marked, mix))
-
-    pay, out_t = spread(rows, emb, mods)
-    feat = exchanged(pay, TILE_AXES).reshape(WIDE, LANES)
-    feat, out_t = lax.optimization_barrier((feat, out_t))
-
-    first, second, gram = fold(feat, rows)
-    n, mvt = heads(exchanged(first, TILE_AXES))
-
+    rows, marked, mix = lax.optimization_barrier((rows, marked, mix))
+
+    pay, out_t = spread(rows, emb, mods, own)
+    feat = exchanged(pay, TILE_AXES)
+
+    first, gram = fold(0, feat, rows)
+    first, feat, rows, out_t = lax.optimization_barrier((first, feat, rows, out_t))
+    first = exchanged(first, TILE_AXES)
+
+    (second,) = fold(1, feat, rows)
     both = jnp.stack([out_t, swapped(out_t, "zh")])
+    first, both, second = lax.optimization_barrier((first, both, second))
+    n, mvt = heads(first)
     four = exchanged(jnp.broadcast_to(both[None], (4,) + both.shape), "x")
     other = swapped(four, "core").reshape(8 * 80, WIDE)
     four = four.reshape(8 * 80, WIDE)
-
-    att, own = attend(False, spot, patches, gram, n, mvt)
+    second = exchanged(second, TILE_AXES)
+
+    att, own = attend(False, spot, feat, gram, n, mvt)
+    att, second = lax.optimization_barrier((att, second))
     noise = output(0, spot, att, own, feat, four, other)
 
     following, after = shifted(noise, TM_AXES, -1), shifted(noise, TM_AXES, -2)
@@ -575,18 +583,16 @@
     latent, edges, patches = middle(
         scale_in[1:2], last, noise, following, after, marked, new_frames[0], mix
     )
-    patches, second = lax.optimization_barrier((patches, second))
     patches = exchanged(patches, TILE_AXES)
-    n, mvt = heads(exchanged(second, TILE_AXES))
-    above = shifted(edges[1], TILE_AXES, 1)
-    below = shifted(edges[0], TILE_AXES, -1)
+    n, mvt = heads(second)
 
     att, own = attend(True, spot, patches, gram, n, mvt)
     noise = output(1, spot, att, own, feat, four, other)
     frames = [shifted(noise, TM_AXES, 1), noise, shifted(noise, TM_AXES, -1)]
-    up = shifted(jnp.stack([x[3] for x in frames]), TILE_AXES, 1)
-    down = shifted(jnp.stack([x[0] for x in frames]), TILE_AXES, -1)
-    return finish(drop[1:2], *frames, up, down, latent, above, below, mix)[None]
+    up = jnp.stack([x[3] for x in frames] + [edges[1]])
+    down = jnp.stack([x[0] for x in frames] + [edges[0]])
+    up, down = shifted(up, TILE_AXES, 1), shifted(down, TILE_AXES, -1)
+    return finish(drop[1:2], *frames, up, down, latent, mix)[None]
 
 
 def solution(mesh):

time: 266 us -> 247 us (0.929)
  the two profiles are of different devices: /device:TPU:31 before, /device:TPU:199 now
where the time goes in v2:
time: 247 us; the launch traced here: 245 us
  starting transfers between devices  82.7 us (33%)
  waiting for transfers between devices  53 us (21%)
  blocking collectives  46.8 us (19%)
  Pallas kernels  39.9 us (16%)
  local copies, waits for them, and re-layouts  19.3 us (8%)
    all_to_all x2, blocking collectives, exchanged(): return lax.all_to_all(copies, axis, split_axis=0, concat_axis=0, tiled=True)  46.8 us
    ppermute x7, starting transfers between devices, shifted(): return lax.ppermute(block, axis, route)  34.4 us
    all_to_all x4, waiting for transfers between devices, exchanged(): return lax.all_to_all(copies, axis, split_axis=0, concat_axis=0, tiled=True)  28.8 us
    all_to_all x4, starting transfers between devices, exchanged(): return lax.all_to_all(copies, axis, split_axis=0, concat_axis=0, tiled=True)  28.6 us
    pallas_call x2, Pallas kernels, attend(): pl.pallas_call(functools.partial(attend_kernel, edges), out_shape=(jax.Sh...  20.2 us
    ppermute x2, starting transfers between devices, swapped(): return lax.ppermute(block, axis, [(0, 1), (1, 0)])  19.8 us
    ppermute x7, waiting for transfers between devices, shifted(): return lax.ppermute(block, axis, route)  15.9 us
    unnamed x51, local copies, waits for them, and re-layouts  12.9 us
  transfers between devices with their start and end apart: 13, of which 7 were waited for; matrix products, arithmetic and copies ran while one was open for 3% of the time, Pallas kernels for 6%

profile of v2, /device:TPU:199, one launch (start us, length us, event | category | flops | bytes accessed | tf_op | source)
XLA Modules:
  0.0 244.8 jit_solution(414322794676727031)
XLA Ops:
  0.0 0.7 add_rsqrt_fusion
  0.7 0.6 fusion.9
  1.4 1.4 concatenate.32
  2.8 4.3 %collective-permute-start = (f32[5,16,128]{2,1,0:T(8,128)S(1)}, f32[5,16,128]{2,1,0:T(8,128)S(1)}, u32[]{:S(2)}, u32[]{:S(2)}) collective-permute-start(f32[5,16,128]{2,1,0:T(8,128)S(1)} %concatenate.32), channel_id=1, source_target_pairs={{16,0},{32,16},{48,32},{64,48},{80,64},{96,80},{112,96},{128,112},... | collective-permute-start | bytes 122888 | tf_op jit(solution)/shard_map/ppermute | solution.py:49
  7.1 0.7 pad_maximum_fusion.3
  7.9 0.8 copy.25
  8.8 0.8 concatenate.31
  9.6 1.1 broadcast_in_dim.53
  10.7 8.1 %all-to-all-start = ((bf16[32,40,384]{2,1,0:T(8,128)(2,1)}), bf16[32,40,384]{2,1,0:T(8,128)(2,1)S(1)}, u32[]{:S(2)}, u32[]{:S(2)}) async-start(bf16[32,40,384]{2,1,0:T(8,128)(2,1)} %broadcast_in_dim.53), calls=%async_computation | async-start | bytes 1966080 | tf_op jit(solution)/shard_map/all_to_all | solution.py:53
  19.6 0.1 fusion
  19.9 0.1 copy.27
  20.3 0.3 mul.104
  20.5 0.4 mul.105
  21.0 0.4 mul.108
  21.4 2.2 prep.1.patch_ref
  23.8 0.2 copy.26
  24.0 0.8 reshape.130.mix_ref
  24.8 16.2 %all-to-all-done = bf16[32,40,384]{2,1,0:T(8,128)(2,1)S(1)} async-done(((bf16[32,40,384]{2,1,0:T(8,128)(2,1)}), bf16[32,40,384]{2,1,0:T(8,128)(2,1)S(1)}, u32[]{:S(2)}, u32[]{:S(2)}) %all-to-all-start) | async-done | bytes 983072 | tf_op jit(solution)/shard_map/all_to_all | solution.py:53
  41.0 0.7 copy-done.10
  41.7 0.8 spread.1
  42.5 31.7 %all_to_all.30.feat_ref.pt_ref = bf16[16,144,128]{2,1,0:T(8,128)(2,1)S(1)} all-to-all(bf16[16,144,128]{2,1,0:T(8,128)(2,1)S(1)} %get-tuple-element.33), channel_id=1, replica_groups=mesh['zl'=4,'y'=8,'zh'=2,'x'=4,'core'=2] {'zh','x','core'}, dimensions={0} | all-to-all | bytes 1179648 | tf_op jit(solution)/shard_map/all_to_all | solution.py:53
  74.2 2.4 fold.2
  76.6 0.6 copy-done.17
  77.2 5.5 %all-to-all-start.2 = ((bf16[16,144,128]{2,1,0:T(8,128)(2,1)}), bf16[16,144,128]{2,1,0:T(8,128)(2,1)S(1)}, u32[]{:S(2)}, u32[]{:S(2)}) async-start(bf16[16,144,128]{2,1,0:T(8,128)(2,1)} %get-tuple-element.38), calls=%async_computation.2 | async-start | bytes 1179648 | tf_op jit(solution)/shard_map/all_to_all | solution.py:53
  82.7 7.0 %collective-permute-start.1 = (bf16[80,1280]{1,0:T(8,128)(2,1)S(1)}, bf16[80,1280]{1,0:T(8,128)(2,1)S(1)}, u32[]{:S(2)}, u32[]{:S(2)}) collective-permute-start(bf16[80,1280]{1,0:T(8,128)(2,1)S(1)} %get-tuple-element.39), channel_id=1, source_target_pairs={{0,8},{8,0},{1,9},{9,1},{2,10},{10,2},{3,11},{11,3},{4,12},{12,4},... | collective-permute-start | bytes 614408 | tf_op jit(solution)/shard_map/ppermute | solution.py:43
  89.7 1.2 fold.3
  90.9 0.8 copy-done.2
  91.8 8.3 %collective-permute-done.1 = bf16[80,1280]{1,0:T(8,128)(2,1)S(1)} collective-permute-done((bf16[80,1280]{1,0:T(8,128)(2,1)S(1)}, bf16[80,1280]{1,0:T(8,128)(2,1)S(1)}, u32[]{:S(2)}, u32[]{:S(2)}) %collective-permute-start.1) | collective-permute-done | bytes 204832 | tf_op jit(solution)/shard_map/ppermute | solution.py:43
  100.1 0.8 copy-done
  100.9 0.1 broadcast_in_dim.56
  101.1 15.1 %all_to_all.31 = bf16[4,2,80,1280]{3,2,1,0:T(8,128)(2,1)S(1)} all-to-all(bf16[4,2,80,1280]{3,2,1,0:T(8,128)(2,1)S(1)} %broadcast_in_dim.56), channel_id=1, replica_groups=mesh['zl'=4,'y'=8,'zh'=2,'x'=4,'core'=2] {'x'}, dimensions={0} | all-to-all | bytes 3276800 | tf_op jit(solution)/shard_map/all_to_all | solution.py:53
  116.2 12.7 %collective-permute-start.2 = (bf16[4,2,80,1280]{3,2,1,0:T(8,128)(2,1)S(1)}, bf16[4,2,80,1280]{3,2,1,0:T(8,128)(2,1)}, u32[]{:S(2)}, u32[]{:S(2)}) collective-permute-start(bf16[4,2,80,1280]{3,2,1,0:T(8,128)(2,1)S(1)} %all_to_all.31), channel_id=1, source_target_pairs={{0,1},{1,0},{2,3},{3,2},{4,5},{5,4},{6,7},{7,6},{8,9},{9,8},{10,11... | collective-permute-start | bytes 4915208 | tf_op jit(solution)/shard_map/ppermute | solution.py:43
  129.0 5.1 %all-to-all-start.3 = ((bf16[16,144,128]{2,1,0:T(8,128)(2,1)}), bf16[16,144,128]{2,1,0:T(8,128)(2,1)S(1)}, u32[]{:S(2)}, u32[]{:S(2)}) async-start(bf16[16,144,128]{2,1,0:T(8,128)(2,1)} %copy-done.2), calls=%async_computation.3 | async-start | bytes 1179648 | tf_op jit(solution)/shard_map/all_to_all | solution.py:53
  134.1 1.1 copy-done.1
  135.2 0.8 heads.2
  135.9 0.7 copy-done.18
  136.7 9.6 %attend.2 = (bf16[1280,128]{1,0:T(8,128)(2,1)S(1)}, bf16[64,128]{1,0:T(8,128)(2,1)S(1)}) custom-call(s32[1]{0:T(128)} %bitcast.1.spot_ref, bf16[16,144,128]{2,1,0:T(8,128)(2,1)S(1)} %all_to_all.30.feat_ref.pt_ref, f32[64,64]{1,0:T(8,128)S(1)} %copy-done.18, bf16[16,128,128]{2,1,0:T(8,128)(2,1)S(1)} %get-tuple-element.42.n_ref, ...), custom_call_target="tpu_custom_call" | custom-call | flops 4294967296 | bytes 2097152 | tf_op jit(solution)/shard_map/attend/pallas_call | solution.py:416
  146.3 1.3 all-to-all-done.3.folded_ref
  147.6 3.8 %output.2.noise_ref = f32[4,16,128]{2,1,0:T(8,128)S(1)} custom-call(s32[1]{0:T(128)} %bitcast.1.spot_ref, bf16[1280,128]{1,0:T(8,128)(2,1)S(1)} %get-tuple-element.46.att_ref, bf16[64,128]{1,0:T(8,128)(2,1)S(1)} %get-tuple-element.47.own_ref, bf16[16,144,128]{2,1,0:T(8,128)(2,1)S(1)} %all_to_all.30.feat_ref.pt_ref, bf16[640,1280]{1,0:T(8,128)(2,1)S(1)} %bitcast.27, ...), custom_call_target="tpu_custom_call" | custom-call | tf_op jit(solution)/shard_map/output/pallas_call | solution.py:440
  151.4 12.9 %collective-permute-start.4 = (f32[4,16,128]{2,1,0:T(8,128)S(1)}, f32[4,16,128]{2,1,0:T(8,128)S(1)}, u32[]{:S(2)}, u32[]{:S(2)}) collective-permute-start(f32[4,16,128]{2,1,0:T(8,128)S(1)} %output.2.noise_ref), channel_id=1, source_target_pairs={{32,0},{48,16},{64,32},{80,48},{96,64},{112,80},{128,96},{144,112}... | collective-permute-start | bytes 98312 | tf_op jit(solution)/shard_map/ppermute | solution.py:49
  164.2 2.4 collective-permute-start.3
  166.7 0.6 copy-done.6
  167.3 1.8 collective-permute-done.3.next_ref
  169.1 0.8 copy-done.4
  169.8 0.8 copy-done.7
  170.6 0.8 copy-done.12
  171.4 0.8 copy-done.13
  172.1 2.4 middle.1
  174.5 9.8 %all-to-all-start.5 = ((bf16[16,96,128]{2,1,0:T(8,128)(2,1)}), bf16[16,96,128]{2,1,0:T(8,128)(2,1)}, u32[]{:S(2)}, u32[]{:S(2)}) async-start(bf16[16,96,128]{2,1,0:T(8,128)(2,1)} %get-tuple-element.51), calls=%async_computation.5 | async-start | bytes 786432 | tf_op jit(solution)/shard_map/all_to_all | solution.py:53
  184.3 0.7 copy-done.9
  185.0 0.8 heads.3
  185.8 0.8 copy-done.15
  186.6 11.3 %all-to-all-done.5.pt_ref = bf16[16,96,128]{2,1,0:T(8,128)(2,1)} async-done(((bf16[16,96,128]{2,1,0:T(8,128)(2,1)}), bf16[16,96,128]{2,1,0:T(8,128)(2,1)}, u32[]{:S(2)}, u32[]{:S(2)}) %all-to-all-start.5) | async-done | bytes 393248 | tf_op jit(solution)/shard_map/all_to_all | solution.py:53
  197.9 1.0 copy-done.16
  198.9 0.8 copy-done.19
  199.7 10.6 %attend.3 = (bf16[1280,128]{1,0:T(8,128)(2,1)S(1)}, bf16[64,128]{1,0:T(8,128)(2,1)S(1)}) custom-call(s32[1]{0:T(128)} %bitcast.1.spot_ref, bf16[16,96,128]{2,1,0:T(8,128)(2,1)} %all-to-all-done.5.pt_ref, f32[64,64]{1,0:T(8,128)S(1)} %copy-done.19, bf16[16,128,128]{2,1,0:T(8,128)(2,1)S(1)} %copy-done.16, bf16[16,80,128]{2,1,0:T(8,128)(2,1)S(1)} %get-tuple-element.54.mvt_ref), custom_call_target="tpu_custom_call" | custom-call | flops 4294967296 | bytes 2097152 | tf_op jit(solution)/shard_map/attend/pallas_call | solution.py:416
  210.3 3.8 %output.3.noise_ref = f32[4,16,128]{2,1,0:T(8,128)S(1)} custom-call(s32[1]{0:T(128)} %bitcast.1.spot_ref, bf16[1280,128]{1,0:T(8,128)(2,1)S(1)} %get-tuple-element.55.att_ref, bf16[64,128]{1,0:T(8,128)(2,1)S(1)} %get-tuple-element.56.own_ref, bf16[16,144,128]{2,1,0:T(8,128)(2,1)S(1)} %all_to_all.30.feat_ref.pt_ref, bf16[640,1280]{1,0:T(8,128)(2,1)S(1)} %bitcast.28, ...), custom_call_target="tpu_custom_call" | custom-call | tf_op jit(solution)/shard_map/output/pallas_call | solution.py:440
  214.1 5.8 %collective-permute-start.6 = (f32[4,16,128]{2,1,0:T(8,128)S(1)}, f32[4,16,128]{2,1,0:T(8,128)S(1)}, u32[]{:S(2)}, u32[]{:S(2)}) collective-permute-start(f32[4,16,128]{2,1,0:T(8,128)S(1)} %output.3.noise_ref), channel_id=1, source_target_pairs={{16,0},{32,16},{48,32},{64,48},{80,64},{96,80},{112,96},{128,112},... | collective-permute-start | bytes 98312 | tf_op jit(solution)/shard_map/ppermute | solution.py:49
  219.9 1.9 collective-permute-start.5
  221.8 4.8 %collective-permute-done.5.before_ref = f32[4,16,128]{2,1,0:T(8,128)S(1)} collective-permute-done((f32[4,16,128]{2,1,0:T(8,128)S(1)}, f32[4,16,128]{2,1,0:T(8,128)S(1)}, u32[]{:S(2)}, u32[]{:S(2)}) %collective-permute-start.5) | collective-permute-done | bytes 32800 | tf_op jit(solution)/shard_map/ppermute | solution.py:49
  226.7 5.1 %collective-permute-start.7 = (f32[4,16,128]{2,1,0:T(8,128)S(1)}, f32[4,16,128]{2,1,0:T(8,128)S(1)}, u32[]{:S(2)}, u32[]{:S(2)}) collective-permute-start(f32[4,16,128]{2,1,0:T(8,128)S(1)} %pad_maximum_fusion.1), channel_id=1, source_target_pairs={{0,1},{1,2},{2,3},{3,4},{4,5},{5,6},{6,7},{7,8},{8,9},{9,10},{10,1... | collective-permute-start | bytes 98312 | tf_op jit(solution)/shard_map/ppermute | solution.py:49
  231.8 1.9 collective-permute-start.8
  233.8 9.3 %collective-permute-done.8.down_ref = f32[4,16,128]{2,1,0:T(8,128)S(1)} collective-permute-done((f32[4,16,128]{2,1,0:T(8,128)S(1)}, f32[4,16,128]{2,1,0:T(8,128)S(1)}, u32[]{:S(2)}, u32[]{:S(2)}) %collective-permute-start.8) | collective-permute-done | bytes 32800 | tf_op jit(solution)/shard_map/ppermute | solution.py:49
  243.1 1.7 finish.1
  (68 shorter events, 1.0 us)
Async XLA Ops:
  2.8 16.8 %copy-start.23 = (s32[2,1]{0,1:T(1,128)S(1)}, s32[2,1]{0,1:T(1,128)}, u32[]{:S(2)}) copy-start(s32[2,1]{0,1:T(1,128)} %param.19) | copy-start | bytes 28
  2.8 22.0 %collective-permute-start = (f32[5,16,128]{2,1,0:T(8,128)S(1)}, f32[5,16,128]{2,1,0:T(8,128)S(1)}, u32[]{:S(2)}, u32[]{:S(2)}) collective-permute-start(f32[5,16,128]{2,1,0:T(8,128)S(1)} %concatenate.32), channel_id=1, source_target_pairs={{16,0},{32,16},{48,32},{64,48},{80,64},{96,80},{112,96},{128,112},... | collective-permute-start | bytes 122888 | tf_op jit(solution)/shard_map/ppermute | solution.py:49
  8.7 11.3 %copy-start.21 = (f32[3,1152]{1,0:T(4,128)S(1)}, f32[3,1152]{1,0:T(4,128)}, u32[]{:S(2)}) copy-start(f32[3,1152]{1,0:T(4,128)} %param.28) | copy-start | bytes 41476
  8.7 11.3 %copy-start.22 = (f32[3,1152]{1,0:T(4,128)S(1)}, f32[3,1152]{1,0:T(4,128)}, u32[]{:S(2)}) copy-start(f32[3,1152]{1,0:T(4,128)} %param.27) | copy-start | bytes 41476
  10.7 13.2 %copy-start.20 = (f32[16,27,16]{1,2,0:T(8,128)S(1)}, f32[16,27,16]{1,2,0:T(8,128)}, u32[]{:S(2)}) copy-start(f32[16,27,16]{1,2,0:T(8,128)} %param.29) | copy-start | bytes 82948
  10.7 30.3 %all-to-all-start = ((bf16[32,40,384]{2,1,0:T(8,128)(2,1)}), bf16[32,40,384]{2,1,0:T(8,128)(2,1)S(1)}, u32[]{:S(2)}, u32[]{:S(2)}) async-start(bf16[32,40,384]{2,1,0:T(8,128)(2,1)} %broadcast_in_dim.53), calls=%async_computation | async-start | bytes 1966080 | tf_op jit(solution)/shard_map/all_to_all | solution.py:53
  18.8 22.2 %copy-start.3 = (bf16[2,64,1280]{2,1,0:T(8,128)(2,1)S(1)}, bf16[2,64,1280]{2,1,0:T(8,128)(2,1)}, u32[]{:S(2)}) copy-start(bf16[2,64,1280]{2,1,0:T(8,128)(2,1)} %constant.67.clone.pick_ref) | copy-start | bytes 983044
  18.8 22.2 %copy-start.14 = (bf16[80,128]{1,0:T(8,128)(2,1)S(1)}, bf16[80,128]{1,0:T(8,128)(2,1)}, u32[]{:S(2)}) copy-start(bf16[80,128]{1,0:T(8,128)(2,1)} %constant.68.clone.order_ref) | copy-start | bytes 61444
  24.8 17.7 %copy-start.11 = (f32[5,16,128]{2,1,0:T(8,128)}, f32[5,16,128]{2,1,0:T(8,128)S(1)}, u32[]{:S(2)}) copy-start(f32[5,16,128]{2,1,0:T(8,128)S(1)} %collective-permute-done.lat_ref) | copy-start | bytes 122884
  41.0 0.7 copy-start.10
  76.6 0.6 copy-start.17
  77.2 22.9 %all-to-all-start.2 = ((bf16[16,144,128]{2,1,0:T(8,128)(2,1)}), bf16[16,144,128]{2,1,0:T(8,128)(2,1)S(1)}, u32[]{:S(2)}, u32[]{:S(2)}) async-start(bf16[16,144,128]{2,1,0:T(8,128)(2,1)} %get-tuple-element.38), calls=%async_computation.2 | async-start | bytes 1179648 | tf_op jit(solution)/shard_map/all_to_all | solution.py:53
  82.7 17.4 %collective-permute-start.1 = (bf16[80,1280]{1,0:T(8,128)(2,1)S(1)}, bf16[80,1280]{1,0:T(8,128)(2,1)S(1)}, u32[]{:S(2)}, u32[]{:S(2)}) collective-permute-start(bf16[80,1280]{1,0:T(8,128)(2,1)S(1)} %get-tuple-element.39), channel_id=1, source_target_pairs={{0,8},{8,0},{1,9},{9,1},{2,10},{10,2},{3,11},{11,3},{4,12},{12,4},... | collective-permute-start | bytes 614408 | tf_op jit(solution)/shard_map/ppermute | solution.py:43
  90.9 0.8 copy-start.2
  100.1 0.8 copy-start
  101.1 33.0 %copy-start.8 = (bf16[80,72]{1,0:T(8,128)(2,1)S(1)}, bf16[80,72]{1,0:T(8,128)(2,1)}, u32[]{:S(2)}) copy-start(bf16[80,72]{1,0:T(8,128)(2,1)} %constant.69.clone.widen_ref) | copy-start | bytes 34564
  116.2 31.4 %collective-permute-start.2 = (bf16[4,2,80,1280]{3,2,1,0:T(8,128)(2,1)S(1)}, bf16[4,2,80,1280]{3,2,1,0:T(8,128)(2,1)}, u32[]{:S(2)}, u32[]{:S(2)}) collective-permute-start(bf16[4,2,80,1280]{3,2,1,0:T(8,128)(2,1)S(1)} %all_to_all.31), channel_id=1, source_target_pairs={{0,1},{1,0},{2,3},{3,2},{4,5},{5,4},{6,7},{7,6},{8,9},{9,8},{10,11... | collective-permute-start | bytes 4915208 | tf_op jit(solution)/shard_map/ppermute | solution.py:43
  129.0 18.6 %all-to-all-start.3 = ((bf16[16,144,128]{2,1,0:T(8,128)(2,1)}), bf16[16,144,128]{2,1,0:T(8,128)(2,1)S(1)}, u32[]{:S(2)}, u32[]{:S(2)}) async-start(bf16[16,144,128]{2,1,0:T(8,128)(2,1)} %copy-done.2), calls=%async_computation.3 | async-start | bytes 1179648 | tf_op jit(solution)/shard_map/all_to_all | solution.py:53
  134.1 1.1 copy-start.1
  135.9 0.8 copy-start.18
  151.4 15.9 %collective-permute-start.4 = (f32[4,16,128]{2,1,0:T(8,128)S(1)}, f32[4,16,128]{2,1,0:T(8,128)S(1)}, u32[]{:S(2)}, u32[]{:S(2)}) collective-permute-start(f32[4,16,128]{2,1,0:T(8,128)S(1)} %output.2.noise_ref), channel_id=1, source_target_pairs={{32,0},{48,16},{64,32},{80,48},{96,64},{112,80},{128,96},{144,112}... | collective-permute-start | bytes 98312 | tf_op jit(solution)/shard_map/ppermute | solution.py:49
  164.2 4.8 %collective-permute-start.3 = (f32[4,16,128]{2,1,0:T(8,128)S(1)}, f32[4,16,128]{2,1,0:T(8,128)S(1)}, u32[]{:S(2)}, u32[]{:S(2)}) collective-permute-start(f32[4,16,128]{2,1,0:T(8,128)S(1)} %output.2.noise_ref), channel_id=1, source_target_pairs={{16,0},{32,16},{48,32},{64,48},{80,64},{96,80},{112,96},{128,112},... | collective-permute-start | bytes 98312 | tf_op jit(solution)/shard_map/ppermute | solution.py:49
  166.7 0.6 copy-start.6
  169.1 0.8 copy-start.4
  169.8 0.8 copy-start.7
  170.6 0.8 copy-start.12
  171.4 0.8 copy-start.13
  174.5 23.4 %all-to-all-start.5 = ((bf16[16,96,128]{2,1,0:T(8,128)(2,1)}), bf16[16,96,128]{2,1,0:T(8,128)(2,1)}, u32[]{:S(2)}, u32[]{:S(2)}) async-start(bf16[16,96,128]{2,1,0:T(8,128)(2,1)} %get-tuple-element.51), calls=%async_computation.5 | async-start | bytes 786432 | tf_op jit(solution)/shard_map/all_to_all | solution.py:53
  184.3 0.7 copy-start.9
  185.8 0.8 copy-start.15
  197.9 1.0 copy-start.16
  198.9 0.8 copy-start.19
  210.3 32.8 %copy-start.5 = (f32[16,432]{1,0:T(8,128)S(1)}, f32[16,432]{1,0:T(8,128)}, u32[]{:S(2)}) copy-start(f32[16,432]{1,0:T(8,128)} %reshape.130.mix_ref) | copy-start | bytes 82948
  214.1 7.7 %collective-permute-start.6 = (f32[4,16,128]{2,1,0:T(8,128)S(1)}, f32[4,16,128]{2,1,0:T(8,128)S(1)}, u32[]{:S(2)}, u32[]{:S(2)}) collective-permute-start(f32[4,16,128]{2,1,0:T(8,128)S(1)} %output.3.noise_ref), channel_id=1, source_target_pairs={{16,0},{32,16},{48,32},{64,48},{80,64},{96,80},{112,96},{128,112},... | collective-permute-start | bytes 98312 | tf_op jit(solution)/shard_map/ppermute | solution.py:49
  219.9 6.8 %collective-permute-start.5 = (f32[4,16,128]{2,1,0:T(8,128)S(1)}, f32[4,16,128]{2,1,0:T(8,128)S(1)}, u32[]{:S(2)}, u32[]{:S(2)}) collective-permute-start(f32[4,16,128]{2,1,0:T(8,128)S(1)} %output.3.noise_ref), channel_id=1, source_target_pairs={{0,16},{16,32},{32,48},{48,64},{64,80},{80,96},{96,112},{112,128},... | collective-permute-start | bytes 98312 | tf_op jit(solution)/shard_map/ppermute | solution.py:49
  226.7 7.1 %collective-permute-start.7 = (f32[4,16,128]{2,1,0:T(8,128)S(1)}, f32[4,16,128]{2,1,0:T(8,128)S(1)}, u32[]{:S(2)}, u32[]{:S(2)}) collective-permute-start(f32[4,16,128]{2,1,0:T(8,128)S(1)} %pad_maximum_fusion.1), channel_id=1, source_target_pairs={{0,1},{1,2},{2,3},{3,4},{4,5},{5,6},{6,7},{7,8},{8,9},{9,10},{10,1... | collective-permute-start | bytes 98312 | tf_op jit(solution)/shard_map/ppermute | solution.py:49
  231.8 11.3 %collective-permute-start.8 = (f32[4,16,128]{2,1,0:T(8,128)S(1)}, f32[4,16,128]{2,1,0:T(8,128)S(1)}, u32[]{:S(2)}, u32[]{:S(2)}) collective-permute-start(f32[4,16,128]{2,1,0:T(8,128)S(1)} %pad_maximum_fusion.2), channel_id=1, source_target_pairs={{1,0},{2,1},{3,2},{4,3},{5,4},{6,5},{7,6},{8,7},{9,8},{10,9},{11,1... | collective-permute-start | bytes 98312 | tf_op jit(solution)/shard_map/ppermute | solution.py:49

commit v3 on v2

--- a/solution.py
+++ b/solution.py
@@ -222,7 +222,10 @@
         upper = centred.astype(BF16)
         lower = (centred - upper.astype(F32)).astype(BF16)
         gram = tn(upper, upper) + tn(upper, lower) + tn(lower, upper)
-        gram_ref[...] = gram[0:PF, 0:PF]
+        gram = gram[0:PF, 0:PF]
+        upper = gram.astype(BF16)
+        gram_ref[0:PF] = upper
+        gram_ref[PF : 2 * PF] = (gram - upper.astype(F32)).astype(BF16)
     at = PF + 3 * step
     lines = jnp.where(
         lane < PF,
@@ -286,13 +289,19 @@
     me = spot_ref[0]
     row = lax.broadcasted_iota(jnp.int32, (PF, TOK), 0)
     ones = jnp.where(row == 0, 1.0, 0.0).astype(F32)
+    blocks = []
     for j in range(TILE):
         rounded = with_edges(pt_ref, j) if edges else pt_ref[j, 0:PF]
         held[j] = rounded
-        patches = rounded.astype(F32)
-        spread = jnp.sum(patches * nn(gram_ref[...], patches, HIGHEST), axis=0, keepdims=True)
-        unit = patches * lax.rsqrt(jnp.maximum(spread, 0.0) * (1.0 / D) + NORM_EPS)
-        wide = jnp.concatenate([unit, ones], axis=0)
+        blocks.append(rounded)
+    patches = jnp.concatenate(blocks, axis=1)
+    product = nn(gram_ref[...], patches)
+    patches = patches.astype(F32)
+    product = patches * (product[0:PF] + product[PF : 2 * PF])
+    spread = jnp.maximum(jnp.sum(product, axis=0, keepdims=True), 0.0)
+    unit = patches * lax.rsqrt(spread * (1.0 / D) + NORM_EPS)
+    for j in range(TILE):
+        wide = jnp.concatenate([unit[:, j * TOK : (j + 1) * TOK], ones], axis=0)
         keys_t[:, j * TOK : (j + 1) * TOK] = wide.astype(BF16)
         keys[j * TOK : (j + 1) * TOK, :] = wide.T.astype(BF16)
     own_ref[...] = held[me]
@@ -312,23 +321,21 @@
             value = nt(mvt_ref[head], mean[k * TOK : (k + 1) * TOK])
             att_ref[pl.ds(pl.multiple_of(head * 80, 80), 80), :] = value.astype(BF16)
 
-    @pl.loop(0, HEADS // 4)
+    @pl.loop(0, HEADS // 8)
     def _(i):
-        two_heads(2 * i)
-        two_heads(2 * i + 1)
+        for k in range(4):
+            two_heads(4 * i + k)
 
 
 def output_kernel(
-    step, spot_ref, att_ref, own_ref, feat_ref, wot_ref, wot2_ref, out_ref, stream_ref
+    step, spot_ref, att_ref, own_ref, feat_ref, wot_ref, out_ref, stream_ref
 ):
     me = spot_ref[0]
-    attended = att_ref[...]
-    for c, ref in enumerate((wot_ref, wot2_ref)):
-        delta = nn(ref[...], attended)
-        for b in range(8):
-            tile = ((me ^ (8 * (b % 2))) & 8) + 2 * (b // 2) + ((me & 1) ^ c)
-            rows = pl.ds(pl.multiple_of(tile * 80, 80), 80)
-            stream_ref[rows, :] = delta[80 * b : 80 * b + 80]
+    delta = nn(wot_ref[...], att_ref[...])
+    for b in range(TILE):
+        tile = ((me ^ (8 * (b % 2))) & 8) + b // 2
+        rows = pl.ds(pl.multiple_of(tile * 80, 80), 80)
+        stream_ref[rows, :] = delta[80 * b : 80 * b + 80]
     feat = jnp.concatenate([feat_ref[t, PF:] for t in range(TILE)], axis=0)
     own = jnp.concatenate([own_ref[...], jnp.zeros((PF, TOK), BF16)], axis=0)
     at = PF + 3 * step + 2
@@ -339,14 +346,12 @@
     center = (stream - mean) * valid
     spread = jnp.sum(center * center, axis=0, keepdims=True) * (1.0 / D)
     final = (center * lax.rsqrt(spread + NORM_EPS)).astype(BF16)
-    out_rows = [
-        ref[80 * b + 32 : 80 * b + 48, :] for ref in (wot_ref, wot2_ref) for b in range(8)
-    ]
+    out_rows = [wot_ref[80 * b + 32 : 80 * b + 48, :] for b in range(TILE)]
     noise = nn(jnp.concatenate(out_rows, axis=0), final)
     feature = lax.broadcasted_iota(jnp.int32, (PF, 256), 0)
     source = lane_of((PF, 256))
     block = source >> 4
-    tile = ((me ^ ((block & 1) << 3)) & 8) + (block & 6) + ((me & 1) ^ (block >> 3))
+    tile = ((me ^ ((block & 1) << 3)) & 8) + (block >> 1)
     q = (source & 15) - 4
     wanted = ((q & 1) << 5) + ((q >> 1) << 4) + tile
     order = jnp.where((q >= 0) & (q < 4) & (feature == wanted), 1.0, 0.0).astype(F32)
@@ -364,6 +369,7 @@
 
 VMEM = pl.BlockSpec(memory_space=pltpu.VMEM)
 SMEM = pl.BlockSpec(memory_space=pltpu.SMEM)
+BLOCK = pl.BlockSpec()
 
 
 def spread(x, emb, mod, patches):
@@ -383,7 +389,7 @@
 def fold(step, feat, x):
     shapes = [jax.ShapeDtypeStruct((TILE, 2 * HEAD, LANES), BF16)]
     if step == 0:
-        shapes.append(jax.ShapeDtypeStruct((PF, PF), F32))
+        shapes.append(jax.ShapeDtypeStruct((2 * PF, PF), BF16))
     return pl.pallas_call(
         functools.partial(fold_kernel, step),
         out_shape=tuple(shapes),
@@ -419,7 +425,7 @@
             jax.ShapeDtypeStruct((WIDE, TOK), BF16),
             jax.ShapeDtypeStruct((PF, TOK), BF16),
         ),
-        in_specs=[SMEM] + [VMEM] * 4,
+        in_specs=[SMEM] + [BLOCK] * 4,
         out_specs=(VMEM, VMEM),
         scratch_shapes=[
             pltpu.VMEM((LANES, SPAN), BF16),
@@ -436,16 +442,16 @@
     )(spot, pt, gram, n, mvt)
 
 
-def output(step, spot, att, own, feat, wot, wot2):
+def output(step, spot, att, own, feat, wot):
     return pl.pallas_call(
         functools.partial(output_kernel, step),
         out_shape=jax.ShapeDtypeStruct((4, C, LANES), F32),
-        in_specs=[SMEM] + [VMEM] * 5,
+        in_specs=[SMEM] + [VMEM] * 4,
         out_specs=VMEM,
         scratch_shapes=[pltpu.VMEM((WIDE, TOK), F32)],
         compiler_params=pltpu.CompilerParams(vmem_limit_bytes=32 * 1024 * 1024),
         name="output",
-    )(spot, att, own, feat, wot, wot2)
+    )(spot, att, own, feat, wot)
 
 
 def prep(scale_in, latent):
@@ -466,7 +472,7 @@
             jax.ShapeDtypeStruct((2, C, LANES), F32),
             jax.ShapeDtypeStruct((TILE, PF + 2 * C, TOK), BF16),
         ),
-        in_specs=[SMEM, SMEM] + [VMEM] * 6,
+        in_specs=[SMEM, SMEM] + [BLOCK] * 6,
         out_specs=(VMEM,) * 3,
         compiler_params=pltpu.CompilerParams(vmem_limit_bytes=32 * 1024 * 1024),
         name="middle",
@@ -477,7 +483,7 @@
     return pl.pallas_call(
         final_kernel,
         out_shape=jax.ShapeDtypeStruct((4, C, LANES), F32),
-        in_specs=[SMEM] + [VMEM] * 7,
+        in_specs=[SMEM] + [BLOCK] * 7,
         out_specs=VMEM,
         compiler_params=pltpu.CompilerParams(vmem_limit_bytes=32 * 1024 * 1024),
         name="finish",
@@ -562,21 +568,20 @@
     feat = exchanged(pay, TILE_AXES)
 
     first, gram = fold(0, feat, rows)
-    first, feat, rows, out_t = lax.optimization_barrier((first, feat, rows, out_t))
+    first, feat, rows = lax.optimization_barrier((first, feat, rows))
     first = exchanged(first, TILE_AXES)
 
     (second,) = fold(1, feat, rows)
+    first, second = lax.optimization_barrier((first, second))
+    n, mvt = heads(first)
+    second = exchanged(second, TILE_AXES)
+
     both = jnp.stack([out_t, swapped(out_t, "zh")])
-    first, both, second = lax.optimization_barrier((first, both, second))
-    n, mvt = heads(first)
-    four = exchanged(jnp.broadcast_to(both[None], (4,) + both.shape), "x")
-    other = swapped(four, "core").reshape(8 * 80, WIDE)
-    four = four.reshape(8 * 80, WIDE)
-    second = exchanged(second, TILE_AXES)
+    full_o = lax.all_gather(both, ("x", "core")).reshape(WIDE, WIDE)
 
     att, own = attend(False, spot, feat, gram, n, mvt)
     att, second = lax.optimization_barrier((att, second))
-    noise = output(0, spot, att, own, feat, four, other)
+    noise = output(0, spot, att, own, feat, full_o)
 
     following, after = shifted(noise, TM_AXES, -1), shifted(noise, TM_AXES, -2)
     last = (frame == TM - 1).astype(jnp.int32)[None]
@@ -587,7 +592,7 @@
     n, mvt = heads(second)
 
     att, own = attend(True, spot, patches, gram, n, mvt)
-    noise = output(1, spot, att, own, feat, four, other)
+    noise = output(1, spot, att, own, feat, full_o)
     frames = [shifted(noise, TM_AXES, 1), noise, shifted(noise, TM_AXES, -1)]
     up = jnp.stack([x[3] for x in frames] + [edges[1]])
     down = jnp.stack([x[0] for x in frames] + [edges[0]])

time: 247 us -> 231 us (0.935)
  the two profiles are of different devices: /device:TPU:199 before, /device:TPU:63 now
where the time goes in v3:
time: 231 us; the launch traced here: 230 us
  waiting for transfers between devices  75.5 us (33%)
  starting transfers between devices  59.7 us (26%)
  Pallas kernels  37.2 us (16%)
  blocking collectives  30.8 us (13%)
  between operations  14.4 us (6%)
  local copies, waits for them, and re-layouts  9.5 us (4%)
  other arithmetic  2.65 us (1%)
    all_to_all x4, waiting for transfers between devices, exchanged(): return lax.all_to_all(copies, axis, split_axis=0, concat_axis=0, tiled=True)  41.2 us
    ppermute x7, waiting for transfers between devices, shifted(): return lax.ppermute(block, axis, route)  31 us
    all_to_all x1, blocking collectives, exchanged(): return lax.all_to_all(copies, axis, split_axis=0, concat_axis=0, tiled=True)  30.8 us
    all_to_all x4, starting transfers between devices, exchanged(): return lax.all_to_all(copies, axis, split_axis=0, concat_axis=0, tiled=True)  27.9 us
    ppermute x7, starting transfers between devices, shifted(): return lax.ppermute(block, axis, route)  23.9 us
    pallas_call x2, Pallas kernels, attend(): pl.pallas_call(functools.partial(attend_kernel, edges), out_shape=(jax.Sh...  18 us
    ppermute x1, starting transfers between devices, swapped(): return lax.ppermute(block, axis, [(0, 1), (1, 0)])  7.94 us
    pallas_call x2, Pallas kernels, output(): pl.pallas_call(functools.partial(output_kernel, step), out_shape=jax.Shap...  6.24 us
  transfers between devices with their start and end apart: 13, of which 10 were waited for; matrix products, arithmetic and copies ran while one was open for 2% of the time, Pallas kernels for 7%

profile of v3, /device:TPU:63, one launch (start us, length us, event | category | flops | bytes accessed | tf_op | source)
XLA Modules:
  0.0 229.7 jit_solution(4190517923077957074)
XLA Ops:
  6.6 0.8 pad_maximum_fusion.3
  7.3 0.1 reshape.124
  7.4 0.8 copy.25
  8.2 0.8 concatenate.31
  9.1 1.0 broadcast_in_dim.47
  10.1 11.9 %all-to-all-start = ((bf16[32,40,384]{2,1,0:T(8,128)(2,1)}), bf16[32,40,384]{2,1,0:T(8,128)(2,1)S(1)}, u32[]{:S(2)}, u32[]{:S(2)}) async-start(bf16[32,40,384]{2,1,0:T(8,128)(2,1)} %broadcast_in_dim.47), calls=%async_computation | async-start | bytes 1966080 | tf_op jit(solution)/shard_map/all_to_all | solution.py:53
  22.0 0.0 all-gather.3.cloned.1.call-start
  22.1 0.7 add_rsqrt_fusion
  22.8 0.7 fusion.9
  23.5 1.4 concatenate.32
  24.9 3.1 %collective-permute-start = (f32[5,16,128]{2,1,0:T(8,128)S(1)}, f32[5,16,128]{2,1,0:T(8,128)S(1)}, u32[]{:S(2)}, u32[]{:S(2)}) collective-permute-start(f32[5,16,128]{2,1,0:T(8,128)S(1)} %concatenate.32), channel_id=1, source_target_pairs={{16,0},{32,16},{48,32},{64,48},{80,64},{96,80},{112,96},{128,112},... | collective-permute-start | bytes 122888 | tf_op jit(solution)/shard_map/ppermute | solution.py:49
  28.0 0.1 mul.107
  28.0 0.4 mul.108
  29.1 0.1 pad.33.clone
  29.2 0.1 fusion
  29.3 0.1 maximum_maximum_fusion.1
  29.4 0.1 copy.27
  29.5 0.3 mul.104
  29.8 0.4 mul.105
  30.2 0.1 pad.28.clone
  30.3 0.1 maximum_maximum_fusion
  30.4 0.1 reshape.127
  30.5 0.2 copy.26
  30.7 0.1 reshape.126.mix_ref
  30.9 0.1 reshape.128
  31.0 0.1 copy.31
  31.1 2.2 prep.1.patch_ref
  33.2 10.6 %collective-permute-done.lat_ref = f32[5,16,128]{2,1,0:T(8,128)S(1)} collective-permute-done((f32[5,16,128]{2,1,0:T(8,128)S(1)}, f32[5,16,128]{2,1,0:T(8,128)S(1)}, u32[]{:S(2)}, u32[]{:S(2)}) %collective-permute-start) | collective-permute-done | bytes 40992 | tf_op jit(solution)/shard_map/ppermute | solution.py:49
  43.8 1.8 all-to-all-done
  45.6 0.7 copy-done.4
  46.3 0.8 spread.1
  47.1 7.9 %collective-permute-start.1 = (bf16[80,1280]{1,0:T(8,128)(2,1)S(1)}, bf16[80,1280]{1,0:T(8,128)(2,1)S(1)}, u32[]{:S(2)}, u32[]{:S(2)}) collective-permute-start(bf16[80,1280]{1,0:T(8,128)(2,1)S(1)} %get-tuple-element.44), channel_id=1, source_target_pairs={{0,8},{8,0},{1,9},{9,1},{2,10},{10,2},{3,11},{11,3},{4,12},{12,4},... | collective-permute-start | bytes 614408 | tf_op jit(solution)/shard_map/ppermute | solution.py:43
  55.0 3.2 %collective-permute-done.1 = bf16[80,1280]{1,0:T(8,128)(2,1)S(1)} collective-permute-done((bf16[80,1280]{1,0:T(8,128)(2,1)S(1)}, bf16[80,1280]{1,0:T(8,128)(2,1)S(1)}, u32[]{:S(2)}, u32[]{:S(2)}) %collective-permute-start.1) | collective-permute-done | bytes 204832 | tf_op jit(solution)/shard_map/ppermute | solution.py:43
  58.3 0.8 pad_maximum_fusion
  59.1 0.0 all-gather.3.cloned.1.call-update
  59.1 30.8 %all_to_all.25.feat_ref.pt_ref = bf16[16,144,128]{2,1,0:T(8,128)(2,1)S(1)} all-to-all(bf16[16,144,128]{2,1,0:T(8,128)(2,1)S(1)} %get-tuple-element.31), channel_id=1, replica_groups=mesh['zl'=4,'y'=8,'zh'=2,'x'=4,'core'=2] {'zh','x','core'}, dimensions={0} | all-to-all | bytes 1179648 | tf_op jit(solution)/shard_map/all_to_all | solution.py:53
  89.8 2.4 %fold.2 = (bf16[16,144,128]{2,1,0:T(8,128)(2,1)}, bf16[128,64]{1,0:T(8,128)(2,1)S(1)}) custom-call(bf16[16,144,128]{2,1,0:T(8,128)(2,1)S(1)} %all_to_all.25.feat_ref.pt_ref, bf16[1280,384]{1,0:T(8,128)(2,1)S(1)} %bitcast.24), custom_call_target="tpu_custom_call" | custom-call | flops 167772160 | bytes 1310720 | tf_op jit(solution)/shard_map/fold/pallas_call | solution.py:393
  92.2 5.5 %all-to-all-start.2 = ((bf16[16,144,128]{2,1,0:T(8,128)(2,1)}), bf16[16,144,128]{2,1,0:T(8,128)(2,1)S(1)}, u32[]{:S(2)}, u32[]{:S(2)}) async-start(bf16[16,144,128]{2,1,0:T(8,128)(2,1)} %get-tuple-element.35), calls=%async_computation.2 | async-start | bytes 1179648 | tf_op jit(solution)/shard_map/all_to_all | solution.py:53
  97.8 2.0 fold.3
  99.8 16.9 %all-to-all-done.2.folded_ref = bf16[16,144,128]{2,1,0:T(8,128)(2,1)S(1)} async-done(((bf16[16,144,128]{2,1,0:T(8,128)(2,1)}), bf16[16,144,128]{2,1,0:T(8,128)(2,1)S(1)}, u32[]{:S(2)}, u32[]{:S(2)}) %all-to-all-start.2) | async-done | bytes 589856 | tf_op jit(solution)/shard_map/all_to_all | solution.py:53
  116.7 4.3 %all-to-all-start.3 = ((bf16[16,144,128]{2,1,0:T(8,128)(2,1)}), bf16[16,144,128]{2,1,0:T(8,128)(2,1)S(1)}, u32[]{:S(2)}, u32[]{:S(2)}) async-start(bf16[16,144,128]{2,1,0:T(8,128)(2,1)} %fold.3), calls=%async_computation.3 | async-start | bytes 1179648 | tf_op jit(solution)/shard_map/all_to_all | solution.py:53
  121.0 0.8 heads.2
  121.8 0.0 copy-start.5
  121.8 9.0 %attend.2 = (bf16[1280,128]{1,0:T(8,128)(2,1)S(1)}, bf16[64,128]{1,0:T(8,128)(2,1)S(1)}) custom-call(s32[1]{0:T(128)} %bitcast.1.spot_ref, bf16[16,144,128]{2,1,0:T(8,128)(2,1)S(1)} %all_to_all.25.feat_ref.pt_ref, bf16[128,64]{1,0:T(8,128)(2,1)S(1)} %get-tuple-element.34.gram_ref, bf16[16,128,128]{2,1,0:T(8,128)(2,1)S(1)} %get-tuple-element.38.n_ref, ...), custom_call_target="tpu_custom_call" | custom-call | flops 4294967296 | bytes 2097152 | tf_op jit(solution)/shard_map/attend/pallas_call | solution.py:422
  130.8 9.1 %all-to-all-done.3.folded_ref = bf16[16,144,128]{2,1,0:T(8,128)(2,1)S(1)} async-done(((bf16[16,144,128]{2,1,0:T(8,128)(2,1)}), bf16[16,144,128]{2,1,0:T(8,128)(2,1)S(1)}, u32[]{:S(2)}, u32[]{:S(2)}) %all-to-all-start.3) | async-done | bytes 589856 | tf_op jit(solution)/shard_map/all_to_all | solution.py:53
  139.9 1.9 copy-done
  141.8 3.1 %output.2.noise_ref = f32[4,16,128]{2,1,0:T(8,128)S(1)} custom-call(s32[1]{0:T(128)} %bitcast.1.spot_ref, bf16[1280,128]{1,0:T(8,128)(2,1)S(1)} %get-tuple-element.42.att_ref, bf16[64,128]{1,0:T(8,128)(2,1)S(1)} %get-tuple-element.43.own_ref, bf16[16,144,128]{2,1,0:T(8,128)(2,1)S(1)} %all_to_all.25.feat_ref.pt_ref, bf16[1280,1280]{1,0:T(8,128)(2,1)S(1)} %bitcast.26), custom_call_target="tpu_custom_call" | custom-call | tf_op jit(solution)/shard_map/output/pallas_call | solution.py:446
  144.9 2.6 %collective-permute-start.2 = (f32[4,16,128]{2,1,0:T(8,128)S(1)}, f32[4,16,128]{2,1,0:T(8,128)S(1)}, u32[]{:S(2)}, u32[]{:S(2)}) collective-permute-start(f32[4,16,128]{2,1,0:T(8,128)S(1)} %output.2.noise_ref), channel_id=1, source_target_pairs={{16,0},{32,16},{48,32},{64,48},{80,64},{96,80},{112,96},{128,112},... | collective-permute-start | bytes 98312 | tf_op jit(solution)/shard_map/ppermute | solution.py:49
  147.6 3.5 %collective-permute-start.3 = (f32[4,16,128]{2,1,0:T(8,128)S(1)}, f32[4,16,128]{2,1,0:T(8,128)S(1)}, u32[]{:S(2)}, u32[]{:S(2)}) collective-permute-start(f32[4,16,128]{2,1,0:T(8,128)S(1)} %output.2.noise_ref), channel_id=1, source_target_pairs={{32,0},{48,16},{64,32},{80,48},{96,64},{112,80},{128,96},{144,112}... | collective-permute-start | bytes 98312 | tf_op jit(solution)/shard_map/ppermute | solution.py:49
  151.1 0.6 collective-permute-done.2.next_ref
  151.7 5.7 %collective-permute-done.3.after_ref = f32[4,16,128]{2,1,0:T(8,128)S(1)} collective-permute-done((f32[4,16,128]{2,1,0:T(8,128)S(1)}, f32[4,16,128]{2,1,0:T(8,128)S(1)}, u32[]{:S(2)}, u32[]{:S(2)}) %collective-permute-start.3) | collective-permute-done | bytes 32800 | tf_op jit(solution)/shard_map/ppermute | solution.py:49
  157.5 2.4 %middle.1 = (f32[4,16,128]{2,1,0:T(8,128)S(1)}, f32[2,16,128]{2,1,0:T(8,128)S(1)}, bf16[16,96,128]{2,1,0:T(8,128)(2,1)}) custom-call(f32[1]{0:T(128)} %bitcast.2.scalar_ref, s32[1]{0:T(128)} %bitcast.3.flag_ref, f32[4,16,128]{2,1,0:T(8,128)S(1)} %output.2.noise_ref, f32[4,16,128]{2,1,0:T(8,128)S(1)} %collective-permute-done.2.next_ref, ...), custom_call_target="tpu_custom_call" | custom-call | tf_op jit(solution)/shard_map/middle/pallas_call | solution.py:468
  159.8 6.2 %all-to-all-start.4 = ((bf16[16,96,128]{2,1,0:T(8,128)(2,1)}), bf16[16,96,128]{2,1,0:T(8,128)(2,1)S(1)}, u32[]{:S(2)}, u32[]{:S(2)}) async-start(bf16[16,96,128]{2,1,0:T(8,128)(2,1)} %get-tuple-element.47), calls=%async_computation.4 | async-start | bytes 786432 | tf_op jit(solution)/shard_map/all_to_all | solution.py:53
  166.0 0.8 heads.3
  166.7 13.3 %all-to-all-done.4.pt_ref = bf16[16,96,128]{2,1,0:T(8,128)(2,1)S(1)} async-done(((bf16[16,96,128]{2,1,0:T(8,128)(2,1)}), bf16[16,96,128]{2,1,0:T(8,128)(2,1)S(1)}, u32[]{:S(2)}, u32[]{:S(2)}) %all-to-all-start.4) | async-done | bytes 393248 | tf_op jit(solution)/shard_map/all_to_all | solution.py:53
  180.1 9.0 %attend.3 = (bf16[1280,128]{1,0:T(8,128)(2,1)S(1)}, bf16[64,128]{1,0:T(8,128)(2,1)S(1)}) custom-call(s32[1]{0:T(128)} %bitcast.1.spot_ref, bf16[16,96,128]{2,1,0:T(8,128)(2,1)S(1)} %all-to-all-done.4.pt_ref, bf16[128,64]{1,0:T(8,128)(2,1)S(1)} %get-tuple-element.34.gram_ref, bf16[16,128,128]{2,1,0:T(8,128)(2,1)S(1)} %get-tuple-element.49.n_ref, ...), custom_call_target="tpu_custom_call" | custom-call | flops 4294967296 | bytes 2097152 | tf_op jit(solution)/shard_map/attend/pallas_call | solution.py:422
  189.1 3.1 %output.3.noise_ref = f32[4,16,128]{2,1,0:T(8,128)S(1)} custom-call(s32[1]{0:T(128)} %bitcast.1.spot_ref, bf16[1280,128]{1,0:T(8,128)(2,1)S(1)} %get-tuple-element.51.att_ref, bf16[64,128]{1,0:T(8,128)(2,1)S(1)} %get-tuple-element.52.own_ref, bf16[16,144,128]{2,1,0:T(8,128)(2,1)S(1)} %all_to_all.25.feat_ref.pt_ref, bf16[1280,1280]{1,0:T(8,128)(2,1)S(1)} %bitcast.27), custom_call_target="tpu_custom_call" | custom-call | tf_op jit(solution)/shard_map/output/pallas_call | solution.py:446
  192.3 5.5 %collective-permute-start.4 = (f32[4,16,128]{2,1,0:T(8,128)S(1)}, f32[4,16,128]{2,1,0:T(8,128)S(1)}, u32[]{:S(2)}, u32[]{:S(2)}) collective-permute-start(f32[4,16,128]{2,1,0:T(8,128)S(1)} %output.3.noise_ref), channel_id=1, source_target_pairs={{0,16},{16,32},{32,48},{48,64},{64,80},{80,96},{96,112},{112,128},... | collective-permute-start | bytes 98312 | tf_op jit(solution)/shard_map/ppermute | solution.py:49
  197.8 1.9 collective-permute-start.5
  199.7 4.8 %collective-permute-done.5.next_ref = f32[4,16,128]{2,1,0:T(8,128)S(1)} collective-permute-done((f32[4,16,128]{2,1,0:T(8,128)S(1)}, f32[4,16,128]{2,1,0:T(8,128)S(1)}, u32[]{:S(2)}, u32[]{:S(2)}) %collective-permute-start.5) | collective-permute-done | bytes 32800 | tf_op jit(solution)/shard_map/ppermute | solution.py:49
  204.6 5.2 %collective-permute-start.6 = (f32[4,16,128]{2,1,0:T(8,128)S(1)}, f32[4,16,128]{2,1,0:T(8,128)S(1)}, u32[]{:S(2)}, u32[]{:S(2)}) collective-permute-start(f32[4,16,128]{2,1,0:T(8,128)S(1)} %pad_maximum_fusion.1), channel_id=1, source_target_pairs={{0,1},{1,2},{2,3},{3,4},{4,5},{5,6},{6,7},{7,8},{8,9},{9,10},{10,1... | collective-permute-start | bytes 98312 | tf_op jit(solution)/shard_map/ppermute | solution.py:49
  209.9 1.9 collective-permute-start.7
  211.8 9.3 %collective-permute-done.7.down_ref = f32[4,16,128]{2,1,0:T(8,128)S(1)} collective-permute-done((f32[4,16,128]{2,1,0:T(8,128)S(1)}, f32[4,16,128]{2,1,0:T(8,128)S(1)}, u32[]{:S(2)}, u32[]{:S(2)}) %collective-permute-start.7) | collective-permute-done | bytes 32800 | tf_op jit(solution)/shard_map/ppermute | solution.py:49
  221.1 1.7 finish.1
  (41 shorter events, 0.2 us)
Async XLA Ops:
  6.5 39.0 %copy-start.2 = (bf16[2,64,1280]{2,1,0:T(8,128)(2,1)S(1)}, bf16[2,64,1280]{2,1,0:T(8,128)(2,1)}, u32[]{:S(2)}) copy-start(bf16[2,64,1280]{2,1,0:T(8,128)(2,1)} %constant.67.clone.pick_ref) | copy-start | bytes 983044
  6.5 39.0 %copy-start.6 = (bf16[80,128]{1,0:T(8,128)(2,1)S(1)}, bf16[80,128]{1,0:T(8,128)(2,1)}, u32[]{:S(2)}) copy-start(bf16[80,128]{1,0:T(8,128)(2,1)} %constant.68.clone.order_ref) | copy-start | bytes 61444
  6.5 22.6 %copy-start.10 = (s32[2,1]{0,1:T(1,128)S(1)}, s32[2,1]{0,1:T(1,128)}, u32[]{:S(2)}) copy-start(s32[2,1]{0,1:T(1,128)} %param.19) | copy-start | bytes 28
  6.5 23.8 %copy-start.8 = (f32[3,1152]{1,0:T(4,128)S(1)}, f32[3,1152]{1,0:T(4,128)}, u32[]{:S(2)}) copy-start(f32[3,1152]{1,0:T(4,128)} %param.28) | copy-start | bytes 41476
  6.5 23.8 %copy-start.9 = (f32[3,1152]{1,0:T(4,128)S(1)}, f32[3,1152]{1,0:T(4,128)}, u32[]{:S(2)}) copy-start(f32[3,1152]{1,0:T(4,128)} %param.27) | copy-start | bytes 41476
  6.5 24.0 %copy-start.7 = (f32[16,27,16]{1,2,0:T(8,128)S(1)}, f32[16,27,16]{1,2,0:T(8,128)}, u32[]{:S(2)}) copy-start(f32[16,27,16]{1,2,0:T(8,128)} %param.29) | copy-start | bytes 82948
  10.1 35.4 %all-to-all-start = ((bf16[32,40,384]{2,1,0:T(8,128)(2,1)}), bf16[32,40,384]{2,1,0:T(8,128)(2,1)S(1)}, u32[]{:S(2)}, u32[]{:S(2)}) async-start(bf16[32,40,384]{2,1,0:T(8,128)(2,1)} %broadcast_in_dim.47), calls=%async_computation | async-start | bytes 1966080 | tf_op jit(solution)/shard_map/all_to_all | solution.py:53
  22.0 117.9 %all-gather.3.cloned.1.call-start = ((), (), s32[]{:S(2)}) async-start(), calls=%async_computation.5 | async-start | bytes 3686400 | tf_op jit(solution)/shard_map/all_gather | solution.py:580
  24.9 18.9 %collective-permute-start = (f32[5,16,128]{2,1,0:T(8,128)S(1)}, f32[5,16,128]{2,1,0:T(8,128)S(1)}, u32[]{:S(2)}, u32[]{:S(2)}) collective-permute-start(f32[5,16,128]{2,1,0:T(8,128)S(1)} %concatenate.32), channel_id=1, source_target_pairs={{16,0},{32,16},{48,32},{64,48},{80,64},{96,80},{112,96},{128,112},... | collective-permute-start | bytes 122888 | tf_op jit(solution)/shard_map/ppermute | solution.py:49
  45.6 0.7 copy-start.4
  47.1 11.2 %collective-permute-start.1 = (bf16[80,1280]{1,0:T(8,128)(2,1)S(1)}, bf16[80,1280]{1,0:T(8,128)(2,1)S(1)}, u32[]{:S(2)}, u32[]{:S(2)}) collective-permute-start(bf16[80,1280]{1,0:T(8,128)(2,1)S(1)} %get-tuple-element.44), channel_id=1, source_target_pairs={{0,8},{8,0},{1,9},{9,1},{2,10},{10,2},{3,11},{11,3},{4,12},{12,4},... | collective-permute-start | bytes 614408 | tf_op jit(solution)/shard_map/ppermute | solution.py:43
  89.8 31.1 %copy-start.3 = (bf16[80,72]{1,0:T(8,128)(2,1)S(1)}, bf16[80,72]{1,0:T(8,128)(2,1)}, u32[]{:S(2)}) copy-start(bf16[80,72]{1,0:T(8,128)(2,1)} %constant.69.clone.widen_ref) | copy-start | bytes 34564
  92.2 24.5 %all-to-all-start.2 = ((bf16[16,144,128]{2,1,0:T(8,128)(2,1)}), bf16[16,144,128]{2,1,0:T(8,128)(2,1)S(1)}, u32[]{:S(2)}, u32[]{:S(2)}) async-start(bf16[16,144,128]{2,1,0:T(8,128)(2,1)} %get-tuple-element.35), calls=%async_computation.2 | async-start | bytes 1179648 | tf_op jit(solution)/shard_map/all_to_all | solution.py:53
  116.7 23.2 %all-to-all-start.3 = ((bf16[16,144,128]{2,1,0:T(8,128)(2,1)}), bf16[16,144,128]{2,1,0:T(8,128)(2,1)S(1)}, u32[]{:S(2)}, u32[]{:S(2)}) async-start(bf16[16,144,128]{2,1,0:T(8,128)(2,1)} %fold.3), calls=%async_computation.3 | async-start | bytes 1179648 | tf_op jit(solution)/shard_map/all_to_all | solution.py:53
  121.8 35.7 %copy-start.5 = (f32[1,4,16,128]{3,2,1,0:T(8,128)S(1)}, f32[1,4,16,128]{3,2,1,0:T(8,128)}, u32[]{:S(2)}) copy-start(f32[1,4,16,128]{3,2,1,0:T(8,128)} %param.18) | copy-start | bytes 98308
  139.9 1.9 copy-start
  144.9 6.8 %collective-permute-start.2 = (f32[4,16,128]{2,1,0:T(8,128)S(1)}, f32[4,16,128]{2,1,0:T(8,128)S(1)}, u32[]{:S(2)}, u32[]{:S(2)}) collective-permute-start(f32[4,16,128]{2,1,0:T(8,128)S(1)} %output.2.noise_ref), channel_id=1, source_target_pairs={{16,0},{32,16},{48,32},{64,48},{80,64},{96,80},{112,96},{128,112},... | collective-permute-start | bytes 98312 | tf_op jit(solution)/shard_map/ppermute | solution.py:49
  147.6 9.9 %collective-permute-start.3 = (f32[4,16,128]{2,1,0:T(8,128)S(1)}, f32[4,16,128]{2,1,0:T(8,128)S(1)}, u32[]{:S(2)}, u32[]{:S(2)}) collective-permute-start(f32[4,16,128]{2,1,0:T(8,128)S(1)} %output.2.noise_ref), channel_id=1, source_target_pairs={{32,0},{48,16},{64,32},{80,48},{96,64},{112,80},{128,96},{144,112}... | collective-permute-start | bytes 98312 | tf_op jit(solution)/shard_map/ppermute | solution.py:49
  159.8 20.3 %all-to-all-start.4 = ((bf16[16,96,128]{2,1,0:T(8,128)(2,1)}), bf16[16,96,128]{2,1,0:T(8,128)(2,1)S(1)}, u32[]{:S(2)}, u32[]{:S(2)}) async-start(bf16[16,96,128]{2,1,0:T(8,128)(2,1)} %get-tuple-element.47), calls=%async_computation.4 | async-start | bytes 786432 | tf_op jit(solution)/shard_map/all_to_all | solution.py:53
  180.1 9.0 %copy-start.1 = (bf16[16,80,1280]{2,1,0:T(8,128)(2,1)S(1)}, bf16[16,80,1280]{2,1,0:T(8,128)(2,1)}, u32[]{:S(2)}) copy-start(bf16[16,80,1280]{2,1,0:T(8,128)(2,1)} %all-gather.3.cloned.1.call-done) | copy-start | bytes 9830404
  192.3 12.3 %collective-permute-start.4 = (f32[4,16,128]{2,1,0:T(8,128)S(1)}, f32[4,16,128]{2,1,0:T(8,128)S(1)}, u32[]{:S(2)}, u32[]{:S(2)}) collective-permute-start(f32[4,16,128]{2,1,0:T(8,128)S(1)} %output.3.noise_ref), channel_id=1, source_target_pairs={{0,16},{16,32},{32,48},{48,64},{64,80},{80,96},{96,112},{112,128},... | collective-permute-start | bytes 98312 | tf_op jit(solution)/shard_map/ppermute | solution.py:49
  197.8 6.8 %collective-permute-start.5 = (f32[4,16,128]{2,1,0:T(8,128)S(1)}, f32[4,16,128]{2,1,0:T(8,128)S(1)}, u32[]{:S(2)}, u32[]{:S(2)}) collective-permute-start(f32[4,16,128]{2,1,0:T(8,128)S(1)} %output.3.noise_ref), channel_id=1, source_target_pairs={{16,0},{32,16},{48,32},{64,48},{80,64},{96,80},{112,96},{128,112},... | collective-permute-start | bytes 98312 | tf_op jit(solution)/shard_map/ppermute | solution.py:49
  204.6 7.2 %collective-permute-start.6 = (f32[4,16,128]{2,1,0:T(8,128)S(1)}, f32[4,16,128]{2,1,0:T(8,128)S(1)}, u32[]{:S(2)}, u32[]{:S(2)}) collective-permute-start(f32[4,16,128]{2,1,0:T(8,128)S(1)} %pad_maximum_fusion.1), channel_id=1, source_target_pairs={{0,1},{1,2},{2,3},{3,4},{4,5},{5,6},{6,7},{7,8},{8,9},{9,10},{10,1... | collective-permute-start | bytes 98312 | tf_op jit(solution)/shard_map/ppermute | solution.py:49
  209.9 11.3 %collective-permute-start.7 = (f32[4,16,128]{2,1,0:T(8,128)S(1)}, f32[4,16,128]{2,1,0:T(8,128)S(1)}, u32[]{:S(2)}, u32[]{:S(2)}) collective-permute-start(f32[4,16,128]{2,1,0:T(8,128)S(1)} %pad_maximum_fusion.2), channel_id=1, source_target_pairs={{1,0},{2,1},{3,2},{4,3},{5,4},{6,5},{7,6},{8,7},{9,8},{10,9},{11,1... | collective-permute-start | bytes 98312 | tf_op jit(solution)/shard_map/ppermute | solution.py:49
Sparse Core Ops, SparseCore 0:
  59.2 45.7 all-gather.2

commit v4 on v3

--- a/solution.py
+++ b/solution.py
@@ -37,10 +37,6 @@
 F32 = jnp.float32
 BF16 = jnp.bfloat16
 HIGHEST = lax.Precision.HIGHEST
-
-
-def swapped(block, axis):
-    return lax.ppermute(block, axis, [(0, 1), (1, 0)])
 
 
 def shifted(block, axis, distance):
@@ -328,20 +324,15 @@
 
 
 def output_kernel(
-    step, spot_ref, att_ref, own_ref, feat_ref, wot_ref, out_ref, stream_ref
+    step, att_ref, own_ref, feat_ref, wot_ref, out_ref
 ):
-    me = spot_ref[0]
     delta = nn(wot_ref[...], att_ref[...])
-    for b in range(TILE):
-        tile = ((me ^ (8 * (b % 2))) & 8) + b // 2
-        rows = pl.ds(pl.multiple_of(tile * 80, 80), 80)
-        stream_ref[rows, :] = delta[80 * b : 80 * b + 80]
     feat = jnp.concatenate([feat_ref[t, PF:] for t in range(TILE)], axis=0)
     own = jnp.concatenate([own_ref[...], jnp.zeros((PF, TOK), BF16)], axis=0)
     at = PF + 3 * step + 2
     gate = feat[:, at : at + 1].astype(F32) + feat[:, at + 6 : at + 7].astype(F32)
     valid = feat[:, 76:77].astype(F32)
-    stream = (nn(feat, own) + gate * stream_ref[...]) * valid
+    stream = (nn(feat, own) + gate * delta) * valid
     mean = jnp.sum(stream, axis=0, keepdims=True) * (1.0 / D)
     center = (stream - mean) * valid
     spread = jnp.sum(center * center, axis=0, keepdims=True) * (1.0 / D)
@@ -351,9 +342,8 @@
     feature = lax.broadcasted_iota(jnp.int32, (PF, 256), 0)
     source = lane_of((PF, 256))
     block = source >> 4
-    tile = ((me ^ ((block & 1) << 3)) & 8) + (block >> 1)
     q = (source & 15) - 4
-    wanted = ((q & 1) << 5) + ((q >> 1) << 4) + tile
+    wanted = ((q & 1) << 5) + ((q >> 1) << 4) + block
     order = jnp.where((q >= 0) & (q < 4) & (feature == wanted), 1.0, 0.0).astype(F32)
     noise = nn(order, noise, HIGHEST)
     for hp in range(2):
@@ -442,16 +432,15 @@
     )(spot, pt, gram, n, mvt)
 
 
-def output(step, spot, att, own, feat, wot):
+def output(step, att, own, feat, wot):
     return pl.pallas_call(
         functools.partial(output_kernel, step),
         out_shape=jax.ShapeDtypeStruct((4, C, LANES), F32),
-        in_specs=[SMEM] + [VMEM] * 4,
+        in_specs=[VMEM] * 4,
         out_specs=VMEM,
-        scratch_shapes=[pltpu.VMEM((WIDE, TOK), F32)],
         compiler_params=pltpu.CompilerParams(vmem_limit_bytes=32 * 1024 * 1024),
         name="output",
-    )(spot, att, own, feat, wot)
+    )(att, own, feat, wot)
 
 
 def prep(scale_in, latent):
@@ -576,14 +565,13 @@
     n, mvt = heads(first)
     second = exchanged(second, TILE_AXES)
 
-    both = jnp.stack([out_t, swapped(out_t, "zh")])
-    full_o = lax.all_gather(both, ("x", "core")).reshape(WIDE, WIDE)
+    full_o = lax.all_gather(out_t, TILE_AXES, tiled=True)
 
     att, own = attend(False, spot, feat, gram, n, mvt)
-    att, second = lax.optimization_barrier((att, second))
-    noise = output(0, spot, att, own, feat, full_o)
+    noise = output(0, att, own, feat, full_o)
 
     following, after = shifted(noise, TM_AXES, -1), shifted(noise, TM_AXES, -2)
+    following, second = lax.optimization_barrier((following, second))
     last = (frame == TM - 1).astype(jnp.int32)[None]
     latent, edges, patches = middle(
         scale_in[1:2], last, noise, following, after, marked, new_frames[0], mix
@@ -592,7 +580,7 @@
     n, mvt = heads(second)
 
     att, own = attend(True, spot, patches, gram, n, mvt)
-    noise = output(1, spot, att, own, feat, full_o)
+    noise = output(1, att, own, feat, full_o)
     frames = [shifted(noise, TM_AXES, 1), noise, shifted(noise, TM_AXES, -1)]
     up = jnp.stack([x[3] for x in frames] + [edges[1]])
     down = jnp.stack([x[0] for x in frames] + [edges[0]])

time: 231 us -> 232 us (level)
  the two profiles are of different devices: /device:TPU:63 before, /device:TPU:376 now
where the time goes in v4:
time: 232 us; the launch traced here: 231 us
  waiting for transfers between devices  77 us (33%)
  starting transfers between devices  61 us (26%)
  Pallas kernels  37.1 us (16%)
  blocking collectives  30.5 us (13%)
  between operations  14.4 us (6%)
  local copies, waits for them, and re-layouts  9.51 us (4%)
    all_to_all x4, waiting for transfers between devices, exchanged(): return lax.all_to_all(copies, axis, split_axis=0, concat_axis=0, tiled=True)  45.7 us
    all_to_all x4, starting transfers between devices, exchanged(): return lax.all_to_all(copies, axis, split_axis=0, concat_axis=0, tiled=True)  36.7 us
    ppermute x7, waiting for transfers between devices, shifted(): return lax.ppermute(block, axis, route)  31.3 us
    all_to_all x1, blocking collectives, exchanged(): return lax.all_to_all(copies, axis, split_axis=0, concat_axis=0, tiled=True)  30.5 us
    ppermute x7, starting transfers between devices, shifted(): return lax.ppermute(block, axis, route)  24.2 us
    pallas_call x2, Pallas kernels, attend(): pl.pallas_call(functools.partial(attend_kernel, edges), out_shape=(jax.Sh...  18 us
    pallas_call x2, Pallas kernels, output(): pl.pallas_call(functools.partial(output_kernel, step), out_shape=jax.Shap...  5.91 us
  transfers between devices with their start and end apart: 12, of which 7 were waited for; matrix products, arithmetic and copies ran while one was open for 3% of the time, Pallas kernels for 9%

profile of v4, /device:TPU:376, one launch (start us, length us, event | category | flops | bytes accessed | tf_op | source)
XLA Modules:
  0.0 231.4 jit_solution(12134680009996858425)
XLA Ops:
  6.6 0.8 add_rsqrt_fusion
  7.4 0.7 fusion.9
  8.0 1.4 concatenate.32
  9.4 3.2 %collective-permute-start = (f32[5,16,128]{2,1,0:T(8,128)S(1)}, f32[5,16,128]{2,1,0:T(8,128)S(1)}, u32[]{:S(2)}, u32[]{:S(2)}) collective-permute-start(f32[5,16,128]{2,1,0:T(8,128)S(1)} %concatenate.32), channel_id=1, source_target_pairs={{16,0},{32,16},{48,32},{64,48},{80,64},{96,80},{112,96},{128,112},... | collective-permute-start | bytes 122888 | tf_op jit(solution)/shard_map/ppermute | solution.py:45
  12.7 0.7 pad_maximum_fusion.2
  13.4 0.1 reshape.121
  13.5 0.8 copy.25
  14.3 0.8 concatenate.31
  15.1 1.0 broadcast_in_dim.47
  16.2 9.0 %all-to-all-start = ((bf16[32,40,384]{2,1,0:T(8,128)(2,1)}), bf16[32,40,384]{2,1,0:T(8,128)(2,1)S(1)}, u32[]{:S(2)}, u32[]{:S(2)}) async-start(bf16[32,40,384]{2,1,0:T(8,128)(2,1)} %broadcast_in_dim.47), calls=%async_computation | async-start | bytes 1966080 | tf_op jit(solution)/shard_map/all_to_all | solution.py:49
  25.2 0.0 all-gather.2.cloned.1.call-start
  25.9 0.1 pad.31.clone
  26.0 0.1 fusion
  26.1 0.1 maximum_maximum_fusion.1
  26.2 0.1 copy.27
  26.3 0.3 mul.104
  26.6 0.4 mul.105
  27.0 0.1 mul.107
  27.1 0.4 mul.108
  27.5 0.1 pad.26.clone
  27.5 0.1 maximum_maximum_fusion
  27.6 0.1 reshape.124
  27.8 0.1 reshape.125
  27.9 0.1 copy.31
  28.0 0.0 copy-done.7
  28.0 0.2 copy.26
  28.2 0.1 reshape.123.mix_ref
  28.3 2.1 prep.1.patch_ref
  30.5 0.0 collective-permute-done.lat_ref
  30.5 18.9 %all-to-all-done = bf16[32,40,384]{2,1,0:T(8,128)(2,1)S(1)} async-done(((bf16[32,40,384]{2,1,0:T(8,128)(2,1)}), bf16[32,40,384]{2,1,0:T(8,128)(2,1)S(1)}, u32[]{:S(2)}, u32[]{:S(2)}) %all-to-all-start) | async-done | bytes 983072 | tf_op jit(solution)/shard_map/all_to_all | solution.py:49
  49.3 0.7 copy-done.4
  50.0 1.0 spread.1
  51.0 0.0 all-gather.2.cloned.1.call-update
  51.0 30.5 %all_to_all.25.feat_ref.pt_ref = bf16[16,144,128]{2,1,0:T(8,128)(2,1)S(1)} all-to-all(bf16[16,144,128]{2,1,0:T(8,128)(2,1)S(1)} %get-tuple-element.31), channel_id=1, replica_groups=mesh['zl'=4,'y'=8,'zh'=2,'x'=4,'core'=2] {'zh','x','core'}, dimensions={0} | all-to-all | bytes 1179648 | tf_op jit(solution)/shard_map/all_to_all | solution.py:49
  81.5 2.4 %fold.2 = (bf16[16,144,128]{2,1,0:T(8,128)(2,1)}, bf16[128,64]{1,0:T(8,128)(2,1)S(1)}) custom-call(bf16[16,144,128]{2,1,0:T(8,128)(2,1)S(1)} %all_to_all.25.feat_ref.pt_ref, bf16[1280,384]{1,0:T(8,128)(2,1)S(1)} %bitcast.21), custom_call_target="tpu_custom_call" | custom-call | flops 167772160 | bytes 1310720 | tf_op jit(solution)/shard_map/fold/pallas_call | solution.py:383
  83.9 8.8 %all-to-all-start.2 = ((bf16[16,144,128]{2,1,0:T(8,128)(2,1)}), bf16[16,144,128]{2,1,0:T(8,128)(2,1)S(1)}, u32[]{:S(2)}, u32[]{:S(2)}) async-start(bf16[16,144,128]{2,1,0:T(8,128)(2,1)} %get-tuple-element.35), calls=%async_computation.2 | async-start | bytes 1179648 | tf_op jit(solution)/shard_map/all_to_all | solution.py:49
  92.7 2.0 fold.3
  94.7 19.5 %all-to-all-done.2.folded_ref = bf16[16,144,128]{2,1,0:T(8,128)(2,1)S(1)} async-done(((bf16[16,144,128]{2,1,0:T(8,128)(2,1)}), bf16[16,144,128]{2,1,0:T(8,128)(2,1)S(1)}, u32[]{:S(2)}, u32[]{:S(2)}) %all-to-all-start.2) | async-done | bytes 589856 | tf_op jit(solution)/shard_map/all_to_all | solution.py:49
  114.3 9.3 %all-to-all-start.3 = ((bf16[16,144,128]{2,1,0:T(8,128)(2,1)}), bf16[16,144,128]{2,1,0:T(8,128)(2,1)S(1)}, u32[]{:S(2)}, u32[]{:S(2)}) async-start(bf16[16,144,128]{2,1,0:T(8,128)(2,1)} %fold.3), calls=%async_computation.3 | async-start | bytes 1179648 | tf_op jit(solution)/shard_map/all_to_all | solution.py:49
  123.6 0.8 heads.2
  124.3 0.0 copy-start.5
  124.3 9.0 %attend.2 = (bf16[1280,128]{1,0:T(8,128)(2,1)S(1)}, bf16[64,128]{1,0:T(8,128)(2,1)S(1)}) custom-call(s32[1]{0:T(128)} %bitcast.1.spot_ref, bf16[16,144,128]{2,1,0:T(8,128)(2,1)S(1)} %all_to_all.25.feat_ref.pt_ref, bf16[128,64]{1,0:T(8,128)(2,1)S(1)} %get-tuple-element.34.gram_ref, bf16[16,128,128]{2,1,0:T(8,128)(2,1)S(1)} %get-tuple-element.38.n_ref, ...), custom_call_target="tpu_custom_call" | custom-call | flops 4294967296 | bytes 2097152 | tf_op jit(solution)/shard_map/attend/pallas_call | solution.py:412
  133.3 0.0 all-gather.2.cloned.1.call-done.wot_ref
  133.4 1.9 copy-done
  135.3 2.9 %output.2.noise_ref = f32[4,16,128]{2,1,0:T(8,128)S(1)} custom-call(bf16[1280,128]{1,0:T(8,128)(2,1)S(1)} %get-tuple-element.40.att_ref, bf16[64,128]{1,0:T(8,128)(2,1)S(1)} %get-tuple-element.41.own_ref, bf16[16,144,128]{2,1,0:T(8,128)(2,1)S(1)} %all_to_all.25.feat_ref.pt_ref, bf16[1280,1280]{1,0:T(8,128)(2,1)S(1)} %copy-done), custom_call_target="tpu_custom_call" | custom-call | tf_op jit(solution)/shard_map/output/pallas_call | solution.py:436
  138.2 3.8 %collective-permute-start.1 = (f32[4,16,128]{2,1,0:T(8,128)S(1)}, f32[4,16,128]{2,1,0:T(8,128)S(1)}, u32[]{:S(2)}, u32[]{:S(2)}) collective-permute-start(f32[4,16,128]{2,1,0:T(8,128)S(1)} %output.2.noise_ref), channel_id=1, source_target_pairs={{16,0},{32,16},{48,32},{64,48},{80,64},{96,80},{112,96},{128,112},... | collective-permute-start | bytes 98312 | tf_op jit(solution)/shard_map/ppermute | solution.py:45
  142.0 1.9 collective-permute-start.2
  144.0 0.0 all-to-all-done.3.folded_ref
  144.0 3.6 %collective-permute-done.1.next_ref = f32[4,16,128]{2,1,0:T(8,128)S(1)} collective-permute-done((f32[4,16,128]{2,1,0:T(8,128)S(1)}, f32[4,16,128]{2,1,0:T(8,128)S(1)}, u32[]{:S(2)}, u32[]{:S(2)}) %collective-permute-start.1) | collective-permute-done | bytes 32800 | tf_op jit(solution)/shard_map/ppermute | solution.py:45
  147.6 12.4 %collective-permute-done.2.after_ref = f32[4,16,128]{2,1,0:T(8,128)S(1)} collective-permute-done((f32[4,16,128]{2,1,0:T(8,128)S(1)}, f32[4,16,128]{2,1,0:T(8,128)S(1)}, u32[]{:S(2)}, u32[]{:S(2)}) %collective-permute-start.2) | collective-permute-done | bytes 32800 | tf_op jit(solution)/shard_map/ppermute | solution.py:45
  160.0 2.4 %middle.1 = (f32[4,16,128]{2,1,0:T(8,128)S(1)}, f32[2,16,128]{2,1,0:T(8,128)S(1)}, bf16[16,96,128]{2,1,0:T(8,128)(2,1)}) custom-call(f32[1]{0:T(128)} %bitcast.2.scalar_ref, s32[1]{0:T(128)} %bitcast.3.flag_ref, f32[4,16,128]{2,1,0:T(8,128)S(1)} %output.2.noise_ref, f32[4,16,128]{2,1,0:T(8,128)S(1)} %collective-permute-done.1.next_ref, ...), custom_call_target="tpu_custom_call" | custom-call | tf_op jit(solution)/shard_map/middle/pallas_call | solution.py:457
  162.4 9.7 %all-to-all-start.4 = ((bf16[16,96,128]{2,1,0:T(8,128)(2,1)}), bf16[16,96,128]{2,1,0:T(8,128)(2,1)S(1)}, u32[]{:S(2)}, u32[]{:S(2)}) async-start(bf16[16,96,128]{2,1,0:T(8,128)(2,1)} %get-tuple-element.47), calls=%async_computation.4 | async-start | bytes 786432 | tf_op jit(solution)/shard_map/all_to_all | solution.py:49
  172.0 0.8 heads.3
  172.8 7.3 %all-to-all-done.4.pt_ref = bf16[16,96,128]{2,1,0:T(8,128)(2,1)S(1)} async-done(((bf16[16,96,128]{2,1,0:T(8,128)(2,1)}), bf16[16,96,128]{2,1,0:T(8,128)(2,1)S(1)}, u32[]{:S(2)}, u32[]{:S(2)}) %all-to-all-start.4) | async-done | bytes 393248 | tf_op jit(solution)/shard_map/all_to_all | solution.py:49
  180.1 9.0 %attend.3 = (bf16[1280,128]{1,0:T(8,128)(2,1)S(1)}, bf16[64,128]{1,0:T(8,128)(2,1)S(1)}) custom-call(s32[1]{0:T(128)} %bitcast.1.spot_ref, bf16[16,96,128]{2,1,0:T(8,128)(2,1)S(1)} %all-to-all-done.4.pt_ref, bf16[128,64]{1,0:T(8,128)(2,1)S(1)} %get-tuple-element.34.gram_ref, bf16[16,128,128]{2,1,0:T(8,128)(2,1)S(1)} %get-tuple-element.49.n_ref, ...), custom_call_target="tpu_custom_call" | custom-call | flops 4294967296 | bytes 2097152 | tf_op jit(solution)/shard_map/attend/pallas_call | solution.py:412
  189.2 3.0 %output.3.noise_ref = f32[4,16,128]{2,1,0:T(8,128)S(1)} custom-call(bf16[1280,128]{1,0:T(8,128)(2,1)S(1)} %get-tuple-element.51.att_ref, bf16[64,128]{1,0:T(8,128)(2,1)S(1)} %get-tuple-element.52.own_ref, bf16[16,144,128]{2,1,0:T(8,128)(2,1)S(1)} %all_to_all.25.feat_ref.pt_ref, bf16[1280,1280]{1,0:T(8,128)(2,1)S(1)} %copy-done.1), custom_call_target="tpu_custom_call" | custom-call | tf_op jit(solution)/shard_map/output/pallas_call | solution.py:436
  192.1 5.1 %collective-permute-start.3 = (f32[4,16,128]{2,1,0:T(8,128)S(1)}, f32[4,16,128]{2,1,0:T(8,128)S(1)}, u32[]{:S(2)}, u32[]{:S(2)}) collective-permute-start(f32[4,16,128]{2,1,0:T(8,128)S(1)} %output.3.noise_ref), channel_id=1, source_target_pairs={{0,16},{16,32},{32,48},{48,64},{64,80},{80,96},{96,112},{112,128},... | collective-permute-start | bytes 98312 | tf_op jit(solution)/shard_map/ppermute | solution.py:45
  197.2 1.9 collective-permute-start.4
  199.2 0.0 collective-permute-done.3.before_ref
  199.2 6.0 %collective-permute-done.4.next_ref = f32[4,16,128]{2,1,0:T(8,128)S(1)} collective-permute-done((f32[4,16,128]{2,1,0:T(8,128)S(1)}, f32[4,16,128]{2,1,0:T(8,128)S(1)}, u32[]{:S(2)}, u32[]{:S(2)}) %collective-permute-start.4) | collective-permute-done | bytes 32800 | tf_op jit(solution)/shard_map/ppermute | solution.py:45
  205.1 6.4 %collective-permute-start.6 = (f32[4,16,128]{2,1,0:T(8,128)S(1)}, f32[4,16,128]{2,1,0:T(8,128)S(1)}, u32[]{:S(2)}, u32[]{:S(2)}) collective-permute-start(f32[4,16,128]{2,1,0:T(8,128)S(1)} %pad_maximum_fusion.1), channel_id=1, source_target_pairs={{1,0},{2,1},{3,2},{4,3},{5,4},{6,5},{7,6},{8,7},{9,8},{10,9},{11,1... | collective-permute-start | bytes 98312 | tf_op jit(solution)/shard_map/ppermute | solution.py:45
  211.5 1.9 collective-permute-start.5
  213.5 9.3 %collective-permute-done.5.up_ref = f32[4,16,128]{2,1,0:T(8,128)S(1)} collective-permute-done((f32[4,16,128]{2,1,0:T(8,128)S(1)}, f32[4,16,128]{2,1,0:T(8,128)S(1)}, u32[]{:S(2)}, u32[]{:S(2)}) %collective-permute-start.5) | collective-permute-done | bytes 32800 | tf_op jit(solution)/shard_map/ppermute | solution.py:45
  222.8 1.7 finish.1
  (38 shorter events, 0.2 us)
Async XLA Ops:
  6.5 42.8 %copy-start.2 = (bf16[2,64,1280]{2,1,0:T(8,128)(2,1)S(1)}, bf16[2,64,1280]{2,1,0:T(8,128)(2,1)}, u32[]{:S(2)}) copy-start(bf16[2,64,1280]{2,1,0:T(8,128)(2,1)} %constant.67.clone.pick_ref) | copy-start | bytes 983044
  6.5 42.8 %copy-start.6 = (bf16[80,128]{1,0:T(8,128)(2,1)S(1)}, bf16[80,128]{1,0:T(8,128)(2,1)}, u32[]{:S(2)}) copy-start(bf16[80,128]{1,0:T(8,128)(2,1)} %constant.68.clone.order_ref) | copy-start | bytes 61444
  6.5 19.4 %copy-start.10 = (s32[2,1]{0,1:T(1,128)S(1)}, s32[2,1]{0,1:T(1,128)}, u32[]{:S(2)}) copy-start(s32[2,1]{0,1:T(1,128)} %param.19) | copy-start | bytes 28
  6.5 21.0 %copy-start.9 = (f32[3,1152]{1,0:T(4,128)S(1)}, f32[3,1152]{1,0:T(4,128)}, u32[]{:S(2)}) copy-start(f32[3,1152]{1,0:T(4,128)} %param.27) | copy-start | bytes 41476
  6.5 21.0 %copy-start.8 = (f32[3,1152]{1,0:T(4,128)S(1)}, f32[3,1152]{1,0:T(4,128)}, u32[]{:S(2)}) copy-start(f32[3,1152]{1,0:T(4,128)} %param.28) | copy-start | bytes 41476
  6.5 21.4 %copy-start.7 = (f32[16,27,16]{1,2,0:T(8,128)S(1)}, f32[16,27,16]{1,2,0:T(8,128)}, u32[]{:S(2)}) copy-start(f32[16,27,16]{1,2,0:T(8,128)} %param.29) | copy-start | bytes 82948
  9.4 21.0 %collective-permute-start = (f32[5,16,128]{2,1,0:T(8,128)S(1)}, f32[5,16,128]{2,1,0:T(8,128)S(1)}, u32[]{:S(2)}, u32[]{:S(2)}) collective-permute-start(f32[5,16,128]{2,1,0:T(8,128)S(1)} %concatenate.32), channel_id=1, source_target_pairs={{16,0},{32,16},{48,32},{64,48},{80,64},{96,80},{112,96},{128,112},... | collective-permute-start | bytes 122888 | tf_op jit(solution)/shard_map/ppermute | solution.py:45
  16.2 33.1 %all-to-all-start = ((bf16[32,40,384]{2,1,0:T(8,128)(2,1)}), bf16[32,40,384]{2,1,0:T(8,128)(2,1)S(1)}, u32[]{:S(2)}, u32[]{:S(2)}) async-start(bf16[32,40,384]{2,1,0:T(8,128)(2,1)} %broadcast_in_dim.47), calls=%async_computation | async-start | bytes 1966080 | tf_op jit(solution)/shard_map/all_to_all | solution.py:49
  25.2 108.2 %all-gather.2.cloned.1.call-start = ((), (), s32[]{:S(2)}) async-start(), calls=%async_computation.5 | async-start | bytes 3481600 | tf_op jit(solution)/shard_map/all_gather | solution.py:568
  49.3 0.7 copy-start.4
  81.5 42.0 %copy-start.3 = (bf16[80,72]{1,0:T(8,128)(2,1)S(1)}, bf16[80,72]{1,0:T(8,128)(2,1)}, u32[]{:S(2)}) copy-start(bf16[80,72]{1,0:T(8,128)(2,1)} %constant.69.clone.widen_ref) | copy-start | bytes 34564
  83.9 30.4 %all-to-all-start.2 = ((bf16[16,144,128]{2,1,0:T(8,128)(2,1)}), bf16[16,144,128]{2,1,0:T(8,128)(2,1)S(1)}, u32[]{:S(2)}, u32[]{:S(2)}) async-start(bf16[16,144,128]{2,1,0:T(8,128)(2,1)} %get-tuple-element.35), calls=%async_computation.2 | async-start | bytes 1179648 | tf_op jit(solution)/shard_map/all_to_all | solution.py:49
  114.3 29.7 %all-to-all-start.3 = ((bf16[16,144,128]{2,1,0:T(8,128)(2,1)}), bf16[16,144,128]{2,1,0:T(8,128)(2,1)S(1)}, u32[]{:S(2)}, u32[]{:S(2)}) async-start(bf16[16,144,128]{2,1,0:T(8,128)(2,1)} %fold.3), calls=%async_computation.3 | async-start | bytes 1179648 | tf_op jit(solution)/shard_map/all_to_all | solution.py:49
  124.3 35.6 %copy-start.5 = (f32[1,4,16,128]{3,2,1,0:T(8,128)S(1)}, f32[1,4,16,128]{3,2,1,0:T(8,128)}, u32[]{:S(2)}) copy-start(f32[1,4,16,128]{3,2,1,0:T(8,128)} %param.18) | copy-start | bytes 98308
  133.4 1.9 copy-start
  138.2 9.3 %collective-permute-start.1 = (f32[4,16,128]{2,1,0:T(8,128)S(1)}, f32[4,16,128]{2,1,0:T(8,128)S(1)}, u32[]{:S(2)}, u32[]{:S(2)}) collective-permute-start(f32[4,16,128]{2,1,0:T(8,128)S(1)} %output.2.noise_ref), channel_id=1, source_target_pairs={{16,0},{32,16},{48,32},{64,48},{80,64},{96,80},{112,96},{128,112},... | collective-permute-start | bytes 98312 | tf_op jit(solution)/shard_map/ppermute | solution.py:45
  142.0 17.9 %collective-permute-start.2 = (f32[4,16,128]{2,1,0:T(8,128)S(1)}, f32[4,16,128]{2,1,0:T(8,128)S(1)}, u32[]{:S(2)}, u32[]{:S(2)}) collective-permute-start(f32[4,16,128]{2,1,0:T(8,128)S(1)} %output.2.noise_ref), channel_id=1, source_target_pairs={{32,0},{48,16},{64,32},{80,48},{96,64},{112,80},{128,96},{144,112}... | collective-permute-start | bytes 98312 | tf_op jit(solution)/shard_map/ppermute | solution.py:45
  162.4 17.8 %all-to-all-start.4 = ((bf16[16,96,128]{2,1,0:T(8,128)(2,1)}), bf16[16,96,128]{2,1,0:T(8,128)(2,1)S(1)}, u32[]{:S(2)}, u32[]{:S(2)}) async-start(bf16[16,96,128]{2,1,0:T(8,128)(2,1)} %get-tuple-element.47), calls=%async_computation.4 | async-start | bytes 786432 | tf_op jit(solution)/shard_map/all_to_all | solution.py:49
  180.1 9.0 %copy-start.1 = (bf16[1280,1280]{1,0:T(8,128)(2,1)S(1)}, bf16[1280,1280]{1,0:T(8,128)(2,1)}, u32[]{:S(2)}) copy-start(bf16[1280,1280]{1,0:T(8,128)(2,1)} %all-gather.2.cloned.1.call-done.wot_ref) | copy-start | bytes 9830404
  192.1 7.0 %collective-permute-start.3 = (f32[4,16,128]{2,1,0:T(8,128)S(1)}, f32[4,16,128]{2,1,0:T(8,128)S(1)}, u32[]{:S(2)}, u32[]{:S(2)}) collective-permute-start(f32[4,16,128]{2,1,0:T(8,128)S(1)} %output.3.noise_ref), channel_id=1, source_target_pairs={{0,16},{16,32},{32,48},{48,64},{64,80},{80,96},{96,112},{112,128},... | collective-permute-start | bytes 98312 | tf_op jit(solution)/shard_map/ppermute | solution.py:45
  197.2 7.9 %collective-permute-start.4 = (f32[4,16,128]{2,1,0:T(8,128)S(1)}, f32[4,16,128]{2,1,0:T(8,128)S(1)}, u32[]{:S(2)}, u32[]{:S(2)}) collective-permute-start(f32[4,16,128]{2,1,0:T(8,128)S(1)} %output.3.noise_ref), channel_id=1, source_target_pairs={{16,0},{32,16},{48,32},{64,48},{80,64},{96,80},{112,96},{128,112},... | collective-permute-start | bytes 98312 | tf_op jit(solution)/shard_map/ppermute | solution.py:45
  205.1 8.3 %collective-permute-start.6 = (f32[4,16,128]{2,1,0:T(8,128)S(1)}, f32[4,16,128]{2,1,0:T(8,128)S(1)}, u32[]{:S(2)}, u32[]{:S(2)}) collective-permute-start(f32[4,16,128]{2,1,0:T(8,128)S(1)} %pad_maximum_fusion.1), channel_id=1, source_target_pairs={{1,0},{2,1},{3,2},{4,3},{5,4},{6,5},{7,6},{8,7},{9,8},{10,9},{11,1... | collective-permute-start | bytes 98312 | tf_op jit(solution)/shard_map/ppermute | solution.py:45
  211.5 11.3 %collective-permute-start.5 = (f32[4,16,128]{2,1,0:T(8,128)S(1)}, f32[4,16,128]{2,1,0:T(8,128)S(1)}, u32[]{:S(2)}, u32[]{:S(2)}) collective-permute-start(f32[4,16,128]{2,1,0:T(8,128)S(1)} %pad_maximum_fusion), channel_id=1, source_target_pairs={{0,1},{1,2},{2,3},{3,4},{4,5},{5,6},{6,7},{7,8},{8,9},{9,10},{10,1... | collective-permute-start | bytes 98312 | tf_op jit(solution)/shard_map/ppermute | solution.py:45
Sparse Core Ops, SparseCore 0:
  51.2 76.1 all-gather.1

commit v5 on v3

--- a/solution.py
+++ b/solution.py
@@ -179,6 +179,23 @@
         if r == 3:
             latent = latent + down_ref[3]
         out_ref[r] = latent + scalar_ref[0] * (noise_ref[r] + mixed[r])
+
+
+def pack_kernel(in_ref, qkv_ref, o_ref, last_ref, time_ref, pos_ref, out_ref, held):
+    held[...] = jnp.zeros_like(held)
+    held[0:ROWS, 0:216] = qkv_ref[...].astype(F32)
+    held[0:ROWS, 256:328] = o_ref[...].astype(F32)
+    held[0:ROWS, 328:332] = last_ref[...].astype(F32)
+    at = 0
+    for ref in (time_ref, pos_ref, in_ref):
+        block = ref[...].astype(F32)
+        for q in range(ref.shape[0]):
+            for h in range(2):
+                held[at : at + 1, 216:252] = block[q : q + 1, ROWS * h : ROWS * h + ROWS]
+                at += 1
+    packed = held[...].astype(BF16)
+    for i in range(TM):
+        out_ref[i] = packed
 
 
 def spread_kernel(x_ref, pick_ref, emb_ref, mod_ref, order_ref, patch_ref, pay_ref, out_t_ref):
@@ -283,9 +300,13 @@
     return (patches + added).astype(BF16)
 
 
-def attend_kernel(
-    edges, spot_ref, pt_ref, gram_ref, n_ref, mvt_ref, att_ref, own_ref, keys_t, keys, held
+def block_kernel(
+    step, spot_ref, pt_ref, gram_ref, n_ref, mvt_ref, feat_ref, far_ref, out_ref,
+    keys_t, keys, held, att_ref, wot_ref, stream_ref, fetched,
 ):
+    fetch = pltpu.make_async_copy(far_ref, wot_ref, fetched)
+    fetch.start()
+    edges = step > 0
     me = spot_ref[0]
     row = lax.broadcasted_iota(jnp.int32, (PF, TOK), 0)
     ones = jnp.where(row == 0, 1.0, 0.0).astype(F32)
@@ -304,7 +325,6 @@
         wide = jnp.concatenate([unit[:, j * TOK : (j + 1) * TOK], ones], axis=0)
         keys_t[:, j * TOK : (j + 1) * TOK] = wide.astype(BF16)
         keys[j * TOK : (j + 1) * TOK, :] = wide.T.astype(BF16)
-    own_ref[...] = held[me]
 
     def two_heads(pair):
         own = keys[pl.ds(pl.multiple_of(me * TOK, TOK), TOK), :]
@@ -326,18 +346,14 @@
         for k in range(4):
             two_heads(4 * i + k)
 
-
-def output_kernel(
-    step, spot_ref, att_ref, own_ref, feat_ref, wot_ref, out_ref, stream_ref
-):
-    me = spot_ref[0]
+    fetch.wait()
     delta = nn(wot_ref[...], att_ref[...])
     for b in range(TILE):
         tile = ((me ^ (8 * (b % 2))) & 8) + b // 2
         rows = pl.ds(pl.multiple_of(tile * 80, 80), 80)
         stream_ref[rows, :] = delta[80 * b : 80 * b + 80]
     feat = jnp.concatenate([feat_ref[t, PF:] for t in range(TILE)], axis=0)
-    own = jnp.concatenate([own_ref[...], jnp.zeros((PF, TOK), BF16)], axis=0)
+    own = jnp.concatenate([held[me], jnp.zeros((PF, TOK), BF16)], axis=0)
     at = PF + 3 * step + 2
     gate = feat[:, at : at + 1].astype(F32) + feat[:, at + 6 : at + 7].astype(F32)
     valid = feat[:, 76:77].astype(F32)
@@ -418,40 +434,29 @@
     )(folded, jnp.asarray(ORDER[:, 0:HEAD], BF16))
 
 
-def attend(edges, spot, pt, gram, n, mvt):
-    return pl.pallas_call(
-        functools.partial(attend_kernel, edges),
-        out_shape=(
-            jax.ShapeDtypeStruct((WIDE, TOK), BF16),
-            jax.ShapeDtypeStruct((PF, TOK), BF16),
-        ),
-        in_specs=[SMEM] + [BLOCK] * 4,
-        out_specs=(VMEM, VMEM),
+def frame_block(step, spot, pt, gram, n, mvt, feat, wot):
+    return pl.pallas_call(
+        functools.partial(block_kernel, step),
+        out_shape=jax.ShapeDtypeStruct((4, C, LANES), F32),
+        in_specs=[SMEM] + [BLOCK] * 5 + [pl.BlockSpec(memory_space=pl.ANY)],
+        out_specs=VMEM,
         scratch_shapes=[
             pltpu.VMEM((LANES, SPAN), BF16),
             pltpu.VMEM((SPAN, LANES), BF16),
             pltpu.VMEM((TILE, PF, TOK), BF16),
+            pltpu.VMEM((WIDE, TOK), BF16),
+            pltpu.VMEM((WIDE, WIDE), BF16),
+            pltpu.VMEM((WIDE, TOK), F32),
+            pltpu.SemaphoreType.DMA,
         ],
-        compiler_params=pltpu.CompilerParams(vmem_limit_bytes=40 * 1024 * 1024),
+        compiler_params=pltpu.CompilerParams(vmem_limit_bytes=48 * 1024 * 1024),
         cost_estimate=pl.CostEstimate(
             flops=4 * 2 * SPAN * SPAN * LANES,
             bytes_accessed=8 * SPAN * LANES,
             transcendentals=SPAN * SPAN,
         ),
-        name="attend",
-    )(spot, pt, gram, n, mvt)
-
-
-def output(step, spot, att, own, feat, wot):
-    return pl.pallas_call(
-        functools.partial(output_kernel, step),
-        out_shape=jax.ShapeDtypeStruct((4, C, LANES), F32),
-        in_specs=[SMEM] + [VMEM] * 4,
-        out_specs=VMEM,
-        scratch_shapes=[pltpu.VMEM((WIDE, TOK), F32)],
-        compiler_params=pltpu.CompilerParams(vmem_limit_bytes=32 * 1024 * 1024),
-        name="output",
-    )(spot, att, own, feat, wot)
+        name="frame_block",
+    )(spot, pt, gram, n, mvt, feat, wot)
 
 
 def prep(scale_in, latent):
@@ -515,11 +520,14 @@
 
 
 def packed_weights(w_in, w_qkv, w_o, w_out, w_time, w_pos):
-    small = jnp.concatenate([w_time, w_pos, w_in], axis=0).reshape(ROWS, ROWS)
-    gap = jnp.zeros((ROWS, 4), BF16)
-    tail = jnp.zeros((ROWS, 52), BF16)
-    packed = jnp.concatenate([w_qkv, small, gap, w_o, w_out, tail], axis=1)
-    return jnp.pad(packed, ((0, 4), (0, 0)))
+    return pl.pallas_call(
+        pack_kernel,
+        out_shape=jax.ShapeDtypeStruct((TM, 40, 384), BF16),
+        in_specs=[BLOCK] * 6,
+        out_specs=VMEM,
+        scratch_shapes=[pltpu.VMEM((40, 384), F32)],
+        name="pack",
+    )(w_in, w_qkv, w_o, w_out, w_time, w_pos)
 
 
 def embeddings(level, position):
@@ -553,7 +561,7 @@
     scale_in = lax.rsqrt(1.0 + sigma_now * sigma_now)
 
     packed = packed_weights(w_in, w_qkv, w_o, w_out, w_time, w_pos)
-    rows = exchanged(jnp.broadcast_to(packed[None], (TM,) + packed.shape), TM_AXES)
+    rows = exchanged(packed, TM_AXES)
     rows = rows.reshape(WIDE, 384)
 
     own = prep(scale_in[0:1], latent)
@@ -579,11 +587,10 @@
     both = jnp.stack([out_t, swapped(out_t, "zh")])
     full_o = lax.all_gather(both, ("x", "core")).reshape(WIDE, WIDE)
 
-    att, own = attend(False, spot, feat, gram, n, mvt)
-    att, second = lax.optimization_barrier((att, second))
-    noise = output(0, spot, att, own, feat, full_o)
+    noise = frame_block(0, spot, feat, gram, n, mvt, feat, full_o)
 
     following, after = shifted(noise, TM_AXES, -1), shifted(noise, TM_AXES, -2)
+    following, second = lax.optimization_barrier((following, second))
     last = (frame == TM - 1).astype(jnp.int32)[None]
     latent, edges, patches = middle(
         scale_in[1:2], last, noise, following, after, marked, new_frames[0], mix
@@ -591,8 +598,7 @@
     patches = exchanged(patches, TILE_AXES)
     n, mvt = heads(second)
 
-    att, own = attend(True, spot, patches, gram, n, mvt)
-    noise = output(1, spot, att, own, feat, full_o)
+    noise = frame_block(1, spot, patches, gram, n, mvt, feat, full_o)
     frames = [shifted(noise, TM_AXES, 1), noise, shifted(noise, TM_AXES, -1)]
     up = jnp.stack([x[3] for x in frames] + [edges[1]])
     down = jnp.stack([x[0] for x in frames] + [edges[0]])

time: 231 us -> 229 us (level)
  waiting for transfers between devices: 75.5 us -> 67.4 us
  starting transfers between devices: 59.7 us -> 63.8 us
  Pallas kernels: 37.2 us -> 40 us
    all_to_all x4, waiting for transfers between devices: 41.2 us -> 32.1 us  [exchanged(): return lax.all_to_all(copies, axis, split_axis=0, concat_axis=0, tiled=True)]
    all_to_all x4, starting transfers between devices: 27.9 us -> 32.2 us  [exchanged(): return lax.all_to_all(copies, axis, split_axis=0, concat_axis=0, tiled=True)]
    pallas_call x4 -> x3, Pallas kernels: 24.3 us -> 27 us  [the longest x2 25.1 us: frame_block(): pl.pallas_call(functools.partial(block_kernel, step), out_shape=jax.Shape...]
    unnamed x25, local copies, waits for them, and re-layouts: 3.74 us -> 6.3 us
  transfers between devices with their start and end apart: 13 -> 13, of which waited for: 10 -> 9; matrix products, arithmetic and copies ran while one was open for 2% -> 2% of each run, Pallas kernels for 7% -> 9%
where the time goes in v5:
time: 229 us; the launch traced here: 228 us
  waiting for transfers between devices  67.4 us (29%)
  starting transfers between devices  63.8 us (28%)
  Pallas kernels  40 us (17%)
  blocking collectives  30.8 us (13%)
  between operations  14.4 us (6%)
  local copies, waits for them, and re-layouts  10.1 us (4%)
    all_to_all x4, starting transfers between devices, exchanged(): return lax.all_to_all(copies, axis, split_axis=0, concat_axis=0, tiled=True)  32.2 us
    all_to_all x4, waiting for transfers between devices, exchanged(): return lax.all_to_all(copies, axis, split_axis=0, concat_axis=0, tiled=True)  32.1 us
    ppermute x7, waiting for transfers between devices, shifted(): return lax.ppermute(block, axis, route)  32 us
    all_to_all x1, blocking collectives, exchanged(): return lax.all_to_all(copies, axis, split_axis=0, concat_axis=0, tiled=True)  30.8 us
    pallas_call x2, Pallas kernels, frame_block(): pl.pallas_call(functools.partial(block_kernel, step), out_shape=jax.Shape...  25.1 us
    ppermute x7, starting transfers between devices, shifted(): return lax.ppermute(block, axis, route)  23.6 us
    ppermute x1, starting transfers between devices, swapped(): return lax.ppermute(block, axis, [(0, 1), (1, 0)])  7.93 us
    unnamed x25, local copies, waits for them, and re-layouts  6.3 us
  transfers between devices with their start and end apart: 13, of which 9 were waited for; matrix products, arithmetic and copies ran while one was open for 2% of the time, Pallas kernels for 9%

profile of v5, /device:TPU:63, one launch (start us, length us, event | category | flops | bytes accessed | tf_op | source)
XLA Modules:
  0.0 228.4 jit_solution(6495184364303470905)
XLA Ops:
  6.6 1.4 copy.25.last_ref
  8.0 1.9 pack.1
  9.9 11.9 %all-to-all-start = ((bf16[32,40,384]{2,1,0:T(8,128)(2,1)}), bf16[32,40,384]{2,1,0:T(8,128)(2,1)S(1)}, u32[]{:S(2)}, u32[]{:S(2)}) async-start(bf16[32,40,384]{2,1,0:T(8,128)(2,1)} %pack.1), calls=%async_computation | async-start | bytes 1966080 | tf_op jit(solution)/shard_map/all_to_all | solution.py:53
  21.8 0.0 all-gather.3.cloned.1.call-start
  21.8 0.7 add_rsqrt_fusion
  22.6 0.7 fusion.9
  23.2 1.4 concatenate.24
  24.7 3.1 %collective-permute-start = (f32[5,16,128]{2,1,0:T(8,128)S(1)}, f32[5,16,128]{2,1,0:T(8,128)S(1)}, u32[]{:S(2)}, u32[]{:S(2)}) collective-permute-start(f32[5,16,128]{2,1,0:T(8,128)S(1)} %concatenate.24), channel_id=1, source_target_pairs={{16,0},{32,16},{48,32},{64,48},{80,64},{96,80},{112,96},{128,112},... | collective-permute-start | bytes 122888 | tf_op jit(solution)/shard_map/ppermute | solution.py:49
  27.8 0.1 mul.107
  27.8 0.4 mul.108
  28.9 0.1 pad.28.clone
  29.0 0.1 fusion
  29.1 0.1 maximum_maximum_fusion.1
  29.2 0.1 copy.27
  29.3 0.3 mul.104
  29.6 0.4 mul.105
  30.0 0.1 pad.23.clone
  30.1 0.0 copy-done.9
  30.1 0.1 maximum_maximum_fusion
  30.2 0.1 reshape.122
  30.3 0.2 copy.26
  30.5 0.1 reshape.121.mix_ref
  30.7 0.1 reshape.123
  30.8 0.1 copy.31
  30.9 2.1 prep.1.patch_ref
  33.0 10.5 %collective-permute-done.lat_ref = f32[5,16,128]{2,1,0:T(8,128)S(1)} collective-permute-done((f32[5,16,128]{2,1,0:T(8,128)S(1)}, f32[5,16,128]{2,1,0:T(8,128)S(1)}, u32[]{:S(2)}, u32[]{:S(2)}) %collective-permute-start) | collective-permute-done | bytes 40992 | tf_op jit(solution)/shard_map/ppermute | solution.py:49
  43.6 1.8 all-to-all-done
  45.3 0.0 copy-done.4
  45.3 0.7 copy-done.2
  46.1 0.8 spread.1
  46.9 7.9 %collective-permute-start.1 = (bf16[80,1280]{1,0:T(8,128)(2,1)S(1)}, bf16[80,1280]{1,0:T(8,128)(2,1)S(1)}, u32[]{:S(2)}, u32[]{:S(2)}) collective-permute-start(bf16[80,1280]{1,0:T(8,128)(2,1)S(1)} %get-tuple-element.36), channel_id=1, source_target_pairs={{0,8},{8,0},{1,9},{9,1},{2,10},{10,2},{3,11},{11,3},{4,12},{12,4},... | collective-permute-start | bytes 614408 | tf_op jit(solution)/shard_map/ppermute | solution.py:43
  54.8 3.2 %collective-permute-done.1 = bf16[80,1280]{1,0:T(8,128)(2,1)S(1)} collective-permute-done((bf16[80,1280]{1,0:T(8,128)(2,1)S(1)}, bf16[80,1280]{1,0:T(8,128)(2,1)S(1)}, u32[]{:S(2)}, u32[]{:S(2)}) %collective-permute-start.1) | collective-permute-done | bytes 204832 | tf_op jit(solution)/shard_map/ppermute | solution.py:43
  58.0 0.8 pad_maximum_fusion
  58.8 0.0 all-gather.3.cloned.1.call-update
  58.9 30.8 %all_to_all.25.feat_ref.pt_ref = bf16[16,144,128]{2,1,0:T(8,128)(2,1)S(1)} all-to-all(bf16[16,144,128]{2,1,0:T(8,128)(2,1)S(1)} %get-tuple-element.27), channel_id=1, replica_groups=mesh['zl'=4,'y'=8,'zh'=2,'x'=4,'core'=2] {'zh','x','core'}, dimensions={0} | all-to-all | bytes 1179648 | tf_op jit(solution)/shard_map/all_to_all | solution.py:53
  89.6 2.4 %fold.2 = (bf16[16,144,128]{2,1,0:T(8,128)(2,1)}, bf16[128,64]{1,0:T(8,128)(2,1)S(1)}) custom-call(bf16[16,144,128]{2,1,0:T(8,128)(2,1)S(1)} %all_to_all.25.feat_ref.pt_ref, bf16[1280,384]{1,0:T(8,128)(2,1)S(1)} %bitcast.24), custom_call_target="tpu_custom_call" | custom-call | flops 167772160 | bytes 1310720 | tf_op jit(solution)/shard_map/fold/pallas_call | solution.py:409
  92.0 5.5 %all-to-all-start.2 = ((bf16[16,144,128]{2,1,0:T(8,128)(2,1)}), bf16[16,144,128]{2,1,0:T(8,128)(2,1)S(1)}, u32[]{:S(2)}, u32[]{:S(2)}) async-start(bf16[16,144,128]{2,1,0:T(8,128)(2,1)} %get-tuple-element.31), calls=%async_computation.2 | async-start | bytes 1179648 | tf_op jit(solution)/shard_map/all_to_all | solution.py:53
  97.6 2.0 fold.3
  99.6 16.9 %all-to-all-done.2.folded_ref = bf16[16,144,128]{2,1,0:T(8,128)(2,1)S(1)} async-done(((bf16[16,144,128]{2,1,0:T(8,128)(2,1)}), bf16[16,144,128]{2,1,0:T(8,128)(2,1)S(1)}, u32[]{:S(2)}, u32[]{:S(2)}) %all-to-all-start.2) | async-done | bytes 589856 | tf_op jit(solution)/shard_map/all_to_all | solution.py:53
  116.5 4.3 %all-to-all-start.3 = ((bf16[16,144,128]{2,1,0:T(8,128)(2,1)}), bf16[16,144,128]{2,1,0:T(8,128)(2,1)S(1)}, u32[]{:S(2)}, u32[]{:S(2)}) async-start(bf16[16,144,128]{2,1,0:T(8,128)(2,1)} %fold.3), calls=%async_computation.3 | async-start | bytes 1179648 | tf_op jit(solution)/shard_map/all_to_all | solution.py:53
  120.8 0.8 heads.2
  121.6 0.0 all-gather.3.cloned.1.call-done
  121.6 1.9 copy-done.5
  123.5 12.5 %frame_block.2.noise_ref = f32[4,16,128]{2,1,0:T(8,128)S(1)} custom-call(s32[1]{0:T(128)} %bitcast.1.spot_ref, bf16[16,144,128]{2,1,0:T(8,128)(2,1)S(1)} %all_to_all.25.feat_ref.pt_ref, bf16[128,64]{1,0:T(8,128)(2,1)S(1)} %get-tuple-element.30.gram_ref, bf16[16,128,128]{2,1,0:T(8,128)(2,1)S(1)} %get-tuple-element.34.n_ref, ...), custom_call_target="tpu_custom_call" | custom-call | flops 4294967296 | bytes 2097152 | tf_op jit(solution)/shard_map/frame_block/pallas_call | solution.py:438
  136.0 2.6 %collective-permute-start.2 = (f32[4,16,128]{2,1,0:T(8,128)S(1)}, f32[4,16,128]{2,1,0:T(8,128)S(1)}, u32[]{:S(2)}, u32[]{:S(2)}) collective-permute-start(f32[4,16,128]{2,1,0:T(8,128)S(1)} %frame_block.2.noise_ref), channel_id=1, source_target_pairs={{16,0},{32,16},{48,32},{64,48},{80,64},{96,80},{112,96},{128,112},... | collective-permute-start | bytes 98312 | tf_op jit(solution)/shard_map/ppermute | solution.py:49
  138.7 3.5 %collective-permute-start.3 = (f32[4,16,128]{2,1,0:T(8,128)S(1)}, f32[4,16,128]{2,1,0:T(8,128)S(1)}, u32[]{:S(2)}, u32[]{:S(2)}) collective-permute-start(f32[4,16,128]{2,1,0:T(8,128)S(1)} %frame_block.2.noise_ref), channel_id=1, source_target_pairs={{32,0},{48,16},{64,32},{80,48},{96,64},{112,80},{128,96},{144,112}... | collective-permute-start | bytes 98312 | tf_op jit(solution)/shard_map/ppermute | solution.py:49
  142.2 0.0 all-to-all-done.3.folded_ref
  142.2 1.5 collective-permute-done.2.next_ref
  143.8 5.8 %collective-permute-done.3.after_ref = f32[4,16,128]{2,1,0:T(8,128)S(1)} collective-permute-done((f32[4,16,128]{2,1,0:T(8,128)S(1)}, f32[4,16,128]{2,1,0:T(8,128)S(1)}, u32[]{:S(2)}, u32[]{:S(2)}) %collective-permute-start.3) | collective-permute-done | bytes 32800 | tf_op jit(solution)/shard_map/ppermute | solution.py:49
  149.6 2.4 %middle.1 = (f32[4,16,128]{2,1,0:T(8,128)S(1)}, f32[2,16,128]{2,1,0:T(8,128)S(1)}, bf16[16,96,128]{2,1,0:T(8,128)(2,1)}) custom-call(f32[1]{0:T(128)} %bitcast.2.scalar_ref, s32[1]{0:T(128)} %bitcast.3.flag_ref, f32[4,16,128]{2,1,0:T(8,128)S(1)} %frame_block.2.noise_ref, f32[4,16,128]{2,1,0:T(8,128)S(1)} %collective-permute-done.2.next_ref, ...), custom_call_target="tpu_custom_call" | custom-call | tf_op jit(solution)/shard_map/middle/pallas_call | solution.py:473
  152.0 10.5 %all-to-all-start.4 = ((bf16[16,96,128]{2,1,0:T(8,128)(2,1)}), bf16[16,96,128]{2,1,0:T(8,128)(2,1)S(1)}, u32[]{:S(2)}, u32[]{:S(2)}) async-start(bf16[16,96,128]{2,1,0:T(8,128)(2,1)} %get-tuple-element.41), calls=%async_computation.4 | async-start | bytes 786432 | tf_op jit(solution)/shard_map/all_to_all | solution.py:53
  162.5 0.8 heads.3
  163.3 13.3 %all-to-all-done.4.pt_ref = bf16[16,96,128]{2,1,0:T(8,128)(2,1)S(1)} async-done(((bf16[16,96,128]{2,1,0:T(8,128)(2,1)}), bf16[16,96,128]{2,1,0:T(8,128)(2,1)S(1)}, u32[]{:S(2)}, u32[]{:S(2)}) %all-to-all-start.4) | async-done | bytes 393248 | tf_op jit(solution)/shard_map/all_to_all | solution.py:53
  176.7 1.9 copy-done.6
  178.6 12.6 %frame_block.3.noise_ref = f32[4,16,128]{2,1,0:T(8,128)S(1)} custom-call(s32[1]{0:T(128)} %bitcast.1.spot_ref, bf16[16,96,128]{2,1,0:T(8,128)(2,1)S(1)} %all-to-all-done.4.pt_ref, bf16[128,64]{1,0:T(8,128)(2,1)S(1)} %get-tuple-element.30.gram_ref, bf16[16,128,128]{2,1,0:T(8,128)(2,1)S(1)} %get-tuple-element.43.n_ref, ...), custom_call_target="tpu_custom_call" | custom-call | flops 4294967296 | bytes 2097152 | tf_op jit(solution)/shard_map/frame_block/pallas_call | solution.py:438
  191.2 5.1 %collective-permute-start.4 = (f32[4,16,128]{2,1,0:T(8,128)S(1)}, f32[4,16,128]{2,1,0:T(8,128)S(1)}, u32[]{:S(2)}, u32[]{:S(2)}) collective-permute-start(f32[4,16,128]{2,1,0:T(8,128)S(1)} %frame_block.3.noise_ref), channel_id=1, source_target_pairs={{0,16},{16,32},{32,48},{48,64},{64,80},{80,96},{96,112},{112,128},... | collective-permute-start | bytes 98312 | tf_op jit(solution)/shard_map/ppermute | solution.py:49
  196.3 1.9 collective-permute-start.5
  198.2 4.8 %collective-permute-done.5.next_ref = f32[4,16,128]{2,1,0:T(8,128)S(1)} collective-permute-done((f32[4,16,128]{2,1,0:T(8,128)S(1)}, f32[4,16,128]{2,1,0:T(8,128)S(1)}, u32[]{:S(2)}, u32[]{:S(2)}) %collective-permute-start.5) | collective-permute-done | bytes 32800 | tf_op jit(solution)/shard_map/ppermute | solution.py:49
  203.0 0.0 collective-permute-done.4.before_ref
  203.1 5.4 %collective-permute-start.6 = (f32[4,16,128]{2,1,0:T(8,128)S(1)}, f32[4,16,128]{2,1,0:T(8,128)S(1)}, u32[]{:S(2)}, u32[]{:S(2)}) collective-permute-start(f32[4,16,128]{2,1,0:T(8,128)S(1)} %pad_maximum_fusion.1), channel_id=1, source_target_pairs={{0,1},{1,2},{2,3},{3,4},{4,5},{5,6},{6,7},{7,8},{8,9},{9,10},{10,1... | collective-permute-start | bytes 98312 | tf_op jit(solution)/shard_map/ppermute | solution.py:49
  208.5 1.9 collective-permute-start.7
  210.4 0.0 collective-permute-done.6.up_ref
  210.4 9.3 %collective-permute-done.7.down_ref = f32[4,16,128]{2,1,0:T(8,128)S(1)} collective-permute-done((f32[4,16,128]{2,1,0:T(8,128)S(1)}, f32[4,16,128]{2,1,0:T(8,128)S(1)}, u32[]{:S(2)}, u32[]{:S(2)}) %collective-permute-start.7) | collective-permute-done | bytes 32800 | tf_op jit(solution)/shard_map/ppermute | solution.py:49
  219.7 1.8 finish.1
  (33 shorter events, 0.1 us)
Async XLA Ops:
  6.5 38.8 %copy-start = (bf16[2,64,1280]{2,1,0:T(8,128)(2,1)S(1)}, bf16[2,64,1280]{2,1,0:T(8,128)(2,1)}, u32[]{:S(2)}) copy-start(bf16[2,64,1280]{2,1,0:T(8,128)(2,1)} %constant.65.clone.pick_ref) | copy-start | bytes 983044
  6.5 38.8 %copy-start.4 = (bf16[80,128]{1,0:T(8,128)(2,1)S(1)}, bf16[80,128]{1,0:T(8,128)(2,1)}, u32[]{:S(2)}) copy-start(bf16[80,128]{1,0:T(8,128)(2,1)} %constant.66.clone.order_ref) | copy-start | bytes 61444
  6.5 22.4 %copy-start.10 = (s32[2,1]{0,1:T(1,128)S(1)}, s32[2,1]{0,1:T(1,128)}, u32[]{:S(2)}) copy-start(s32[2,1]{0,1:T(1,128)} %param.19) | copy-start | bytes 28
  6.5 23.6 %copy-start.8 = (f32[3,1152]{1,0:T(4,128)S(1)}, f32[3,1152]{1,0:T(4,128)}, u32[]{:S(2)}) copy-start(f32[3,1152]{1,0:T(4,128)} %param.28) | copy-start | bytes 41476
  6.5 23.6 %copy-start.9 = (f32[3,1152]{1,0:T(4,128)S(1)}, f32[3,1152]{1,0:T(4,128)}, u32[]{:S(2)}) copy-start(f32[3,1152]{1,0:T(4,128)} %param.27) | copy-start | bytes 41476
  6.5 23.8 %copy-start.7 = (f32[16,27,16]{1,2,0:T(8,128)S(1)}, f32[16,27,16]{1,2,0:T(8,128)}, u32[]{:S(2)}) copy-start(f32[16,27,16]{1,2,0:T(8,128)} %param.29) | copy-start | bytes 82948
  9.9 35.4 %all-to-all-start = ((bf16[32,40,384]{2,1,0:T(8,128)(2,1)}), bf16[32,40,384]{2,1,0:T(8,128)(2,1)S(1)}, u32[]{:S(2)}, u32[]{:S(2)}) async-start(bf16[32,40,384]{2,1,0:T(8,128)(2,1)} %pack.1), calls=%async_computation | async-start | bytes 1966080 | tf_op jit(solution)/shard_map/all_to_all | solution.py:53
  21.8 99.8 %all-gather.3.cloned.1.call-start = ((), (), s32[]{:S(2)}) async-start(), calls=%async_computation.5 | async-start | bytes 3686400 | tf_op jit(solution)/shard_map/all_gather | solution.py:588
  24.7 18.9 %collective-permute-start = (f32[5,16,128]{2,1,0:T(8,128)S(1)}, f32[5,16,128]{2,1,0:T(8,128)S(1)}, u32[]{:S(2)}, u32[]{:S(2)}) collective-permute-start(f32[5,16,128]{2,1,0:T(8,128)S(1)} %concatenate.24), channel_id=1, source_target_pairs={{16,0},{32,16},{48,32},{64,48},{80,64},{96,80},{112,96},{128,112},... | collective-permute-start | bytes 122888 | tf_op jit(solution)/shard_map/ppermute | solution.py:49
  45.3 0.7 copy-start.2
  46.9 11.2 %collective-permute-start.1 = (bf16[80,1280]{1,0:T(8,128)(2,1)S(1)}, bf16[80,1280]{1,0:T(8,128)(2,1)S(1)}, u32[]{:S(2)}, u32[]{:S(2)}) collective-permute-start(bf16[80,1280]{1,0:T(8,128)(2,1)S(1)} %get-tuple-element.36), channel_id=1, source_target_pairs={{0,8},{8,0},{1,9},{9,1},{2,10},{10,2},{3,11},{11,3},{4,12},{12,4},... | collective-permute-start | bytes 614408 | tf_op jit(solution)/shard_map/ppermute | solution.py:43
  89.6 31.2 %copy-start.1 = (bf16[80,72]{1,0:T(8,128)(2,1)S(1)}, bf16[80,72]{1,0:T(8,128)(2,1)}, u32[]{:S(2)}) copy-start(bf16[80,72]{1,0:T(8,128)(2,1)} %constant.67.clone.widen_ref) | copy-start | bytes 34564
  92.0 24.5 %all-to-all-start.2 = ((bf16[16,144,128]{2,1,0:T(8,128)(2,1)}), bf16[16,144,128]{2,1,0:T(8,128)(2,1)S(1)}, u32[]{:S(2)}, u32[]{:S(2)}) async-start(bf16[16,144,128]{2,1,0:T(8,128)(2,1)} %get-tuple-element.31), calls=%async_computation.2 | async-start | bytes 1179648 | tf_op jit(solution)/shard_map/all_to_all | solution.py:53
  116.5 25.7 %all-to-all-start.3 = ((bf16[16,144,128]{2,1,0:T(8,128)(2,1)}), bf16[16,144,128]{2,1,0:T(8,128)(2,1)S(1)}, u32[]{:S(2)}, u32[]{:S(2)}) async-start(bf16[16,144,128]{2,1,0:T(8,128)(2,1)} %fold.3), calls=%async_computation.3 | async-start | bytes 1179648 | tf_op jit(solution)/shard_map/all_to_all | solution.py:53
  121.6 1.9 copy-start.5
  123.5 26.1 %copy-start.3 = (f32[1,4,16,128]{3,2,1,0:T(8,128)S(1)}, f32[1,4,16,128]{3,2,1,0:T(8,128)}, u32[]{:S(2)}) copy-start(f32[1,4,16,128]{3,2,1,0:T(8,128)} %param.18) | copy-start | bytes 98308
  136.0 7.7 %collective-permute-start.2 = (f32[4,16,128]{2,1,0:T(8,128)S(1)}, f32[4,16,128]{2,1,0:T(8,128)S(1)}, u32[]{:S(2)}, u32[]{:S(2)}) collective-permute-start(f32[4,16,128]{2,1,0:T(8,128)S(1)} %frame_block.2.noise_ref), channel_id=1, source_target_pairs={{16,0},{32,16},{48,32},{64,48},{80,64},{96,80},{112,96},{128,112},... | collective-permute-start | bytes 98312 | tf_op jit(solution)/shard_map/ppermute | solution.py:49
  138.7 10.9 %collective-permute-start.3 = (f32[4,16,128]{2,1,0:T(8,128)S(1)}, f32[4,16,128]{2,1,0:T(8,128)S(1)}, u32[]{:S(2)}, u32[]{:S(2)}) collective-permute-start(f32[4,16,128]{2,1,0:T(8,128)S(1)} %frame_block.2.noise_ref), channel_id=1, source_target_pairs={{32,0},{48,16},{64,32},{80,48},{96,64},{112,80},{128,96},{144,112}... | collective-permute-start | bytes 98312 | tf_op jit(solution)/shard_map/ppermute | solution.py:49
  152.0 24.6 %all-to-all-start.4 = ((bf16[16,96,128]{2,1,0:T(8,128)(2,1)}), bf16[16,96,128]{2,1,0:T(8,128)(2,1)S(1)}, u32[]{:S(2)}, u32[]{:S(2)}) async-start(bf16[16,96,128]{2,1,0:T(8,128)(2,1)} %get-tuple-element.41), calls=%async_computation.4 | async-start | bytes 786432 | tf_op jit(solution)/shard_map/all_to_all | solution.py:53
  176.7 1.9 copy-start.6
  191.2 11.9 %collective-permute-start.4 = (f32[4,16,128]{2,1,0:T(8,128)S(1)}, f32[4,16,128]{2,1,0:T(8,128)S(1)}, u32[]{:S(2)}, u32[]{:S(2)}) collective-permute-start(f32[4,16,128]{2,1,0:T(8,128)S(1)} %frame_block.3.noise_ref), channel_id=1, source_target_pairs={{0,16},{16,32},{32,48},{48,64},{64,80},{80,96},{96,112},{112,128},... | collective-permute-start | bytes 98312 | tf_op jit(solution)/shard_map/ppermute | solution.py:49
  196.3 6.8 %collective-permute-start.5 = (f32[4,16,128]{2,1,0:T(8,128)S(1)}, f32[4,16,128]{2,1,0:T(8,128)S(1)}, u32[]{:S(2)}, u32[]{:S(2)}) collective-permute-start(f32[4,16,128]{2,1,0:T(8,128)S(1)} %frame_block.3.noise_ref), channel_id=1, source_target_pairs={{16,0},{32,16},{48,32},{64,48},{80,64},{96,80},{112,96},{128,112},... | collective-permute-start | bytes 98312 | tf_op jit(solution)/shard_map/ppermute | solution.py:49
  203.1 7.4 %collective-permute-start.6 = (f32[4,16,128]{2,1,0:T(8,128)S(1)}, f32[4,16,128]{2,1,0:T(8,128)S(1)}, u32[]{:S(2)}, u32[]{:S(2)}) collective-permute-start(f32[4,16,128]{2,1,0:T(8,128)S(1)} %pad_maximum_fusion.1), channel_id=1, source_target_pairs={{0,1},{1,2},{2,3},{3,4},{4,5},{5,6},{6,7},{7,8},{8,9},{9,10},{10,1... | collective-permute-start | bytes 98312 | tf_op jit(solution)/shard_map/ppermute | solution.py:49
  208.5 11.3 %collective-permute-start.7 = (f32[4,16,128]{2,1,0:T(8,128)S(1)}, f32[4,16,128]{2,1,0:T(8,128)S(1)}, u32[]{:S(2)}, u32[]{:S(2)}) collective-permute-start(f32[4,16,128]{2,1,0:T(8,128)S(1)} %pad_maximum_fusion.2), channel_id=1, source_target_pairs={{1,0},{2,1},{3,2},{4,3},{5,4},{6,5},{7,6},{8,7},{9,8},{10,9},{11,1... | collective-permute-start | bytes 98312 | tf_op jit(solution)/shard_map/ppermute | solution.py:49
Sparse Core Ops, SparseCore 0:
  59.0 45.2 all-gather.2

commit v6 on v3

--- a/solution.py
+++ b/solution.py
@@ -179,6 +179,23 @@
         if r == 3:
             latent = latent + down_ref[3]
         out_ref[r] = latent + scalar_ref[0] * (noise_ref[r] + mixed[r])
+
+
+def pack_kernel(in_ref, qkv_ref, o_ref, last_ref, time_ref, pos_ref, out_ref, held):
+    held[...] = jnp.zeros_like(held)
+    held[0:ROWS, 0:216] = qkv_ref[...].astype(F32)
+    held[0:ROWS, 256:328] = o_ref[...].astype(F32)
+    held[0:ROWS, 328:332] = last_ref[...].astype(F32)
+    at = 0
+    for ref in (time_ref, pos_ref, in_ref):
+        block = ref[...].astype(F32)
+        for q in range(ref.shape[0]):
+            for h in range(2):
+                held[at : at + 1, 216:252] = block[q : q + 1, ROWS * h : ROWS * h + ROWS]
+                at += 1
+    packed = held[...].astype(BF16)
+    for i in range(TM):
+        out_ref[i] = packed
 
 
 def spread_kernel(x_ref, pick_ref, emb_ref, mod_ref, order_ref, patch_ref, pay_ref, out_t_ref):
@@ -515,11 +532,14 @@
 
 
 def packed_weights(w_in, w_qkv, w_o, w_out, w_time, w_pos):
-    small = jnp.concatenate([w_time, w_pos, w_in], axis=0).reshape(ROWS, ROWS)
-    gap = jnp.zeros((ROWS, 4), BF16)
-    tail = jnp.zeros((ROWS, 52), BF16)
-    packed = jnp.concatenate([w_qkv, small, gap, w_o, w_out, tail], axis=1)
-    return jnp.pad(packed, ((0, 4), (0, 0)))
+    return pl.pallas_call(
+        pack_kernel,
+        out_shape=jax.ShapeDtypeStruct((TM, 40, 384), BF16),
+        in_specs=[BLOCK] * 6,
+        out_specs=VMEM,
+        scratch_shapes=[pltpu.VMEM((40, 384), F32)],
+        name="pack",
+    )(w_in, w_qkv, w_o, w_out, w_time, w_pos)
 
 
 def embeddings(level, position):
@@ -553,7 +573,7 @@
     scale_in = lax.rsqrt(1.0 + sigma_now * sigma_now)
 
     packed = packed_weights(w_in, w_qkv, w_o, w_out, w_time, w_pos)
-    rows = exchanged(jnp.broadcast_to(packed[None], (TM,) + packed.shape), TM_AXES)
+    rows = exchanged(packed, TM_AXES)
     rows = rows.reshape(WIDE, 384)
 
     own = prep(scale_in[0:1], latent)
@@ -565,7 +585,9 @@
     rows, marked, mix = lax.optimization_barrier((rows, marked, mix))
 
     pay, out_t = spread(rows, emb, mods, own)
+    across = swapped(out_t, "zh")
     feat = exchanged(pay, TILE_AXES)
+    feat, out_t = lax.optimization_barrier((feat, out_t))
 
     first, gram = fold(0, feat, rows)
     first, feat, rows = lax.optimization_barrier((first, feat, rows))
@@ -576,14 +598,14 @@
     n, mvt = heads(first)
     second = exchanged(second, TILE_AXES)
 
-    both = jnp.stack([out_t, swapped(out_t, "zh")])
+    both = jnp.stack([out_t, across])
     full_o = lax.all_gather(both, ("x", "core")).reshape(WIDE, WIDE)
 
     att, own = attend(False, spot, feat, gram, n, mvt)
-    att, second = lax.optimization_barrier((att, second))
     noise = output(0, spot, att, own, feat, full_o)
 
     following, after = shifted(noise, TM_AXES, -1), shifted(noise, TM_AXES, -2)
+    following, second = lax.optimization_barrier((following, second))
     last = (frame == TM - 1).astype(jnp.int32)[None]
     latent, edges, patches = middle(
         scale_in[1:2], last, noise, following, after, marked, new_frames[0], mix

time: 231 us -> 222 us (0.961)
  blocking collectives: 30.8 us -> 0 us
  starting transfers between devices: 59.7 us -> 79.4 us
  Pallas kernels: 37.2 us -> 40.1 us
    all_to_all x1 -> x0, blocking collectives: 30.8 us -> none  [exchanged(): return lax.all_to_all(copies, axis, split_axis=0, concat_axis=0, tiled=True)]
    all_to_all x4 -> x5, starting transfers between devices: 27.9 us -> 46.3 us  [exchanged(): return lax.all_to_all(copies, axis, split_axis=0, concat_axis=0, tiled=True)]
    all_gather x1, waiting for transfers between devices: 0.01 us -> 7.92 us  [per_device(): full_o = lax.all_gather(both, ('x', 'core')).reshape(WIDE, WIDE)]
    all_to_all x4 -> x5, waiting for transfers between devices: 41.2 us -> 34.8 us  [exchanged(): return lax.all_to_all(copies, axis, split_axis=0, concat_axis=0, tiled=True)]
  transfers between devices with their start and end apart: 13 -> 14, of which waited for: 10 -> 11; matrix products, arithmetic and copies ran while one was open for 2% -> 2% of each run, Pallas kernels for 7% -> 9%
where the time goes in v6:
time: 222 us; the launch traced here: 221 us
  starting transfers between devices  79.4 us (36%)
  waiting for transfers between devices  77.4 us (35%)
  Pallas kernels  40.1 us (18%)
  between operations  14.4 us (6%)
  local copies, waits for them, and re-layouts  8.2 us (4%)
    all_to_all x5, starting transfers between devices, exchanged(): return lax.all_to_all(copies, axis, split_axis=0, concat_axis=0, tiled=True)  46.3 us
    all_to_all x5, waiting for transfers between devices, exchanged(): return lax.all_to_all(copies, axis, split_axis=0, concat_axis=0, tiled=True)  34.8 us
    ppermute x7, waiting for transfers between devices, shifted(): return lax.ppermute(block, axis, route)  31 us
    ppermute x7, starting transfers between devices, shifted(): return lax.ppermute(block, axis, route)  26.1 us
    pallas_call x2, Pallas kernels, attend(): pl.pallas_call(functools.partial(attend_kernel, edges), out_shape=(jax.Sh...  18 us
    all_gather x1, waiting for transfers between devices, per_device(): full_o = lax.all_gather(both, ('x', 'core')).reshape(WIDE, WIDE)  7.92 us
    ppermute x1, starting transfers between devices, swapped(): return lax.ppermute(block, axis, [(0, 1), (1, 0)])  7 us
    pallas_call x2, Pallas kernels, output(): pl.pallas_call(functools.partial(output_kernel, step), out_shape=jax.Shap...  6.25 us
  transfers between devices with their start and end apart: 14, of which 11 were waited for; matrix products, arithmetic and copies ran while one was open for 2% of the time, Pallas kernels for 9%

profile of v6, /device:TPU:63, one launch (start us, length us, event | category | flops | bytes accessed | tf_op | source)
XLA Modules:
  0.0 221.4 jit_solution(2073368643908256485)
XLA Ops:
  6.6 1.4 copy.25.last_ref
  8.0 1.9 pack.1
  9.9 11.9 %all-to-all-start = ((bf16[32,40,384]{2,1,0:T(8,128)(2,1)}), bf16[32,40,384]{2,1,0:T(8,128)(2,1)S(1)}, u32[]{:S(2)}, u32[]{:S(2)}) async-start(bf16[32,40,384]{2,1,0:T(8,128)(2,1)} %pack.1), calls=%async_computation | async-start | bytes 1966080 | tf_op jit(solution)/shard_map/all_to_all | solution.py:53
  21.8 0.7 add_rsqrt_fusion
  22.5 0.7 fusion.9
  23.2 1.4 concatenate.24
  24.6 3.1 %collective-permute-start = (f32[5,16,128]{2,1,0:T(8,128)S(1)}, f32[5,16,128]{2,1,0:T(8,128)S(1)}, u32[]{:S(2)}, u32[]{:S(2)}) collective-permute-start(f32[5,16,128]{2,1,0:T(8,128)S(1)} %concatenate.24), channel_id=1, source_target_pairs={{16,0},{32,16},{48,32},{64,48},{80,64},{96,80},{112,96},{128,112},... | collective-permute-start | bytes 122888 | tf_op jit(solution)/shard_map/ppermute | solution.py:49
  27.7 0.1 mul.107
  27.8 0.4 mul.108
  28.9 0.1 pad.28.clone
  29.0 0.1 fusion
  29.1 0.1 maximum_maximum_fusion.1
  29.2 0.1 copy.27
  29.3 0.3 mul.104
  29.6 0.4 mul.105
  30.0 0.1 pad.23.clone
  30.1 0.1 maximum_maximum_fusion
  30.1 0.1 reshape.122
  30.3 0.2 copy.26
  30.5 0.1 reshape.121.mix_ref
  30.7 0.1 reshape.123
  30.7 0.1 copy.31
  30.8 2.2 prep.1.patch_ref
  33.0 10.5 %collective-permute-done.lat_ref = f32[5,16,128]{2,1,0:T(8,128)S(1)} collective-permute-done((f32[5,16,128]{2,1,0:T(8,128)S(1)}, f32[5,16,128]{2,1,0:T(8,128)S(1)}, u32[]{:S(2)}, u32[]{:S(2)}) %collective-permute-start) | collective-permute-done | bytes 40992 | tf_op jit(solution)/shard_map/ppermute | solution.py:49
  43.6 1.8 all-to-all-done
  45.4 0.7 copy-done.4
  46.1 1.6 spread.1
  47.7 12.7 %all-to-all-start.1 = ((bf16[16,144,128]{2,1,0:T(8,128)(2,1)}), bf16[16,144,128]{2,1,0:T(8,128)(2,1)S(1)}, u32[]{:S(2)}, u32[]{:S(2)}) async-start(bf16[16,144,128]{2,1,0:T(8,128)(2,1)} %get-tuple-element.33), calls=%async_computation.1 | async-start | bytes 1179648 | tf_op jit(solution)/shard_map/all_to_all | solution.py:53
  60.4 0.0 all-gather.3.cloned.1.call-start
  60.5 7.0 %collective-permute-start.1 = (bf16[80,1280]{1,0:T(8,128)(2,1)S(1)}, bf16[80,1280]{1,0:T(8,128)(2,1)S(1)}, u32[]{:S(2)}, u32[]{:S(2)}) collective-permute-start(bf16[80,1280]{1,0:T(8,128)(2,1)S(1)} %get-tuple-element.46), channel_id=1, source_target_pairs={{0,8},{8,0},{1,9},{9,1},{2,10},{10,2},{3,11},{11,3},{4,12},{12,4},... | collective-permute-start | bytes 614408 | tf_op jit(solution)/shard_map/ppermute | solution.py:43
  67.5 7.6 %all-to-all-done.1.feat_ref.pt_ref = bf16[16,144,128]{2,1,0:T(8,128)(2,1)S(1)} async-done(((bf16[16,144,128]{2,1,0:T(8,128)(2,1)}), bf16[16,144,128]{2,1,0:T(8,128)(2,1)S(1)}, u32[]{:S(2)}, u32[]{:S(2)}) %all-to-all-start.1) | async-done | bytes 589856 | tf_op jit(solution)/shard_map/all_to_all | solution.py:53
  75.1 3.6 %collective-permute-done.1 = bf16[80,1280]{1,0:T(8,128)(2,1)S(1)} collective-permute-done((bf16[80,1280]{1,0:T(8,128)(2,1)S(1)}, bf16[80,1280]{1,0:T(8,128)(2,1)S(1)}, u32[]{:S(2)}, u32[]{:S(2)}) %collective-permute-start.1) | collective-permute-done | bytes 204832 | tf_op jit(solution)/shard_map/ppermute | solution.py:43
  78.8 0.8 pad_maximum_fusion
  79.5 0.0 all-gather.3.cloned.1.call-update
  79.6 2.4 %fold.2 = (bf16[16,144,128]{2,1,0:T(8,128)(2,1)}, bf16[128,64]{1,0:T(8,128)(2,1)S(1)}) custom-call(bf16[16,144,128]{2,1,0:T(8,128)(2,1)S(1)} %all-to-all-done.1.feat_ref.pt_ref, bf16[1280,384]{1,0:T(8,128)(2,1)S(1)} %bitcast.24), custom_call_target="tpu_custom_call" | custom-call | flops 167772160 | bytes 1310720 | tf_op jit(solution)/shard_map/fold/pallas_call | solution.py:410
  82.0 5.6 %all-to-all-start.2 = ((bf16[16,144,128]{2,1,0:T(8,128)(2,1)}), bf16[16,144,128]{2,1,0:T(8,128)(2,1)S(1)}, u32[]{:S(2)}, u32[]{:S(2)}) async-start(bf16[16,144,128]{2,1,0:T(8,128)(2,1)} %get-tuple-element.39), calls=%async_computation.2 | async-start | bytes 1179648 | tf_op jit(solution)/shard_map/all_to_all | solution.py:53
  87.5 2.0 fold.3
  89.5 11.5 %all-to-all-done.2.folded_ref = bf16[16,144,128]{2,1,0:T(8,128)(2,1)S(1)} async-done(((bf16[16,144,128]{2,1,0:T(8,128)(2,1)}), bf16[16,144,128]{2,1,0:T(8,128)(2,1)S(1)}, u32[]{:S(2)}, u32[]{:S(2)}) %all-to-all-start.2) | async-done | bytes 589856 | tf_op jit(solution)/shard_map/all_to_all | solution.py:53
  101.0 5.5 %all-to-all-start.3 = ((bf16[16,144,128]{2,1,0:T(8,128)(2,1)}), bf16[16,144,128]{2,1,0:T(8,128)(2,1)S(1)}, u32[]{:S(2)}, u32[]{:S(2)}) async-start(bf16[16,144,128]{2,1,0:T(8,128)(2,1)} %fold.3), calls=%async_computation.3 | async-start | bytes 1179648 | tf_op jit(solution)/shard_map/all_to_all | solution.py:53
  106.6 0.8 heads.2
  107.3 0.0 copy-start.5
  107.3 9.0 %attend.2 = (bf16[1280,128]{1,0:T(8,128)(2,1)S(1)}, bf16[64,128]{1,0:T(8,128)(2,1)S(1)}) custom-call(s32[1]{0:T(128)} %bitcast.1.spot_ref, bf16[16,144,128]{2,1,0:T(8,128)(2,1)S(1)} %all-to-all-done.1.feat_ref.pt_ref, bf16[128,64]{1,0:T(8,128)(2,1)S(1)} %get-tuple-element.38.gram_ref, bf16[16,128,128]{2,1,0:T(8,128)(2,1)S(1)} %get-tuple-element.42.n_ref, ...), custom_call_target="tpu_custom_call" | custom-call | flops 4294967296 | bytes 2097152 | tf_op jit(solution)/shard_map/attend/pallas_call | solution.py:439
  116.3 7.9 %all-gather.3.cloned.1.call-done = bf16[16,80,1280]{2,1,0:T(8,128)(2,1)} async-done(((bf16[2,80,1280]{2,1,0:T(8,128)(2,1)}), bf16[16,80,1280]{2,1,0:T(8,128)(2,1)}) %all-gather.3.cloned.1.call-update) | async-done | bytes 3276816 | tf_op jit(solution)/shard_map/all_gather | solution.py:602
  124.2 1.9 copy-done
  126.2 3.1 %output.2.noise_ref = f32[4,16,128]{2,1,0:T(8,128)S(1)} custom-call(s32[1]{0:T(128)} %bitcast.1.spot_ref, bf16[1280,128]{1,0:T(8,128)(2,1)S(1)} %get-tuple-element.44.att_ref, bf16[64,128]{1,0:T(8,128)(2,1)S(1)} %get-tuple-element.45.own_ref, bf16[16,144,128]{2,1,0:T(8,128)(2,1)S(1)} %all-to-all-done.1.feat_ref.pt_ref, bf16[1280,1280]{1,0:T(8,128)(2,1)S(1)} %bitcast.26), custom_call_target="tpu_custom_call" | custom-call | tf_op jit(solution)/shard_map/output/pallas_call | solution.py:463
  129.3 6.4 %collective-permute-start.2 = (f32[4,16,128]{2,1,0:T(8,128)S(1)}, f32[4,16,128]{2,1,0:T(8,128)S(1)}, u32[]{:S(2)}, u32[]{:S(2)}) collective-permute-start(f32[4,16,128]{2,1,0:T(8,128)S(1)} %output.2.noise_ref), channel_id=1, source_target_pairs={{16,0},{32,16},{48,32},{64,48},{80,64},{96,80},{112,96},{128,112},... | collective-permute-start | bytes 98312 | tf_op jit(solution)/shard_map/ppermute | solution.py:49
  135.7 3.1 %collective-permute-start.3 = (f32[4,16,128]{2,1,0:T(8,128)S(1)}, f32[4,16,128]{2,1,0:T(8,128)S(1)}, u32[]{:S(2)}, u32[]{:S(2)}) collective-permute-start(f32[4,16,128]{2,1,0:T(8,128)S(1)} %output.2.noise_ref), channel_id=1, source_target_pairs={{32,0},{48,16},{64,32},{80,48},{96,64},{112,80},{128,96},{144,112}... | collective-permute-start | bytes 98312 | tf_op jit(solution)/shard_map/ppermute | solution.py:49
  138.8 0.0 all-to-all-done.3.folded_ref
  138.8 1.5 collective-permute-done.2.next_ref
  140.3 4.9 %collective-permute-done.3.after_ref = f32[4,16,128]{2,1,0:T(8,128)S(1)} collective-permute-done((f32[4,16,128]{2,1,0:T(8,128)S(1)}, f32[4,16,128]{2,1,0:T(8,128)S(1)}, u32[]{:S(2)}, u32[]{:S(2)}) %collective-permute-start.3) | collective-permute-done | bytes 32800 | tf_op jit(solution)/shard_map/ppermute | solution.py:49
  145.2 2.4 %middle.1 = (f32[4,16,128]{2,1,0:T(8,128)S(1)}, f32[2,16,128]{2,1,0:T(8,128)S(1)}, bf16[16,96,128]{2,1,0:T(8,128)(2,1)}) custom-call(f32[1]{0:T(128)} %bitcast.2.scalar_ref, s32[1]{0:T(128)} %bitcast.3.flag_ref, f32[4,16,128]{2,1,0:T(8,128)S(1)} %output.2.noise_ref, f32[4,16,128]{2,1,0:T(8,128)S(1)} %collective-permute-done.2.next_ref, ...), custom_call_target="tpu_custom_call" | custom-call | tf_op jit(solution)/shard_map/middle/pallas_call | solution.py:485
  147.6 10.5 %all-to-all-start.4 = ((bf16[16,96,128]{2,1,0:T(8,128)(2,1)}), bf16[16,96,128]{2,1,0:T(8,128)(2,1)S(1)}, u32[]{:S(2)}, u32[]{:S(2)}) async-start(bf16[16,96,128]{2,1,0:T(8,128)(2,1)} %get-tuple-element.51), calls=%async_computation.4 | async-start | bytes 786432 | tf_op jit(solution)/shard_map/all_to_all | solution.py:53
  158.2 0.8 heads.3
  158.9 13.9 %all-to-all-done.4.pt_ref = bf16[16,96,128]{2,1,0:T(8,128)(2,1)S(1)} async-done(((bf16[16,96,128]{2,1,0:T(8,128)(2,1)}), bf16[16,96,128]{2,1,0:T(8,128)(2,1)S(1)}, u32[]{:S(2)}, u32[]{:S(2)}) %all-to-all-start.4) | async-done | bytes 393248 | tf_op jit(solution)/shard_map/all_to_all | solution.py:53
  172.8 9.0 %attend.3 = (bf16[1280,128]{1,0:T(8,128)(2,1)S(1)}, bf16[64,128]{1,0:T(8,128)(2,1)S(1)}) custom-call(s32[1]{0:T(128)} %bitcast.1.spot_ref, bf16[16,96,128]{2,1,0:T(8,128)(2,1)S(1)} %all-to-all-done.4.pt_ref, bf16[128,64]{1,0:T(8,128)(2,1)S(1)} %get-tuple-element.38.gram_ref, bf16[16,128,128]{2,1,0:T(8,128)(2,1)S(1)} %get-tuple-element.53.n_ref, ...), custom_call_target="tpu_custom_call" | custom-call | flops 4294967296 | bytes 2097152 | tf_op jit(solution)/shard_map/attend/pallas_call | solution.py:439
  181.9 3.1 %output.3.noise_ref = f32[4,16,128]{2,1,0:T(8,128)S(1)} custom-call(s32[1]{0:T(128)} %bitcast.1.spot_ref, bf16[1280,128]{1,0:T(8,128)(2,1)S(1)} %get-tuple-element.55.att_ref, bf16[64,128]{1,0:T(8,128)(2,1)S(1)} %get-tuple-element.56.own_ref, bf16[16,144,128]{2,1,0:T(8,128)(2,1)S(1)} %all-to-all-done.1.feat_ref.pt_ref, bf16[1280,1280]{1,0:T(8,128)(2,1)S(1)} %bitcast.27), custom_call_target="tpu_custom_call" | custom-call | tf_op jit(solution)/shard_map/output/pallas_call | solution.py:463
  185.0 4.5 %collective-permute-start.4 = (f32[4,16,128]{2,1,0:T(8,128)S(1)}, f32[4,16,128]{2,1,0:T(8,128)S(1)}, u32[]{:S(2)}, u32[]{:S(2)}) collective-permute-start(f32[4,16,128]{2,1,0:T(8,128)S(1)} %output.3.noise_ref), channel_id=1, source_target_pairs={{0,16},{16,32},{32,48},{48,64},{64,80},{80,96},{96,112},{112,128},... | collective-permute-start | bytes 98312 | tf_op jit(solution)/shard_map/ppermute | solution.py:49
  189.5 1.9 collective-permute-start.5
  191.4 4.8 %collective-permute-done.5.next_ref = f32[4,16,128]{2,1,0:T(8,128)S(1)} collective-permute-done((f32[4,16,128]{2,1,0:T(8,128)S(1)}, f32[4,16,128]{2,1,0:T(8,128)S(1)}, u32[]{:S(2)}, u32[]{:S(2)}) %collective-permute-start.5) | collective-permute-done | bytes 32800 | tf_op jit(solution)/shard_map/ppermute | solution.py:49
  196.3 0.0 collective-permute-done.4.before_ref
  196.3 5.2 %collective-permute-start.6 = (f32[4,16,128]{2,1,0:T(8,128)S(1)}, f32[4,16,128]{2,1,0:T(8,128)S(1)}, u32[]{:S(2)}, u32[]{:S(2)}) collective-permute-start(f32[4,16,128]{2,1,0:T(8,128)S(1)} %pad_maximum_fusion.1), channel_id=1, source_target_pairs={{0,1},{1,2},{2,3},{3,4},{4,5},{5,6},{6,7},{7,8},{8,9},{9,10},{10,1... | collective-permute-start | bytes 98312 | tf_op jit(solution)/shard_map/ppermute | solution.py:49
  201.5 1.9 collective-permute-start.7
  203.4 9.3 %collective-permute-done.7.down_ref = f32[4,16,128]{2,1,0:T(8,128)S(1)} collective-permute-done((f32[4,16,128]{2,1,0:T(8,128)S(1)}, f32[4,16,128]{2,1,0:T(8,128)S(1)}, u32[]{:S(2)}, u32[]{:S(2)}) %collective-permute-start.7) | collective-permute-done | bytes 32800 | tf_op jit(solution)/shard_map/ppermute | solution.py:49
  212.7 1.8 finish.1
  (36 shorter events, 0.1 us)
Async XLA Ops:
  6.5 38.8 %copy-start.2 = (bf16[2,64,1280]{2,1,0:T(8,128)(2,1)S(1)}, bf16[2,64,1280]{2,1,0:T(8,128)(2,1)}, u32[]{:S(2)}) copy-start(bf16[2,64,1280]{2,1,0:T(8,128)(2,1)} %constant.65.clone.pick_ref) | copy-start | bytes 983044
  6.5 38.8 %copy-start.6 = (bf16[80,128]{1,0:T(8,128)(2,1)S(1)}, bf16[80,128]{1,0:T(8,128)(2,1)}, u32[]{:S(2)}) copy-start(bf16[80,128]{1,0:T(8,128)(2,1)} %constant.66.clone.order_ref) | copy-start | bytes 61444
  6.5 22.4 %copy-start.10 = (s32[2,1]{0,1:T(1,128)S(1)}, s32[2,1]{0,1:T(1,128)}, u32[]{:S(2)}) copy-start(s32[2,1]{0,1:T(1,128)} %param.19) | copy-start | bytes 28
  6.5 23.5 %copy-start.8 = (f32[3,1152]{1,0:T(4,128)S(1)}, f32[3,1152]{1,0:T(4,128)}, u32[]{:S(2)}) copy-start(f32[3,1152]{1,0:T(4,128)} %param.28) | copy-start | bytes 41476
  6.5 23.5 %copy-start.9 = (f32[3,1152]{1,0:T(4,128)S(1)}, f32[3,1152]{1,0:T(4,128)}, u32[]{:S(2)}) copy-start(f32[3,1152]{1,0:T(4,128)} %param.27) | copy-start | bytes 41476
  6.5 23.8 %copy-start.7 = (f32[16,27,16]{1,2,0:T(8,128)S(1)}, f32[16,27,16]{1,2,0:T(8,128)}, u32[]{:S(2)}) copy-start(f32[16,27,16]{1,2,0:T(8,128)} %param.29) | copy-start | bytes 82948
  9.9 35.4 %all-to-all-start = ((bf16[32,40,384]{2,1,0:T(8,128)(2,1)}), bf16[32,40,384]{2,1,0:T(8,128)(2,1)S(1)}, u32[]{:S(2)}, u32[]{:S(2)}) async-start(bf16[32,40,384]{2,1,0:T(8,128)(2,1)} %pack.1), calls=%async_computation | async-start | bytes 1966080 | tf_op jit(solution)/shard_map/all_to_all | solution.py:53
  24.6 19.0 %collective-permute-start = (f32[5,16,128]{2,1,0:T(8,128)S(1)}, f32[5,16,128]{2,1,0:T(8,128)S(1)}, u32[]{:S(2)}, u32[]{:S(2)}) collective-permute-start(f32[5,16,128]{2,1,0:T(8,128)S(1)} %concatenate.24), channel_id=1, source_target_pairs={{16,0},{32,16},{48,32},{64,48},{80,64},{96,80},{112,96},{128,112},... | collective-permute-start | bytes 122888 | tf_op jit(solution)/shard_map/ppermute | solution.py:49
  45.4 0.7 copy-start.4
  47.7 27.4 %all-to-all-start.1 = ((bf16[16,144,128]{2,1,0:T(8,128)(2,1)}), bf16[16,144,128]{2,1,0:T(8,128)(2,1)S(1)}, u32[]{:S(2)}, u32[]{:S(2)}) async-start(bf16[16,144,128]{2,1,0:T(8,128)(2,1)} %get-tuple-element.33), calls=%async_computation.1 | async-start | bytes 1179648 | tf_op jit(solution)/shard_map/all_to_all | solution.py:53
  60.4 63.8 %all-gather.3.cloned.1.call-start = ((), (), s32[]{:S(2)}) async-start(), calls=%async_computation.5 | async-start | bytes 3686400 | tf_op jit(solution)/shard_map/all_gather | solution.py:602
  60.5 18.3 %collective-permute-start.1 = (bf16[80,1280]{1,0:T(8,128)(2,1)S(1)}, bf16[80,1280]{1,0:T(8,128)(2,1)S(1)}, u32[]{:S(2)}, u32[]{:S(2)}) collective-permute-start(bf16[80,1280]{1,0:T(8,128)(2,1)S(1)} %get-tuple-element.46), channel_id=1, source_target_pairs={{0,8},{8,0},{1,9},{9,1},{2,10},{10,2},{3,11},{11,3},{4,12},{12,4},... | collective-permute-start | bytes 614408 | tf_op jit(solution)/shard_map/ppermute | solution.py:43
  79.5 27.0 %copy-start.3 = (bf16[80,72]{1,0:T(8,128)(2,1)S(1)}, bf16[80,72]{1,0:T(8,128)(2,1)}, u32[]{:S(2)}) copy-start(bf16[80,72]{1,0:T(8,128)(2,1)} %constant.67.clone.widen_ref) | copy-start | bytes 34564
  82.0 19.0 %all-to-all-start.2 = ((bf16[16,144,128]{2,1,0:T(8,128)(2,1)}), bf16[16,144,128]{2,1,0:T(8,128)(2,1)S(1)}, u32[]{:S(2)}, u32[]{:S(2)}) async-start(bf16[16,144,128]{2,1,0:T(8,128)(2,1)} %get-tuple-element.39), calls=%async_computation.2 | async-start | bytes 1179648 | tf_op jit(solution)/shard_map/all_to_all | solution.py:53
  101.0 37.8 %all-to-all-start.3 = ((bf16[16,144,128]{2,1,0:T(8,128)(2,1)}), bf16[16,144,128]{2,1,0:T(8,128)(2,1)S(1)}, u32[]{:S(2)}, u32[]{:S(2)}) async-start(bf16[16,144,128]{2,1,0:T(8,128)(2,1)} %fold.3), calls=%async_computation.3 | async-start | bytes 1179648 | tf_op jit(solution)/shard_map/all_to_all | solution.py:53
  107.3 37.9 %copy-start.5 = (f32[1,4,16,128]{3,2,1,0:T(8,128)S(1)}, f32[1,4,16,128]{3,2,1,0:T(8,128)}, u32[]{:S(2)}) copy-start(f32[1,4,16,128]{3,2,1,0:T(8,128)} %param.18) | copy-start | bytes 98308
  124.2 1.9 copy-start
  129.3 11.0 %collective-permute-start.2 = (f32[4,16,128]{2,1,0:T(8,128)S(1)}, f32[4,16,128]{2,1,0:T(8,128)S(1)}, u32[]{:S(2)}, u32[]{:S(2)}) collective-permute-start(f32[4,16,128]{2,1,0:T(8,128)S(1)} %output.2.noise_ref), channel_id=1, source_target_pairs={{16,0},{32,16},{48,32},{64,48},{80,64},{96,80},{112,96},{128,112},... | collective-permute-start | bytes 98312 | tf_op jit(solution)/shard_map/ppermute | solution.py:49
  135.7 9.5 %collective-permute-start.3 = (f32[4,16,128]{2,1,0:T(8,128)S(1)}, f32[4,16,128]{2,1,0:T(8,128)S(1)}, u32[]{:S(2)}, u32[]{:S(2)}) collective-permute-start(f32[4,16,128]{2,1,0:T(8,128)S(1)} %output.2.noise_ref), channel_id=1, source_target_pairs={{32,0},{48,16},{64,32},{80,48},{96,64},{112,80},{128,96},{144,112}... | collective-permute-start | bytes 98312 | tf_op jit(solution)/shard_map/ppermute | solution.py:49
  147.6 25.2 %all-to-all-start.4 = ((bf16[16,96,128]{2,1,0:T(8,128)(2,1)}), bf16[16,96,128]{2,1,0:T(8,128)(2,1)S(1)}, u32[]{:S(2)}, u32[]{:S(2)}) async-start(bf16[16,96,128]{2,1,0:T(8,128)(2,1)} %get-tuple-element.51), calls=%async_computation.4 | async-start | bytes 786432 | tf_op jit(solution)/shard_map/all_to_all | solution.py:53
  172.8 9.0 %copy-start.1 = (bf16[16,80,1280]{2,1,0:T(8,128)(2,1)S(1)}, bf16[16,80,1280]{2,1,0:T(8,128)(2,1)}, u32[]{:S(2)}) copy-start(bf16[16,80,1280]{2,1,0:T(8,128)(2,1)} %all-gather.3.cloned.1.call-done) | copy-start | bytes 9830404
  185.0 11.3 %collective-permute-start.4 = (f32[4,16,128]{2,1,0:T(8,128)S(1)}, f32[4,16,128]{2,1,0:T(8,128)S(1)}, u32[]{:S(2)}, u32[]{:S(2)}) collective-permute-start(f32[4,16,128]{2,1,0:T(8,128)S(1)} %output.3.noise_ref), channel_id=1, source_target_pairs={{0,16},{16,32},{32,48},{48,64},{64,80},{80,96},{96,112},{112,128},... | collective-permute-start | bytes 98312 | tf_op jit(solution)/shard_map/ppermute | solution.py:49
  189.5 6.8 %collective-permute-start.5 = (f32[4,16,128]{2,1,0:T(8,128)S(1)}, f32[4,16,128]{2,1,0:T(8,128)S(1)}, u32[]{:S(2)}, u32[]{:S(2)}) collective-permute-start(f32[4,16,128]{2,1,0:T(8,128)S(1)} %output.3.noise_ref), channel_id=1, source_target_pairs={{16,0},{32,16},{48,32},{64,48},{80,64},{96,80},{112,96},{128,112},... | collective-permute-start | bytes 98312 | tf_op jit(solution)/shard_map/ppermute | solution.py:49
  196.3 7.1 %collective-permute-start.6 = (f32[4,16,128]{2,1,0:T(8,128)S(1)}, f32[4,16,128]{2,1,0:T(8,128)S(1)}, u32[]{:S(2)}, u32[]{:S(2)}) collective-permute-start(f32[4,16,128]{2,1,0:T(8,128)S(1)} %pad_maximum_fusion.1), channel_id=1, source_target_pairs={{0,1},{1,2},{2,3},{3,4},{4,5},{5,6},{6,7},{7,8},{8,9},{9,10},{10,1... | collective-permute-start | bytes 98312 | tf_op jit(solution)/shard_map/ppermute | solution.py:49
  201.5 11.3 %collective-permute-start.7 = (f32[4,16,128]{2,1,0:T(8,128)S(1)}, f32[4,16,128]{2,1,0:T(8,128)S(1)}, u32[]{:S(2)}, u32[]{:S(2)}) collective-permute-start(f32[4,16,128]{2,1,0:T(8,128)S(1)} %pad_maximum_fusion.2), channel_id=1, source_target_pairs={{1,0},{2,1},{3,2},{4,3},{5,4},{6,5},{7,6},{8,7},{9,8},{10,9},{11,1... | collective-permute-start | bytes 98312 | tf_op jit(solution)/shard_map/ppermute | solution.py:49
Sparse Core Ops, SparseCore 0:
  79.7 44.5 all-gather.2
